TPU v7x, 32 devices: a whole 2x2x4 slice. The times are simulated.
32 devices in a mesh: row: 8 (over z, y), col: 4 (over x, core).
Axes of the slice: x: 2, y: 2, z: 4, core: 2. Of those that a mesh axis runs over, the one named last changes fastest.
Arguments:
- trail_adjoint: float32 [6144, 6144], P('row', 'col'), may hold values from -3 to 3
- panel: float32 [6144, 256], P(('row', 'col')), may hold values from -0.078125 to 0.078125
- panel_adjoint: float32 [6144, 256], P(('row', 'col')), may hold values from -6 to 6
- diag_factor: float32 [256, 256], replicated, as said below
- diag_inverse: float32 [256, 256], replicated, as said below
- diag_adjoint: float32 [256, 256], replicated, may hold values from -6 to 6
Outputs:
- panel_grad: float32 [6144, 256], P(('row', 'col'))
- diag_grad: float32 [256, 256], replicated
Inputs may be any that keep to these rules, and one draw needn't show every extreme that they name: diag_factor is lower triangular with a diagonal between 1 and 2, and diag_inverse is its inverse. diag_factor is lower triangular with a diagonal between 1 and 2.
All inputs are finite; a program needn't handle non-finite values.
Results may differ from a plain program's by a relative error of at most 0.000057.
Values sent between devices are 32-bit elements; how exact they have to be, the bound alone decides.
No kernel may reach another device: no remote copies, remote signals or barrier semaphores. Data moves between devices by JAX's collectives and lax.ppermute only.
A program may use at most 128 MiB of HBM per device.

v0:
```python
import jax
import jax.numpy as jnp
from jax import lax
from jax.sharding import PartitionSpec as P


def lower_half(matrix):
    return jnp.tril(matrix) - 0.5 * jnp.diag(jnp.diag(matrix))


def on_device(trail_adjoint, panel, panel_adjoint, diag_factor, diag_inverse, diag_adjoint):
    highest = lax.Precision.HIGHEST
    col_place = lax.axis_index("col")
    trail_width = trail_adjoint.shape[1]
    row_block = lax.all_gather(panel, "col", axis=0, tiled=True)
    full_panel = lax.all_gather(row_block, "row", axis=0, tiled=True)
    column_panel = lax.dynamic_slice_in_dim(full_panel, col_place * trail_width, trail_width, 0)
    image = lax.psum_scatter(
        jnp.dot(trail_adjoint, column_panel, precision=highest, preferred_element_type=jnp.float32),
        "col",
        scatter_dimension=0,
        tiled=True,
    )
    updated = panel_adjoint - 2.0 * image
    panel_grad = jnp.dot(
        updated, diag_inverse, precision=highest, preferred_element_type=jnp.float32
    )
    local_gram = jnp.dot(panel_grad.T, panel, precision=highest, preferred_element_type=jnp.float32)
    gram = lax.psum(local_gram, ("row", "col"))
    corner = diag_adjoint - gram
    inner = lower_half(
        jnp.dot(diag_factor.T, corner, precision=highest, preferred_element_type=jnp.float32)
    )
    left_part = jnp.dot(
        diag_inverse.T, inner, precision=highest, preferred_element_type=jnp.float32
    )
    diag_grad = lower_half(
        jnp.dot(left_part, diag_inverse, precision=highest, preferred_element_type=jnp.float32)
    )
    return (panel_grad, diag_grad)


def solution(mesh):
    in_specs = (P("row", "col"), P(("row", "col"), None), P(("row", "col"), None), P(), P(), P())
    out_specs = (P(("row", "col"), None), P())
    return jax.shard_map(
        on_device, mesh=mesh, in_specs=in_specs, out_specs=out_specs, check_vma=False
    )
```

profile of v0, /device:TPU:0, one launch (start us, length us, event | category | flops | bytes accessed | tf_op | source)
XLA Modules:
  0.0 294.6 jit_solution(13242674921587057162)
XLA Ops:
  7.2 0.0 copy-start
  7.2 0.0 copy-start.5
  7.2 0.0 all-gather.2.cloned.1.call-start
  7.2 11.8 %all_gather.6 = f32[768,256]{1,0:T(8,128)} all-gather(f32[192,256]{1,0:T(8,128)} %param.7), channel_id=1, replica_groups=mesh['row'=8,'col'=4] {'col'}, dimensions={0}, use_global_device_ids=true | all-gather | bytes 983040 | tf_op jit(solution)/shard_map/all_gather | solution.py:15
  19.0 0.0 copy-start.1
  19.0 0.0 all-gather.2.cloned.1.call-update
  19.0 0.0 reduce-scatter.2.cloned.1.call-start
  19.1 0.0 copy-start.3
  19.1 0.0 copy-start.4
  19.1 99.5 %all-gather.2.cloned.1.call-done = f32[6144,256]{1,0:T(8,128)} async-done(((f32[768,256]{1,0:T(8,128)}), f32[6144,256]{1,0:T(8,128)}) %all-gather.2.cloned.1.call-update) | async-done | bytes 6291472 | tf_op jit(solution)/shard_map/all_gather | solution.py:16
  118.6 7.6 %fusion.2 = f32[768,256]{1,0:T(8,128)} fusion(f32[768,1536]{1,0:T(8,128)} %param.6, f32[6144,256]{1,0:T(8,128)} %all-gather.2.cloned.1.call-done, s32[]{:T(128)S(6)} %select_n.26), kind=kOutput, calls=%fused_computation.4 | convolution fusion | flops 3623878656 | bytes 7077892 | tf_op jit(solution)/shard_map/dot_general | solution.py:19
  126.1 0.0 reduce-scatter.2.cloned.1.call-update
  126.2 0.0 all-reduce.2.cloned.1.call-start
  126.2 21.6 %reduce-scatter.2.cloned.1.call-done = f32[192,256]{1,0:T(8,128)} async-done(((f32[768,256]{1,0:T(8,128)}), f32[192,256]{1,0:T(8,128)}) %reduce-scatter.2.cloned.1.call-update) | async-done | bytes 196624 | tf_op jit(solution)/shard_map/reduce_scatter | solution.py:18
  147.8 0.0 copy-done
  147.8 0.0 copy-done.5
  147.8 1.3 fusion.11
  149.1 0.0 copy-done.1
  149.1 0.0 copy-start.2
  149.1 1.4 fusion.22
  150.5 0.0 all-reduce.2.cloned.1.call-update
  150.5 129.2 %all-reduce.2.cloned.1.call-done = f32[256,256]{1,0:T(8,128)} async-done(((f32[256,256]{1,0:T(8,128)}), f32[256,256]{1,0:T(8,128)}) %all-reduce.2.cloned.1.call-update) | async-done | bytes 262160 | tf_op jit(solution)/shard_map/psum | solution.py:29
  279.7 0.0 copy-done.3
  279.7 0.0 copy-done.4
  279.7 1.5 convolution_bitcast_fusion
  281.3 2.4 gather_fusion
  283.7 0.4 fusion.5
  284.1 0.6 fusion.23
  284.7 0.1 copy.10
  284.8 2.3 gather_fusion.1
  287.2 0.8 copy.11
  288.0 0.0 copy-done.2
  (2 shorter events, 0.0 us)
Async XLA Ops:
  7.2 140.6 %copy-start = (f32[256,256]{1,0:T(8,128)S(1)}, f32[256,256]{1,0:T(8,128)}, u32[]{:S(2)}) copy-start(f32[256,256]{1,0:T(8,128)} %param.10) | copy-start | bytes 786436
  7.2 140.6 %copy-start.5 = (f32[192,256]{1,0:T(8,128)S(1)}, f32[192,256]{1,0:T(8,128)}, u32[]{:S(2)}) copy-start(f32[192,256]{1,0:T(8,128)} %param.8) | copy-start | bytes 589828
  7.2 111.4 %all-gather.2.cloned.1.call-start = ((), (), s32[]{:S(2)}) async-start(), calls=%async_computation.1 | async-start | bytes 7077888 | tf_op jit(solution)/shard_map/all_gather | solution.py:16
  19.0 130.0 %copy-start.1 = (f32[192,256]{1,0:T(8,128)S(1)}, f32[192,256]{1,0:T(8,128)}, u32[]{:S(2)}) copy-start(f32[192,256]{1,0:T(8,128)} %param.7) | copy-start | bytes 589828
  19.0 128.7 %reduce-scatter.2.cloned.1.call-start = ((), (), s32[]{:S(2)}) async-start(), calls=%async_computation.2 | async-start | bytes 983040 | tf_op jit(solution)/shard_map/reduce_scatter | solution.py:18
  19.1 260.6 %copy-start.3 = (f32[256,256]{1,0:T(8,128)S(1)}, f32[256,256]{1,0:T(8,128)}, u32[]{:S(2)}) copy-start(f32[256,256]{1,0:T(8,128)} %param.9) | copy-start | bytes 786436
  19.1 260.6 %copy-start.4 = (f32[256,256]{1,0:T(8,128)S(1)}, f32[256,256]{1,0:T(8,128)}, u32[]{:S(2)}) copy-start(f32[256,256]{1,0:T(8,128)} %param.11) | copy-start | bytes 786436
  126.2 153.6 %all-reduce.2.cloned.1.call-start = ((), (), s32[]{:S(2)}) async-start(), calls=%async_computation.3 | async-start | bytes 524288 | tf_op jit(solution)/shard_map/psum | solution.py:29
  149.1 139.0 %copy-start.2 = (f32[192,256]{1,0:T(8,128)}, f32[192,256]{1,0:T(8,128)S(1)}, u32[]{:S(2)}) copy-start(f32[192,256]{1,0:T(8,128)S(1)} %fusion.11) | copy-start | bytes 589828
Sparse Core Ops, SparseCore 0:
  19.2 99.3 all-gather.1
  126.3 21.4 reduce-scatter.1
  154.8 124.9 all-reduce.1
where the time goes:
time: 295 us
  waiting for transfers between devices  250 us (85%)
  between operations  13.9 us (5%)
  matrix products  12.7 us (4%)
  blocking collectives  11.8 us (4%)
  local copies, waits for them, and re-layouts  5.72 us (2%)
    psum x1, waiting for transfers between devices, on_device(): gram = lax.psum(local_gram, ('row', 'col'))  129 us
    all_gather x1, waiting for transfers between devices, on_device(): full_panel = lax.all_gather(row_block, 'row', axis=0, tiled=True)  99.5 us
    reduce_scatter x1, waiting for transfers between devices, on_device(): lax.psum_scatter(jnp.dot(trail_adjoint, column_panel, precision=highest,...  21.6 us
    all_gather x1, blocking collectives, on_device(): row_block = lax.all_gather(panel, 'col', axis=0, tiled=True)  11.8 us
    dot_general x1, matrix products, on_device(): jnp.dot(trail_adjoint, column_panel, precision=highest, preferred_element...  7.57 us
  transfers between devices with their start and end apart: 3, of which 3 were waited for; matrix products, arithmetic and copies ran while one was open for 0% of the time, Pallas kernels for 0%

commit v1 on v0

v1 whole, which is shorter than its diff:
```python
import jax
import jax.numpy as jnp
from jax import lax
from jax.sharding import PartitionSpec as P

HIGHEST = lax.Precision.HIGHEST
HIGH = lax.Precision.HIGH
AXES = ("row", "col")


def dot(a, b, precision=HIGHEST):
    return jnp.dot(a, b, precision=precision, preferred_element_type=jnp.float32)


def dot_t(a, b, precision=HIGHEST):
    return lax.dot_general(
        a, b, (((0,), (0,)), ((), ())), precision=precision, preferred_element_type=jnp.float32
    )


def lower_half(matrix):
    return jnp.tril(matrix) - 0.5 * jnp.diag(jnp.diag(matrix))


def make_on_device(rows, cols):
    group = rows // cols
    devices = rows * cols

    def index(plane, y, c):
        return (plane * group + y) * cols + c

    def plane_flip(mask):
        return [
            (index(p, y, c), index(p ^ mask, y, c))
            for p in range(cols) for y in range(group) for c in range(cols)
        ]

    def col_flip(mask):
        return [(r * cols + c, r * cols + (c ^ mask)) for r in range(rows) for c in range(cols)]

    planes = [[index(p, y, c) for y in range(group) for c in range(cols)] for p in range(cols)]

    def flip_plane(x, mask):
        return lax.ppermute(x, AXES, plane_flip(mask))

    def flip_col(x, mask):
        return lax.ppermute(x, AXES, col_flip(mask))

    def place(pieces, position):
        height = pieces[0].shape[0]
        out = jnp.zeros((len(pieces) * height,) + pieces[0].shape[1:], pieces[0].dtype)
        for d, piece in enumerate(pieces):
            out = lax.dynamic_update_slice_in_dim(out, piece, (position ^ d) * height, 0)
        return out

    def along_planes(panel, plane):
        pieces = [panel] + [None] * (cols - 1)
        if cols == 4:
            pieces[3] = flip_plane(panel, 3)
            pieces[1] = flip_plane(panel, 1)
            pieces[2] = flip_plane(pieces[3], 1)
        else:
            for d in range(1, cols):
                pieces[d] = flip_plane(panel, d)
        return place(pieces, plane)

    def on_device(trail_adjoint, panel, panel_adjoint, diag_factor, diag_inverse, diag_adjoint):
        size = panel.shape[1]
        height = panel.shape[0]
        row_place = lax.axis_index("row")
        col_place = lax.axis_index("col")
        me = row_place * cols + col_place

        by_plane = along_planes(panel, row_place // group)
        row_pieces = [panel]
        mask = cols // 2
        gathered = panel[None]
        order = [0]
        while mask:
            other = flip_col(gathered, mask)
            gathered = jnp.concatenate([gathered, other])
            order = order + [o ^ mask for o in order]
            mask //= 2
        row_pieces = [gathered[order.index(d)] for d in range(cols)]
        row_panel = place(row_pieces, col_place)

        column_panel = lax.all_to_all(
            jnp.concatenate([by_plane] * group), AXES, 0, 0, axis_index_groups=planes, tiled=True
        )
        partial = dot(trail_adjoint, column_panel, HIGH)
        gram_t = dot_t(panel, panel_adjoint) - 2.0 * dot_t(row_panel, partial)

        held = partial.reshape(cols, height, size)
        mask = cols // 2
        while mask:
            bit = (col_place // mask) % 2
            halves = held.reshape(2, held.shape[0] // 2, height, size)
            mine = lax.dynamic_index_in_dim(halves, bit, 0, keepdims=False)
            theirs = lax.dynamic_index_in_dim(halves, 1 - bit, 0, keepdims=False)
            held = mine + flip_col(theirs, mask)
            mask //= 2
        image = held[0]

        share = size // devices
        summed = jnp.sum(
            lax.all_to_all(gram_t, AXES, 0, 0, tiled=True).reshape(devices, share, size), axis=0
        )
        corner_t = lax.dynamic_slice_in_dim(diag_adjoint, me * share, share, 1).T - dot(
            summed, diag_inverse
        )
        inner_t = dot(corner_t, diag_factor)
        at = lax.broadcasted_iota(jnp.int32, inner_t.shape, 0) + me * share
        across = lax.broadcasted_iota(jnp.int32, inner_t.shape, 1)
        inner_t = jnp.where(across > at, inner_t, jnp.where(across == at, 0.5 * inner_t, 0.0))
        left_t = dot(inner_t, diag_inverse)
        left_t = lax.all_to_all(jnp.tile(left_t, (devices, 1)), AXES, 0, 0, tiled=True)
        diag_grad = lower_half(dot_t(left_t, diag_inverse))

        panel_grad = dot(panel_adjoint - 2.0 * image, diag_inverse)
        return panel_grad, diag_grad

    return on_device


def solution(mesh):
    in_specs = (P("row", "col"), P(("row", "col"), None), P(("row", "col"), None), P(), P(), P())
    out_specs = (P(("row", "col"), None), P())
    return jax.shard_map(
        make_on_device(mesh.shape["row"], mesh.shape["col"]),
        mesh=mesh, in_specs=in_specs, out_specs=out_specs, check_vma=False,
    )
```

time: 295 us -> 90 us (0.31)
  waiting for transfers between devices: 250 us -> 43.2 us
  starting transfers between devices: 0.12 us -> 20.8 us
  between operations: 13.9 us -> 0.88 us
  blocking collectives: 11.8 us -> 0 us
  other arithmetic: 0.04 us -> 3.98 us
    psum x1 -> x0, waiting for transfers between devices: 129 us -> none  [on_device(): gram = lax.psum(local_gram, ('row', 'col'))]
    all_gather x1 -> x0, waiting for transfers between devices: 99.5 us -> none  [on_device(): full_panel = lax.all_gather(row_block, 'row', axis=0, tiled=True)]
    all_to_all x0 -> x3, waiting for transfers between devices: none -> 28.7 us  [the longest x1 16.1 us: on_device(): lax.all_to_all(jnp.concatenate([by_plane] * group), AXES, 0, 0, axis_inde...]
    reduce_scatter x1 -> x0, waiting for transfers between devices: 21.6 us -> none  [on_device(): lax.psum_scatter(jnp.dot(trail_adjoint, column_panel, precision=highest,...]
    ppermute x0 -> x7, waiting for transfers between devices: none -> 14.6 us  [the longest x3 8.06 us: flip_plane(): return lax.ppermute(x, AXES, plane_flip(mask))]
    all_gather x1 -> x0, blocking collectives: 11.8 us -> none  [on_device(): row_block = lax.all_gather(panel, 'col', axis=0, tiled=True)]
    ppermute x0 -> x7, starting transfers between devices: none -> 10.8 us  [the longest x3 8.17 us: flip_plane(): return lax.ppermute(x, AXES, plane_flip(mask))]
    all_to_all x0 -> x3, starting transfers between devices: none -> 9.92 us  [the longest x1 3.85 us: on_device(): lax.all_to_all(jnp.concatenate([by_plane] * group), AXES, 0, 0, axis_inde...]
  transfers between devices with their start and end apart: 3 -> 10, of which waited for: 3 -> 8; matrix products, arithmetic and copies ran while one was open for 0% -> 12% of each run, Pallas kernels for 0% -> 0%
where the time goes in v1:
time: 90 us; the launch traced here: 89.5 us
  waiting for transfers between devices  43.2 us (48%)
  starting transfers between devices  20.8 us (23%)
  matrix products  13.4 us (15%)
  local copies, waits for them, and re-layouts  7.25 us (8%)
  other arithmetic  3.98 us (4%)
    all_to_all x1, waiting for transfers between devices, on_device(): lax.all_to_all(jnp.concatenate([by_plane] * group), AXES, 0, 0, axis_inde...  16.1 us
    dot_general x5, matrix products, dot(): jnp.dot(a, b, precision=precision, preferred_element_type=jnp.float32)  9.32 us
    ppermute x3, starting transfers between devices, flip_plane(): return lax.ppermute(x, AXES, plane_flip(mask))  8.17 us
    ppermute x3, waiting for transfers between devices, flip_plane(): return lax.ppermute(x, AXES, plane_flip(mask))  8.06 us
    all_to_all x1, waiting for transfers between devices, on_device(): lax.all_to_all(jnp.tile(left_t, (devices, 1)), AXES, 0, 0, tiled=True)  8.03 us
    ppermute x4, waiting for transfers between devices, flip_col(): return lax.ppermute(x, AXES, col_flip(mask))  6.52 us
    all_to_all x1, waiting for transfers between devices, on_device(): lax.all_to_all(gram_t, AXES, 0, 0, tiled=True).reshape(devices, share, size)  4.53 us
    dot_general x3, matrix products, dot_t(): lax.dot_general(a, b, (((0,), (0,)), ((), ())), precision=precision, pref...  4.08 us
  transfers between devices with their start and end apart: 10, of which 8 were waited for; matrix products, arithmetic and copies ran while one was open for 12% of the time, Pallas kernels for 0%

profile of v1, /device:TPU:0, one launch (start us, length us, event | category | flops | bytes accessed | tf_op | source)
XLA Modules:
  0.0 89.5 jit_solution(14443203444752642111)
XLA Ops:
  0.6 0.0 copy-start
  0.6 5.1 %collective-permute-start.1 = (f32[192,256]{1,0:T(8,128)}, f32[192,256]{1,0:T(8,128)S(1)}, u32[]{:S(2)}, u32[]{:S(2)}) collective-permute-start(f32[192,256]{1,0:T(8,128)} %param.7), channel_id=1, source_target_pairs={{0,24},{1,25},{2,26},{3,27},{4,28},{5,29},{6,30},{7,31},{8,16},{9,... | collective-permute-start | bytes 589832 | tf_op jit(solution)/shard_map/ppermute | solution.py:44
  5.8 0.0 collective-permute-start
  5.8 1.5 %collective-permute-start.5 = (f32[1,192,256]{2,1,0:T(8,128)}, f32[1,192,256]{2,1,0:T(8,128)S(1)}, u32[]{:S(2)}, u32[]{:S(2)}) collective-permute-start(f32[1,192,256]{2,1,0:T(8,128)} %bitcast.48), channel_id=1, source_target_pairs={{0,2},{1,3},{2,0},{3,1},{4,6},{5,7},{6,4},{7,5},{8,10},{9,11},{10,... | collective-permute-start | bytes 589832 | tf_op jit(solution)/shard_map/ppermute | solution.py:47
  7.3 4.5 %collective-permute-done.1 = f32[192,256]{1,0:T(8,128)S(1)} collective-permute-done((f32[192,256]{1,0:T(8,128)}, f32[192,256]{1,0:T(8,128)S(1)}, u32[]{:S(2)}, u32[]{:S(2)}) %collective-permute-start.1) | collective-permute-done | bytes 196640 | tf_op jit(solution)/shard_map/ppermute | solution.py:44
  11.8 3.0 %collective-permute-start.2 = (f32[192,256]{1,0:T(8,128)S(1)}, f32[192,256]{1,0:T(8,128)S(1)}, u32[]{:S(2)}, u32[]{:S(2)}) collective-permute-start(f32[192,256]{1,0:T(8,128)S(1)} %collective-permute-done.1), channel_id=1, source_target_pairs={{0,8},{1,9},{2,10},{3,11},{4,12},{5,13},{6,14},{7,15},{8,0},{9,1},... | collective-permute-start | bytes 589832 | tf_op jit(solution)/shard_map/ppermute | solution.py:44
  14.8 0.1 broadcast.23.clone
  14.9 0.9 %constant_dynamic-update-slice_fusion.4 = f32[768,256]{1,0:T(8,128)S(1)} fusion(f32[768,256]{1,0:T(8,128)S(1)} %broadcast.23.clone, f32[192,256]{1,0:T(8,128)} %param.7, s32[]{:T(128)S(6)} %select_n.84), kind=kLoop, calls=%fused_computation.40 | loop fusion | bytes 393220 | tf_op jit(solution)/shard_map/dynamic_update_slice | solution.py:53
  15.8 0.0 collective-permute-done
  15.8 3.6 %collective-permute-done.2 = f32[192,256]{1,0:T(8,128)S(1)} collective-permute-done((f32[192,256]{1,0:T(8,128)S(1)}, f32[192,256]{1,0:T(8,128)S(1)}, u32[]{:S(2)}, u32[]{:S(2)}) %collective-permute-start.2) | collective-permute-done | bytes 196640 | tf_op jit(solution)/shard_map/ppermute | solution.py:44
  19.5 1.3 %pad_maximum_fusion = f32[1536,256]{1,0:T(8,128)} fusion(f32[768,256]{1,0:T(8,128)S(1)} %constant_dynamic-update-slice_fusion.1), kind=kLoop, calls=%fused_computation.1 | loop fusion | flops 393216 | bytes 2359296 | tf_op jit(solution)/shard_map/concatenate | solution.py:88
  20.8 0.0 copy-start.1
  20.8 3.9 %all-to-all-start = ((f32[8,192,256]{2,1,0:T(8,128)}), f32[8,192,256]{2,1,0:T(8,128)S(1)}, u32[]{:S(2)}, u32[]{:S(2)}) async-start(f32[8,192,256]{2,1,0:T(8,128)} %bitcast), calls=%async_computation | async-start | bytes 3145728 | tf_op jit(solution)/shard_map/all_to_all | solution.py:87
  24.6 0.0 copy-start.3
  24.6 0.0 collective-permute-done.5
  24.6 0.0 copy-done.1
  24.6 0.8 pad_maximum_fusion.1
  25.4 0.5 collective-permute-start.6
  25.9 0.1 broadcast.23.clone.1
  26.0 0.0 copy-done.3
  26.0 1.4 %fusion.23 = f32[256,256]{1,0:T(8,128)} fusion(f32[192,256]{1,0:T(8,128)S(1)} %copy-done.1, f32[192,256]{1,0:T(8,128)S(1)} %copy-done.3), kind=kOutput, calls=%fused_computation.47 | convolution fusion | flops 150994944 | bytes 655360 | tf_op jit(solution)/shard_map/dot_general | solution.py:16
  27.4 0.2 collective-permute-done.6
  27.6 0.9 %fusion.5 = f32[768,256]{1,0:T(8,128)S(1)} fusion(f32[768,256]{1,0:T(8,128)S(1)} %constant_dynamic-update-slice_fusion, s32[]{:T(128)S(6)} %select_n.97, f32[2,192,256]{2,1,0:T(8,128)} %collective-permute-done.6), kind=kLoop, calls=%fused_computation.17 | loop fusion | bytes 393220 | tf_op jit(solution)/shard_map/dynamic_update_slice | solution.py:53
  28.6 0.9 %fusion.4 = f32[768,256]{1,0:T(8,128)S(1)} fusion(f32[768,256]{1,0:T(8,128)S(1)} %bitcast_dynamic-update-slice_fusion, s32[]{:T(128)S(6)} %select_n.99, f32[2,192,256]{2,1,0:T(8,128)} %collective-permute-done.6), kind=kLoop, calls=%fused_computation.15 | loop fusion | bytes 393220 | tf_op jit(solution)/shard_map/dynamic_update_slice | solution.py:53
  29.5 16.1 %all-to-all-done = f32[8,192,256]{2,1,0:T(8,128)S(1)} async-done(((f32[8,192,256]{2,1,0:T(8,128)}), f32[8,192,256]{2,1,0:T(8,128)S(1)}, u32[]{:S(2)}, u32[]{:S(2)}) %all-to-all-start) | async-done | bytes 1572896 | tf_op jit(solution)/shard_map/all_to_all | solution.py:87
  45.6 6.2 %fusion.22 = f32[256,768]{1,0:T(8,128)S(1)} fusion(f32[1536,256]{1,0:T(8,128)S(1)} %bitcast.45, f32[768,1536]{1,0:T(8,128)} %param.6), kind=kOutput, calls=%fused_computation.46 | convolution fusion | flops 1811939328 | bytes 7077888 | tf_op jit(solution)/shard_map/dot_general | solution.py:12
  51.9 0.0 copy-start.2
  51.9 0.3 copy.10
  52.1 0.8 dynamic-slice_bitcast_fusion
  52.9 0.5 collective-permute-start.3
  53.5 0.0 copy-done.2
  53.5 2.1 %fusion.1 = f32[32,8,256]{2,1,0:T(8,128)} fusion(f32[256,256]{1,0:T(8,128)S(1)} %copy-done.2, f32[768,256]{1,0:T(8,128)S(1)} %fusion.4, f32[256,768]{1,0:T(8,128)S(1)} %fusion.22), kind=kOutput, calls=%fused_computation.4 | convolution fusion | flops 604110848 | bytes 2097152 | tf_op jit(solution)/shard_map/dot_general | solution.py:16
  55.6 0.0 copy-start.5
  55.6 3.5 %all-to-all-start.1 = ((f32[32,8,256]{2,1,0:T(8,128)}), f32[32,8,256]{2,1,0:T(8,128)S(1)}, u32[]{:S(2)}, u32[]{:S(2)}) async-start(f32[32,8,256]{2,1,0:T(8,128)} %fusion.1), calls=%async_computation.1 | async-start | bytes 524288 | tf_op jit(solution)/shard_map/all_to_all | solution.py:106
  59.1 5.0 %collective-permute-done.3 = f32[2,192,256]{2,1,0:T(8,128)} collective-permute-done((f32[2,192,256]{2,1,0:T(8,128)}, f32[2,192,256]{2,1,0:T(8,128)}, u32[]{:S(2)}, u32[]{:S(2)}) %collective-permute-start.3) | collective-permute-done | bytes 393248 | tf_op jit(solution)/shard_map/ppermute | solution.py:47
  64.1 1.0 %bitcast_add_fusion = f32[2,192,256]{2,1,0:T(8,128)S(1)} fusion(f32[2,192,256]{2,1,0:T(8,128)} %collective-permute-done.3, f32[2,2,192,256]{3,2,1,0:T(8,128)S(1)} %bitcast.47, s32[]{:T(128)S(6)} %select_n.90), kind=kLoop, calls=%fused_computation.7 | loop fusion | flops 98304 | bytes 1179652 | tf_op jit(solution)/shard_map/add | solution.py:100
  65.1 0.0 copy-start.4
  65.1 4.5 %all-to-all-done.1 = f32[32,8,256]{2,1,0:T(8,128)S(1)} async-done(((f32[32,8,256]{2,1,0:T(8,128)}), f32[32,8,256]{2,1,0:T(8,128)S(1)}, u32[]{:S(2)}, u32[]{:S(2)}) %all-to-all-start.1) | async-done | bytes 262176 | tf_op jit(solution)/shard_map/all_to_all | solution.py:106
  69.7 0.0 copy-done
  69.7 1.5 %convolution_subtract_fusion = f32[8,256]{0,1:T(8,128)S(1)} fusion(f32[8,256]{1,0:T(8,128)S(1)} %reduce_sum.9, f32[256,256]{1,0:T(8,128)S(1)} %copy-done, f32[256,256]{1,0:T(8,128)} %param.11, s32[]{:T(128)S(6)} %select_n.95), kind=kOutput, calls=%fused_computation.5 | convolution fusion | flops 6293504 | bytes 286724 | tf_op jit(solution)/shard_map/dot_general | solution.py:12
  71.2 0.0 copy-done.5
  71.2 0.3 fusion.24
  71.5 0.3 fusion.11
  71.8 0.8 tile.2
  72.6 2.6 %all-to-all-start.2 = ((f32[32,8,256]{2,1,0:T(8,128)}), f32[32,8,256]{2,1,0:T(8,128)S(1)}, u32[]{:S(2)}, u32[]{:S(2)}) async-start(f32[32,8,256]{2,1,0:T(8,128)} %tile.2), calls=%async_computation.2 | async-start | bytes 524288 | tf_op jit(solution)/shard_map/all_to_all | solution.py:116
  75.2 0.2 collective-permute-start.4
  75.4 1.3 %collective-permute-done.4 = f32[1,192,256]{2,1,0:T(8,128)S(1)} collective-permute-done((f32[1,192,256]{2,1,0:T(8,128)S(1)}, f32[1,192,256]{2,1,0:T(8,128)S(1)}, u32[]{:S(2)}, u32[]{:S(2)}) %collective-permute-start.4) | collective-permute-done | bytes 196640 | tf_op jit(solution)/shard_map/ppermute | solution.py:47
  76.7 0.0 copy-done.4
  76.7 1.0 %fusion.6 = f32[192,256]{1,0:T(8,128)} fusion(f32[256,256]{1,0:T(8,128)S(1)} %copy-done, f32[192,256]{1,0:T(8,128)S(1)} %copy-done.4, f32[1,192,256]{2,1,0:T(8,128)S(1)} %collective-permute-done.4, f32[2,192,256]{2,1,0:T(8,128)S(1)} %bitcast_add_fusion, s32[]{:T(128)S(6)} %select_n.93), kind=kOutput, calls=%fused_computation.20 | convolution fusion | flops 151142400 | bytes 1048580 | tf_op jit(solution)/shard_map/dot_general | solution.py:12
  77.7 8.0 %all-to-all-done.2 = f32[32,8,256]{2,1,0:T(8,128)S(1)} async-done(((f32[32,8,256]{2,1,0:T(8,128)}), f32[32,8,256]{2,1,0:T(8,128)S(1)}, u32[]{:S(2)}, u32[]{:S(2)}) %all-to-all-start.2) | async-done | bytes 262176 | tf_op jit(solution)/shard_map/all_to_all | solution.py:116
  85.8 0.6 fusion.2
  86.4 2.3 %gather_fusion = f32[256]{0:T(256)S(1)} fusion(f32[256,256]{1,0:T(8,128)S(1)} %fusion.2, s32[256]{0:T(256)S(1)} %bitcast.43), kind=kCustom, calls=%fused_computation | custom fusion | bytes 4096 | tf_op jit(solution)/shard_map/jit(_diag)/jit(diagonal)/cond/branch_0_fun/gather | solution.py:22
  88.7 0.8 multiply_subtract_fusion
  (9 shorter events, 0.2 us)
Async XLA Ops:
  0.6 69.1 %copy-start = (f32[256,256]{1,0:T(8,128)S(1)}, f32[256,256]{1,0:T(8,128)}, u32[]{:S(2)}) copy-start(f32[256,256]{1,0:T(8,128)} %param.10) | copy-start | bytes 786436
  0.6 11.1 %collective-permute-start.1 = (f32[192,256]{1,0:T(8,128)}, f32[192,256]{1,0:T(8,128)S(1)}, u32[]{:S(2)}, u32[]{:S(2)}) collective-permute-start(f32[192,256]{1,0:T(8,128)} %param.7), channel_id=1, source_target_pairs={{0,24},{1,25},{2,26},{3,27},{4,28},{5,29},{6,30},{7,31},{8,16},{9,... | collective-permute-start | bytes 589832 | tf_op jit(solution)/shard_map/ppermute | solution.py:44
  5.8 10.0 %collective-permute-start = (f32[192,256]{1,0:T(8,128)}, f32[192,256]{1,0:T(8,128)S(1)}, u32[]{:S(2)}, u32[]{:S(2)}) collective-permute-start(f32[192,256]{1,0:T(8,128)} %param.7), channel_id=1, source_target_pairs={{0,8},{1,9},{2,10},{3,11},{4,12},{5,13},{6,14},{7,15},{8,0},{9,1},... | collective-permute-start | bytes 589832 | tf_op jit(solution)/shard_map/ppermute | solution.py:44
  5.8 18.9 %collective-permute-start.5 = (f32[1,192,256]{2,1,0:T(8,128)}, f32[1,192,256]{2,1,0:T(8,128)S(1)}, u32[]{:S(2)}, u32[]{:S(2)}) collective-permute-start(f32[1,192,256]{2,1,0:T(8,128)} %bitcast.48), channel_id=1, source_target_pairs={{0,2},{1,3},{2,0},{3,1},{4,6},{5,7},{6,4},{7,5},{8,10},{9,11},{10,... | collective-permute-start | bytes 589832 | tf_op jit(solution)/shard_map/ppermute | solution.py:47
  11.8 7.7 %collective-permute-start.2 = (f32[192,256]{1,0:T(8,128)S(1)}, f32[192,256]{1,0:T(8,128)S(1)}, u32[]{:S(2)}, u32[]{:S(2)}) collective-permute-start(f32[192,256]{1,0:T(8,128)S(1)} %collective-permute-done.1), channel_id=1, source_target_pairs={{0,8},{1,9},{2,10},{3,11},{4,12},{5,13},{6,14},{7,15},{8,0},{9,1},... | collective-permute-start | bytes 589832 | tf_op jit(solution)/shard_map/ppermute | solution.py:44
  20.8 3.9 %copy-start.1 = (f32[192,256]{1,0:T(8,128)S(1)}, f32[192,256]{1,0:T(8,128)}, u32[]{:S(2)}) copy-start(f32[192,256]{1,0:T(8,128)} %param.7) | copy-start | bytes 589828
  20.8 24.9 %all-to-all-start = ((f32[8,192,256]{2,1,0:T(8,128)}), f32[8,192,256]{2,1,0:T(8,128)S(1)}, u32[]{:S(2)}, u32[]{:S(2)}) async-start(f32[8,192,256]{2,1,0:T(8,128)} %bitcast), calls=%async_computation | async-start | bytes 3145728 | tf_op jit(solution)/shard_map/all_to_all | solution.py:87
  24.6 1.4 %copy-start.3 = (f32[192,256]{1,0:T(8,128)S(1)}, f32[192,256]{1,0:T(8,128)}, u32[]{:S(2)}) copy-start(f32[192,256]{1,0:T(8,128)} %param.8) | copy-start | bytes 589828
  25.4 2.2 %collective-permute-start.6 = (f32[2,192,256]{2,1,0:T(8,128)}, f32[2,192,256]{2,1,0:T(8,128)}, u32[]{:S(2)}, u32[]{:S(2)}) collective-permute-start(f32[2,192,256]{2,1,0:T(8,128)} %pad_maximum_fusion.1), channel_id=1, source_target_pairs={{0,1},{1,0},{2,3},{3,2},{4,5},{5,4},{6,7},{7,6},{8,9},{9,8},{10,11... | collective-permute-start | bytes 1179656 | tf_op jit(solution)/shard_map/ppermute | solution.py:47
  51.9 1.6 %copy-start.2 = (f32[256,256]{1,0:T(8,128)S(1)}, f32[256,256]{1,0:T(8,128)}, u32[]{:S(2)}) copy-start(f32[256,256]{1,0:T(8,128)} %fusion.23) | copy-start | bytes 786436
  52.9 11.1 %collective-permute-start.3 = (f32[2,192,256]{2,1,0:T(8,128)}, f32[2,192,256]{2,1,0:T(8,128)}, u32[]{:S(2)}, u32[]{:S(2)}) collective-permute-start(f32[2,192,256]{2,1,0:T(8,128)} %dynamic-slice_bitcast_fusion), channel_id=1, source_target_pairs={{0,2},{1,3},{2,0},{3,1},{4,6},{5,7},{6,4},{7,5},{8,10},{9,11},{10,... | collective-permute-start | bytes 1179656 | tf_op jit(solution)/shard_map/ppermute | solution.py:47
  55.6 15.7 %copy-start.5 = (f32[256,256]{1,0:T(8,128)S(1)}, f32[256,256]{1,0:T(8,128)}, u32[]{:S(2)}) copy-start(f32[256,256]{1,0:T(8,128)} %param.9) | copy-start | bytes 786436
  55.6 14.1 %all-to-all-start.1 = ((f32[32,8,256]{2,1,0:T(8,128)}), f32[32,8,256]{2,1,0:T(8,128)S(1)}, u32[]{:S(2)}, u32[]{:S(2)}) async-start(f32[32,8,256]{2,1,0:T(8,128)} %fusion.1), calls=%async_computation.1 | async-start | bytes 524288 | tf_op jit(solution)/shard_map/all_to_all | solution.py:106
  65.1 11.6 %copy-start.4 = (f32[192,256]{1,0:T(8,128)S(1)}, f32[192,256]{1,0:T(8,128)}, u32[]{:S(2)}) copy-start(f32[192,256]{1,0:T(8,128)} %param.8) | copy-start | bytes 589828
  72.6 13.2 %all-to-all-start.2 = ((f32[32,8,256]{2,1,0:T(8,128)}), f32[32,8,256]{2,1,0:T(8,128)S(1)}, u32[]{:S(2)}, u32[]{:S(2)}) async-start(f32[32,8,256]{2,1,0:T(8,128)} %tile.2), calls=%async_computation.2 | async-start | bytes 524288 | tf_op jit(solution)/shard_map/all_to_all | solution.py:116
  75.2 1.5 %collective-permute-start.4 = (f32[1,192,256]{2,1,0:T(8,128)S(1)}, f32[1,192,256]{2,1,0:T(8,128)S(1)}, u32[]{:S(2)}, u32[]{:S(2)}) collective-permute-start(f32[1,192,256]{2,1,0:T(8,128)S(1)} %constant_dynamic-slice_fusion), channel_id=1, source_target_pairs={{0,1},{1,0},{2,3},{3,2},{4,5},{5,4},{6,7},{7,6},{8,9},{9,8},{10,11... | collective-permute-start | bytes 589832 | tf_op jit(solution)/shard_map/ppermute | solution.py:47

commit v2 on v1

v2 whole, which is shorter than its diff:
```python
import functools

import jax
import jax.numpy as jnp
from jax import lax
from jax.experimental import pallas as pl
from jax.experimental.pallas import tpu as pltpu
from jax.sharding import PartitionSpec as P

HIGHEST = lax.Precision.HIGHEST
AXES = ("row", "col")
VMEM = pl.BlockSpec(memory_space=pltpu.VMEM)
SMEM = pl.BlockSpec(memory_space=pltpu.SMEM)
LIMIT = 48 * 1024 * 1024


def dot(a, b, precision=HIGHEST):
    return jnp.dot(a, b, precision=precision, preferred_element_type=jnp.float32)


def dot_t(a, b, precision=HIGHEST):
    return lax.dot_general(
        a, b, (((0,), (0,)), ((), ())), precision=precision, preferred_element_type=jnp.float32
    )


def parts(x):
    high = lax.reduce_precision(x, 8, 7)
    return high.astype(jnp.bfloat16), (x - high).astype(jnp.bfloat16)


def kernel_parts(x):
    high = x.astype(jnp.bfloat16)
    return high, (x - high.astype(jnp.float32)).astype(jnp.bfloat16)


def product_kernel(
    group, cols, height, half, last,
    place, a_high, a_low, pieces, rowt_high, rowt_low, start, before, keep, send, gram_t, wide, split,
):
    step = pl.program_id(0)
    col, plane = place[0], place[1]

    @pl.when(step == 0)
    def _():
        for y in range(group):
            for c in range(cols):
                high, low = kernel_parts(pieces[y * cols + (plane ^ c)])
                at = pl.ds((y * cols + c) * height, height)
                wide[at, :half] = high
                wide[at, half:] = low

    both = dot(a_high[...], wide[...], None) + dot(a_low[...], wide[...], None)
    block = both[:, :half] + both[:, half:]
    target = step ^ col
    near = cols // 2

    @pl.when(target < near)
    def _():
        keep[target] = block

    @pl.when(target >= near)
    def _():
        send[target - near] = block

    at = pl.ds(pl.multiple_of(step * height, height), height)
    high, low = kernel_parts(block)
    split[at, :half] = high
    split[at, half:] = low

    @pl.when(step == cols - 1)
    def _():
        total = dot(rowt_high[...], split[...], None) + dot(rowt_low[...], split[...], None)
        total = total[:, :half] + total[:, half:]
        if last:
            gram_t[:, :half] = before[...]
            gram_t[:, half:] = start[:, half:] - 2.0 * total
        else:
            gram_t[...] = start[:, :half] - 2.0 * total


def half_product(place, a_high, a_low, pieces, rowt_high, rowt_low, start, before, group, cols, last):
    rows, width = a_high.shape
    height, half = pieces.shape[1], pieces.shape[2]
    size = rowt_high.shape[0]
    whole = lambda *shape: pl.BlockSpec(shape, lambda i: (0,) * len(shape))
    near = cols // 2
    gram_width = size if last else half
    return pl.pallas_call(
        functools.partial(product_kernel, group, cols, height, half, last),
        grid=(cols,),
        in_specs=[
            SMEM,
            pl.BlockSpec((height, width), lambda i: (i, 0)),
            pl.BlockSpec((height, width), lambda i: (i, 0)),
            whole(*pieces.shape),
            whole(*rowt_high.shape),
            whole(*rowt_low.shape),
            whole(*start.shape),
            whole(*before.shape),
        ],
        out_specs=[whole(near, height, half), whole(cols - near, height, half), whole(size, gram_width)],
        out_shape=[
            jax.ShapeDtypeStruct((near, height, half), jnp.float32),
            jax.ShapeDtypeStruct((cols - near, height, half), jnp.float32),
            jax.ShapeDtypeStruct((size, gram_width), jnp.float32),
        ],
        scratch_shapes=[
            pltpu.VMEM((width, 2 * half), jnp.bfloat16),
            pltpu.VMEM((rows, 2 * half), jnp.bfloat16),
        ],
        compiler_params=pltpu.CompilerParams(vmem_limit_bytes=LIMIT),
        cost_estimate=pl.CostEstimate(
            flops=8 * rows * width * half, bytes_accessed=4 * rows * width, transcendentals=0
        ),
        name="half_product",
    )(place, a_high, a_low, pieces, rowt_high, rowt_low, start, before)


def middle_kernel(devices, share, place, shares, adjoint_t, factor, inverse, out):
    total = shares[pl.ds(0, share), :]
    for i in range(1, devices):
        total = total + shares[pl.ds(i * share, share), :]
    inner_t = dot(adjoint_t[...] - dot(total, inverse[...]), factor[...])
    at = lax.broadcasted_iota(jnp.int32, inner_t.shape, 0) + place[2] * share
    across = lax.broadcasted_iota(jnp.int32, inner_t.shape, 1)
    inner_t = jnp.where(across > at, inner_t, jnp.where(across == at, 0.5 * inner_t, 0.0))
    left_t = dot(inner_t, inverse[...])
    for i in range(devices):
        out[pl.ds(i * share, share), :] = left_t


def last_kernel(left_t, inverse, out):
    full = dot_t(left_t[...], inverse[...])
    at = lax.broadcasted_iota(jnp.int32, full.shape, 0)
    across = lax.broadcasted_iota(jnp.int32, full.shape, 1)
    out[...] = jnp.where(across < at, full, jnp.where(across == at, 0.5 * full, 0.0))


def panel_kernel(count, adjoint, inverse, *refs):
    sums, out = refs[:-1], refs[-1]
    images = [sums[2 * i][...] + sums[2 * i + 1][...] for i in range(count)]
    image = jnp.concatenate(images, axis=1)
    out[...] = dot(adjoint[...] - 2.0 * image, inverse[...])


def call(kernel, shape, *args, name):
    return pl.pallas_call(
        kernel,
        out_shape=jax.ShapeDtypeStruct(shape, jnp.float32),
        in_specs=[SMEM if x.dtype == jnp.int32 else VMEM for x in args],
        out_specs=VMEM,
        compiler_params=pltpu.CompilerParams(vmem_limit_bytes=LIMIT),
        name=name,
    )(*args)


def make_on_device(rows, cols):
    group = rows // cols
    devices = rows * cols

    def index(plane, y, c):
        return (plane * group + y) * cols + c

    def plane_flip(mask):
        return [
            (index(p, y, c), index(p ^ mask, y, c))
            for p in range(cols) for y in range(group) for c in range(cols)
        ]

    def col_flip(mask):
        return [(r * cols + c, r * cols + (c ^ mask)) for r in range(rows) for c in range(cols)]

    planes = [[index(p, y, p ^ d) for y in range(group) for d in range(cols)] for p in range(cols)]

    def flip_plane(x, mask):
        return lax.ppermute(x, AXES, plane_flip(mask))

    def flip_col(x, mask):
        return lax.ppermute(x, AXES, col_flip(mask))

    def along_planes(panel):
        pieces = [panel] + [None] * (cols - 1)
        if cols == 4:
            pieces[3] = flip_plane(panel, 3)
            pieces[1] = flip_plane(panel, 1)
            pieces[2] = flip_plane(pieces[3], 1)
        else:
            for d in range(1, cols):
                pieces[d] = flip_plane(panel, d)
        return pieces

    def of_row(panel, col_place):
        height = panel.shape[0]
        gathered, order, mask = panel[None], [0], cols // 2
        while mask:
            gathered = jnp.concatenate([gathered, flip_col(gathered, mask)])
            order = order + [o ^ mask for o in order]
            mask //= 2
        out = jnp.zeros((cols * height, panel.shape[1]), panel.dtype)
        for i, d in enumerate(order):
            out = lax.dynamic_update_slice_in_dim(out, gathered[i], (col_place ^ d) * height, 0)
        return out

    def on_device(trail_adjoint, panel, panel_adjoint, diag_factor, diag_inverse, diag_adjoint):
        height, size = panel.shape
        half = size // 2
        row_place = lax.axis_index("row")
        col_place = lax.axis_index("col")
        me = row_place * cols + col_place
        place = jnp.stack([col_place, row_place // group, me]).astype(jnp.int32)

        halves = []
        for h in range(2):
            pieces = jnp.stack(along_planes(panel[:, h * half : (h + 1) * half]) * group)
            halves.append(
                lax.all_to_all(pieces, AXES, 0, 0, axis_index_groups=planes, tiled=True)
            )
        rowt_high, rowt_low = parts(of_row(panel, col_place).T)
        a_high, a_low = parts(trail_adjoint)
        start = dot_t(panel, panel_adjoint)

        sums = []
        gram_t = start
        for h in range(2):
            keep, send, gram_t = half_product(
                place, a_high, a_low, halves[h], rowt_high, rowt_low, start, gram_t,
                group, cols, h == 1,
            )
            mask = cols // 2
            while mask:
                came = flip_col(send, mask)
                mask //= 2
                if mask:
                    keep, send = keep[:mask] + came[:mask], keep[mask:] + came[mask:]
            sums += [keep[0], came[0]]

        share = size // devices
        shares = lax.all_to_all(gram_t, AXES, 0, 0, tiled=True)
        adjoint_t = lax.dynamic_slice_in_dim(diag_adjoint.T, me * share, share, 0)
        if share % 8 == 0:
            left_t = call(
                functools.partial(middle_kernel, devices, share), (size, size),
                place, shares, adjoint_t, diag_factor, diag_inverse, name="middle",
            )
        else:
            total = jnp.sum(shares.reshape(devices, share, size), axis=0)
            inner_t = dot(adjoint_t - dot(total, diag_inverse), diag_factor)
            at = lax.broadcasted_iota(jnp.int32, inner_t.shape, 0) + me * share
            across = lax.broadcasted_iota(jnp.int32, inner_t.shape, 1)
            inner_t = jnp.where(across > at, inner_t, jnp.where(across == at, 0.5 * inner_t, 0.0))
            left_t = jnp.tile(dot(inner_t, diag_inverse), (devices, 1))
        left_t = lax.all_to_all(left_t, AXES, 0, 0, tiled=True)
        diag_grad = call(last_kernel, (size, size), left_t, diag_inverse, name="diag_grad")
        panel_grad = call(
            functools.partial(panel_kernel, 2), panel.shape,
            panel_adjoint, diag_inverse, *sums, name="panel_grad",
        )
        return panel_grad, diag_grad

    return on_device


def solution(mesh):
    in_specs = (P("row", "col"), P(("row", "col"), None), P(("row", "col"), None), P(), P(), P())
    out_specs = (P(("row", "col"), None), P())
    return jax.shard_map(
        make_on_device(mesh.shape["row"], mesh.shape["col"]),
        mesh=mesh, in_specs=in_specs, out_specs=out_specs, check_vma=False,
    )
```

time: 90 us -> 108 us (1.20)
  local copies, waits for them, and re-layouts: 7.25 us -> 36 us
  waiting for transfers between devices: 43.2 us -> 18 us
  Pallas kernels: 0 us -> 13.3 us
  matrix products: 13.4 us -> 0.66 us
  starting transfers between devices: 20.8 us -> 28.8 us
  other arithmetic: 3.98 us -> 9.51 us
    unnamed x12 -> x47, local copies, waits for them, and re-layouts: 0.03 us -> 21.4 us
    pallas_call x0 -> x5, Pallas kernels: none -> 13.3 us  [the longest x2 9.08 us: half_product(): pl.pallas_call(functools.partial(product_kernel, group, cols, height, hal...]
    all_to_all x3 -> x4, waiting for transfers between devices: 28.7 us -> 17 us  [the longest x1 8.31 us: on_device(): shares = lax.all_to_all(gram_t, AXES, 0, 0, tiled=True)]
    dot_general x5 -> x0, matrix products: 9.32 us -> none  [dot(): jnp.dot(a, b, precision=precision, preferred_element_type=jnp.float32)]
    ppermute x3 -> x6, waiting for transfers between devices: 8.06 us -> 0.02 us  [flip_plane(): return lax.ppermute(x, AXES, plane_flip(mask))]
    convert_element_type x0 -> x2, other arithmetic: none -> 5.71 us  [parts(): return (high.astype(jnp.bfloat16), (x - high).astype(jnp.bfloat16))]
    ppermute x4 -> x6, waiting for transfers between devices: 6.52 us -> 0.95 us  [flip_col(): return lax.ppermute(x, AXES, col_flip(mask))]
    dynamic_update_slice x8 -> x4, local copies, waits for them, and re-layouts: 2.93 us -> 7.73 us  [of_row(): lax.dynamic_update_slice_in_dim(out, gathered[i], (col_place ^ d) * heigh...]
  transfers between devices with their start and end apart: 10 -> 16, of which waited for: 8 -> 4; matrix products, arithmetic and copies ran while one was open for 12% -> 34% of each run, Pallas kernels for 0% -> 7%
where the time goes in v2:
time: 108 us; the launch traced here: 107 us
  local copies, waits for them, and re-layouts  36 us (33%)
  starting transfers between devices  28.8 us (27%)
  waiting for transfers between devices  18 us (17%)
  Pallas kernels  13.3 us (12%)
  other arithmetic  9.51 us (9%)
    unnamed x47, local copies, waits for them, and re-layouts  21.4 us
    ppermute x6, starting transfers between devices, flip_plane(): return lax.ppermute(x, AXES, plane_flip(mask))  9.1 us
    pallas_call x2, Pallas kernels, half_product(): pl.pallas_call(functools.partial(product_kernel, group, cols, height, hal...  9.08 us
    all_to_all x2, starting transfers between devices, on_device(): lax.all_to_all(pieces, AXES, 0, 0, axis_index_groups=planes, tiled=True)  8.42 us
    all_to_all x1, waiting for transfers between devices, on_device(): shares = lax.all_to_all(gram_t, AXES, 0, 0, tiled=True)  8.31 us
    dynamic_update_slice x4, local copies, waits for them, and re-layouts, of_row(): lax.dynamic_update_slice_in_dim(out, gathered[i], (col_place ^ d) * heigh...  7.73 us
    convert_element_type x2, other arithmetic, parts(): return (high.astype(jnp.bfloat16), (x - high).astype(jnp.bfloat16))  5.71 us
    all_to_all x1, waiting for transfers between devices, on_device(): left_t = lax.all_to_all(left_t, AXES, 0, 0, tiled=True)  5.11 us
  transfers between devices with their start and end apart: 16, of which 4 were waited for; matrix products, arithmetic and copies ran while one was open for 34% of the time, Pallas kernels for 7%

profile of v2, /device:TPU:0, one launch (start us, length us, event | category | flops | bytes accessed | tf_op | source)
XLA Modules:
  0.0 107.1 jit_solution(1340544812231445648)
XLA Ops:
  0.6 1.7 %fusion.4 = (f32[192,128]{1,0:T(8,128)}, f32[192,128]{1,0:T(8,128)}) fusion(f32[192,256]{1,0:T(8,128)} %param.7), kind=kLoop, calls=%fused_computation.33 | loop fusion | bytes 393216 | tf_op jit(solution)/shard_map/slice | solution.py:215
  2.3 3.0 %collective-permute-start.7 = (f32[192,128]{1,0:T(8,128)}, f32[192,128]{1,0:T(8,128)}, u32[]{:S(2)}, u32[]{:S(2)}) collective-permute-start(f32[192,128]{1,0:T(8,128)} %get-tuple-element.26), channel_id=1, source_target_pairs={{0,8},{1,9},{2,10},{3,11},{4,12},{5,13},{6,14},{7,15},{8,0},{9,1},... | collective-permute-start | bytes 294920 | tf_op jit(solution)/shard_map/ppermute | solution.py:177
  5.3 2.5 %collective-permute-start.8 = (f32[192,128]{1,0:T(8,128)}, f32[192,128]{1,0:T(8,128)S(1)}, u32[]{:S(2)}, u32[]{:S(2)}) collective-permute-start(f32[192,128]{1,0:T(8,128)} %get-tuple-element.26), channel_id=1, source_target_pairs={{0,24},{1,25},{2,26},{3,27},{4,28},{5,29},{6,30},{7,31},{8,16},{9,... | collective-permute-start | bytes 294920 | tf_op jit(solution)/shard_map/ppermute | solution.py:177
  7.8 0.7 collective-permute-start
  8.5 0.9 collective-permute-start.1
  9.4 1.1 copy.8
  10.5 1.6 %collective-permute-start.3 = (f32[1,192,256]{1,2,0:T(8,128)S(1)}, f32[1,192,256]{1,2,0:T(8,128)}, u32[]{:S(2)}, u32[]{:S(2)}) collective-permute-start(f32[1,192,256]{1,2,0:T(8,128)S(1)} %bitcast.55), channel_id=1, source_target_pairs={{0,2},{1,3},{2,0},{3,1},{4,6},{5,7},{6,4},{7,5},{8,10},{9,11},{10,... | collective-permute-start | bytes 589832 | tf_op jit(solution)/shard_map/ppermute | solution.py:180
  12.0 4.5 %fusion = (bf16[768,1536]{1,0:T(8,128)(2,1)}, bf16[768,1536]{1,0:T(8,128)(2,1)S(1)}) fusion(f32[768,1536]{1,0:T(8,128)} %param.6), kind=kLoop, calls=%fused_computation.2 | loop fusion | flops 4718592 | bytes 9437184 | tf_op jit(solution)/shard_map/convert_element_type | solution.py:29
  16.5 0.7 bitcast_dynamic-update-slice_fusion.6
  17.2 0.9 collective-permute-start.9
  18.1 1.1 %collective-permute-start.2 = (f32[192,128]{1,0:T(8,128)}, f32[192,128]{1,0:T(8,128)S(1)}, u32[]{:S(2)}, u32[]{:S(2)}) collective-permute-start(f32[192,128]{1,0:T(8,128)} %collective-permute-done.1), channel_id=1, source_target_pairs={{0,8},{1,9},{2,10},{3,11},{4,12},{5,13},{6,14},{7,15},{8,0},{9,1},... | collective-permute-start | bytes 294920 | tf_op jit(solution)/shard_map/ppermute | solution.py:177
  19.2 1.5 %bitcast_dynamic-update-slice_fusion.4 = f32[8,192,128]{2,1,0:T(8,128)} fusion(f32[8,192,128]{2,1,0:T(8,128)} %get-tuple-element.28, f32[192,128]{1,0:T(8,128)} %collective-permute-done.7), kind=kLoop, calls=%fused_computation.19 | loop fusion | bytes 196608
  20.8 1.5 %bitcast_dynamic-update-slice_fusion.12 = f32[8,192,128]{2,1,0:T(8,128)} fusion(f32[8,192,128]{2,1,0:T(8,128)} %get-tuple-element.29, f32[192,128]{1,0:T(8,128)} %collective-permute-done), kind=kLoop, calls=%fused_computation.27 | loop fusion | bytes 196608
  22.3 0.7 bitcast_dynamic-update-slice_fusion.2
  23.0 0.6 bitcast_dynamic-update-slice_fusion
  23.6 0.6 bitcast_dynamic-update-slice_fusion.10
  24.3 1.5 %bitcast_dynamic-update-slice_fusion.8 = f32[8,192,128]{2,1,0:T(8,128)} fusion(f32[8,192,128]{2,1,0:T(8,128)} %bitcast_dynamic-update-slice_fusion.10, f32[192,128]{1,0:T(8,128)} %collective-permute-done.1), kind=kLoop, calls=%fused_computation.23 | loop fusion | bytes 196608
  25.8 0.7 bitcast_dynamic-update-slice_fusion.7
  26.5 1.6 %bitcast_dynamic-update-slice_fusion.5 = (f32[8,192,128]{2,1,0:T(8,128)}, f32[8,192,128]{2,1,0:T(8,128)}) fusion(f32[8,192,128]{2,1,0:T(8,128)} %get-tuple-element.24, f32[192,128]{1,0:T(8,128)} %collective-permute-done.7, f32[8,192,128]{2,1,0:T(8,128)} %get-tuple-element.25, f32[192,128]{1,0:T(8,128)} %collective-permute-done), kind=kLoop, calls=%fused_computation.20 | loop fusion | bytes 393216
  28.1 0.6 bitcast_dynamic-update-slice_fusion.11
  28.8 1.5 %bitcast_dynamic-update-slice_fusion.9 = f32[8,192,128]{2,1,0:T(8,128)} fusion(f32[8,192,128]{2,1,0:T(8,128)} %bitcast_dynamic-update-slice_fusion.11, f32[192,128]{1,0:T(8,128)} %collective-permute-done.1), kind=kLoop, calls=%fused_computation.24 | loop fusion | bytes 196608 | tf_op jit(solution)/shard_map/stack | solution.py:215
  30.3 4.2 %all-to-all-start = ((f32[8,192,128]{2,1,0:T(8,128)}), f32[8,192,128]{2,1,0:T(8,128)}, u32[]{:S(2)}, u32[]{:S(2)}) async-start(f32[8,192,128]{2,1,0:T(8,128)} %bitcast_dynamic-update-slice_fusion.9), calls=%async_computation | async-start | bytes 1572864 | tf_op jit(solution)/shard_map/all_to_all | solution.py:217
  34.5 0.7 fusion.5.start.before
  35.2 1.0 broadcast_in_dim.6
  36.2 1.9 %dynamic_update_slice.12 = f32[768,256]{0,1:T(8,128)} dynamic-update-slice(f32[768,256]{0,1:T(8,128)} %broadcast_in_dim.6, f32[192,256]{0,1:T(8,128)S(1)} %copy.8, s32[]{:T(128)S(6)} %select_n.21, s32[]{:T(128)} %constant.30.clone.1) | dynamic-update-slice | bytes 393220 | tf_op jit(solution)/shard_map/dynamic_update_slice | solution.py:202
  38.1 1.8 %pad_maximum_fusion = f32[2,192,256]{1,2,0:T(8,128)} fusion(f32[1,192,256]{1,2,0:T(8,128)} %collective-permute-done.3, f32[1,192,256]{1,2,0:T(8,128)S(1)} %bitcast.56), kind=kLoop, calls=%fused_computation.6 | loop fusion | flops 98304 | bytes 786432 | tf_op jit(solution)/shard_map/concatenate | solution.py:197
  39.9 0.6 collective-permute-start.4
  40.5 1.5 %bitcast_dynamic-update-slice_fusion.3 = f32[8,192,128]{2,1,0:T(8,128)} fusion(f32[8,192,128]{2,1,0:T(8,128)} %get-tuple-element.30, f32[192,128]{1,0:T(8,128)} %copy-done.16), kind=kLoop, calls=%fused_computation.18 | loop fusion | bytes 196608
  42.0 1.5 %bitcast_dynamic-update-slice_fusion.1 = f32[8,192,128]{2,1,0:T(8,128)} fusion(f32[8,192,128]{2,1,0:T(8,128)} %bitcast_dynamic-update-slice_fusion.3, f32[192,128]{1,0:T(8,128)} %copy-done.15), kind=kLoop, calls=%fused_computation.16 | loop fusion | bytes 196608 | tf_op jit(solution)/shard_map/stack | solution.py:215
  43.6 3.6 %all-to-all-done.pieces = f32[8,192,128]{2,1,0:T(8,128)} async-done(((f32[8,192,128]{2,1,0:T(8,128)}), f32[8,192,128]{2,1,0:T(8,128)}, u32[]{:S(2)}, u32[]{:S(2)}) %all-to-all-start) | async-done | bytes 786464 | tf_op jit(solution)/shard_map/all_to_all | solution.py:217
  47.1 4.2 %all-to-all-start.1 = ((f32[8,192,128]{2,1,0:T(8,128)}), f32[8,192,128]{2,1,0:T(8,128)}, u32[]{:S(2)}, u32[]{:S(2)}) async-start(f32[8,192,128]{2,1,0:T(8,128)} %bitcast_dynamic-update-slice_fusion.1), calls=%async_computation.1 | async-start | bytes 1572864 | tf_op jit(solution)/shard_map/all_to_all | solution.py:217
  51.4 1.9 %dynamic_update_slice.13 = f32[768,256]{0,1:T(8,128)} dynamic-update-slice(f32[768,256]{0,1:T(8,128)} %dynamic_update_slice.12, f32[192,256]{0,1:T(8,128)} %bitcast.8, s32[]{:T(128)S(6)} %select_n.22, s32[]{:T(128)} %constant.30.clone.1) | dynamic-update-slice | bytes 393220 | tf_op jit(solution)/shard_map/dynamic_update_slice | solution.py:202
  53.3 1.1 slice_bitcast_fusion
  54.4 2.1 %dynamic_update_slice.14 = f32[768,256]{0,1:T(8,128)} dynamic-update-slice(f32[768,256]{0,1:T(8,128)} %dynamic_update_slice.13, f32[192,256]{0,1:T(8,128)S(1)} %get-tuple-element.19, s32[]{:T(128)S(6)} %select_n.23, s32[]{:T(128)} %constant.30.clone.1) | dynamic-update-slice | bytes 393220 | tf_op jit(solution)/shard_map/dynamic_update_slice | solution.py:202
  56.5 1.9 %dynamic_update_slice.15 = f32[768,256]{0,1:T(8,128)} dynamic-update-slice(f32[768,256]{0,1:T(8,128)} %dynamic_update_slice.14, f32[192,256]{0,1:T(8,128)S(1)} %get-tuple-element.18, s32[]{:T(128)S(6)} %select_n.24, s32[]{:T(128)} %constant.30.clone.1) | dynamic-update-slice | bytes 393220 | tf_op jit(solution)/shard_map/dynamic_update_slice | solution.py:202
  58.4 1.2 %fusion.1 = (bf16[256,768]{1,0:T(8,128)(2,1)S(1)}, bf16[256,768]{1,0:T(8,128)(2,1)S(1)}) fusion(f32[768,256]{0,1:T(8,128)} %dynamic_update_slice.15), kind=kLoop, calls=%fused_computation.5 | loop fusion | flops 786432 | bytes 1572864 | tf_op jit(solution)/shard_map/convert_element_type | solution.py:29
  59.6 4.6 %half_product.2 = (f32[2,192,128]{2,1,0:T(8,128)S(1)}, f32[2,192,128]{2,1,0:T(8,128)S(1)}, f32[256,128]{1,0:T(8,128)S(1)}) custom-call(s32[3]{0:T(128)S(1)} %pad_add_fusion.place, bf16[768,1536]{1,0:T(8,128)(2,1)S(1)} %get-tuple-element.15.a_high, bf16[768,1536]{1,0:T(8,128)(2,1)} %get-tuple-element.14.a_low, f32[8,192,128]{2,1,0:T(8,128)} %all-to-all-done.pieces, ...), custom_call_target="tpu_custom_call" | custom-call | flops 1207959552 | bytes 4718592 | tf_op jit(solution)/shard_map/half_product/pallas_call | solution.py:89
  64.2 0.7 copy-done.1
  64.9 0.7 copy-done.9
  65.6 0.7 copy-done.10
  66.2 0.7 copy-done.13
  66.9 1.0 copy-done.2
  67.9 0.9 copy-done.11
  68.8 4.5 %half_product.3 = (f32[2,192,128]{2,1,0:T(8,128)S(1)}, f32[2,192,128]{2,1,0:T(8,128)S(1)}, f32[256,256]{1,0:T(8,128)S(1)}) custom-call(s32[3]{0:T(128)S(1)} %pad_add_fusion.place, bf16[768,1536]{1,0:T(8,128)(2,1)S(1)} %get-tuple-element.15.a_high, bf16[768,1536]{1,0:T(8,128)(2,1)} %get-tuple-element.14.a_low, f32[8,192,128]{2,1,0:T(8,128)} %all-to-all-done.1.pieces, ...), custom_call_target="tpu_custom_call" | custom-call | flops 1207959552 | bytes 4718592 | tf_op jit(solution)/shard_map/half_product/pallas_call | solution.py:89
  73.3 0.7 copy-done.6
  74.0 0.7 copy-done.8
  74.7 0.7 copy-done.12
  75.4 3.7 %all-to-all-start.2 = ((f32[32,8,256]{2,1,0:T(8,128)}), f32[32,8,256]{2,1,0:T(8,128)S(1)}, u32[]{:S(2)}, u32[]{:S(2)}) async-start(f32[32,8,256]{2,1,0:T(8,128)} %bitcast.51), calls=%async_computation.2 | async-start | bytes 524288 | tf_op jit(solution)/shard_map/all_to_all | solution.py:239
  79.1 1.8 %collective-permute-start.5 = (f32[2,192,128]{2,1,0:T(8,128)}, f32[2,192,128]{2,1,0:T(8,128)S(1)}, u32[]{:S(2)}, u32[]{:S(2)}) collective-permute-start(f32[2,192,128]{2,1,0:T(8,128)} %copy-done.13), channel_id=1, source_target_pairs={{0,2},{1,3},{2,0},{3,1},{4,6},{5,7},{6,4},{7,5},{8,10},{9,11},{10,... | collective-permute-start | bytes 589832 | tf_op jit(solution)/shard_map/ppermute | solution.py:180
  80.9 0.1 constant_dynamic-slice_fusion
  81.1 0.3 collective-permute-start.10
  81.4 8.3 %all-to-all-done.2 = f32[32,8,256]{2,1,0:T(8,128)S(1)} async-done(((f32[32,8,256]{2,1,0:T(8,128)}), f32[32,8,256]{2,1,0:T(8,128)S(1)}, u32[]{:S(2)}, u32[]{:S(2)}) %all-to-all-start.2) | async-done | bytes 262176 | tf_op jit(solution)/shard_map/all_to_all | solution.py:239
  89.7 0.9 copy-done.7
  90.7 2.1 %middle.1 = f32[256,256]{1,0:T(8,128)} custom-call(s32[3]{0:T(128)S(1)} %pad_add_fusion.place, f32[256,256]{1,0:T(8,128)S(1)} %bitcast.50, f32[8,256]{1,0:T(8,128)S(1)} %bitcast.54, f32[256,256]{1,0:T(8,128)S(1)} %copy-done.7, f32[256,256]{1,0:T(8,128)S(1)} %copy-done.3), custom_call_target="tpu_custom_call" | custom-call | tf_op jit(solution)/shard_map/middle/pallas_call | solution.py:148
  92.8 2.6 %all-to-all-start.3 = ((f32[32,8,256]{2,1,0:T(8,128)}), f32[32,8,256]{2,1,0:T(8,128)S(1)}, u32[]{:S(2)}, u32[]{:S(2)}) async-start(f32[32,8,256]{2,1,0:T(8,128)} %bitcast.23), calls=%async_computation.3 | async-start | bytes 524288 | tf_op jit(solution)/shard_map/all_to_all | solution.py:253
  95.4 1.0 slice_add_fusion.2
  96.3 0.2 collective-permute-start.6
  96.5 1.0 slice_add_fusion
  97.5 0.5 collective-permute-start.11
  98.0 0.9 collective-permute-done.11
  98.9 0.9 copy-done.5
  99.8 1.0 panel_grad.1
  100.8 5.1 %all-to-all-done.3 = f32[32,8,256]{2,1,0:T(8,128)S(1)} async-done(((f32[32,8,256]{2,1,0:T(8,128)}), f32[32,8,256]{2,1,0:T(8,128)S(1)}, u32[]{:S(2)}, u32[]{:S(2)}) %all-to-all-start.3) | async-done | bytes 262176 | tf_op jit(solution)/shard_map/all_to_all | solution.py:253
  106.0 1.1 %diag_grad.1 = f32[256,256]{1,0:T(8,128)} custom-call(f32[256,256]{1,0:T(8,128)S(1)} %bitcast.49, f32[256,256]{1,0:T(8,128)S(1)} %copy-done.3), custom_call_target="tpu_custom_call" | custom-call | tf_op jit(solution)/shard_map/diag_grad/pallas_call | solution.py:148
  (37 shorter events, 0.2 us)
Async XLA Ops:
  0.6 80.3 %copy-start = (f32[256,256]{1,0:T(8,128)S(1)}, f32[256,256]{1,0:T(8,128)}, u32[]{:S(2)}) copy-start(f32[256,256]{1,0:T(8,128)} %param.11) | copy-start | bytes 786436
  2.3 16.9 %collective-permute-start.7 = (f32[192,128]{1,0:T(8,128)}, f32[192,128]{1,0:T(8,128)}, u32[]{:S(2)}, u32[]{:S(2)}) collective-permute-start(f32[192,128]{1,0:T(8,128)} %get-tuple-element.26), channel_id=1, source_target_pairs={{0,8},{1,9},{2,10},{3,11},{4,12},{5,13},{6,14},{7,15},{8,0},{9,1},... | collective-permute-start | bytes 294920 | tf_op jit(solution)/shard_map/ppermute | solution.py:177
  5.3 11.9 %collective-permute-start.8 = (f32[192,128]{1,0:T(8,128)}, f32[192,128]{1,0:T(8,128)S(1)}, u32[]{:S(2)}, u32[]{:S(2)}) collective-permute-start(f32[192,128]{1,0:T(8,128)} %get-tuple-element.26), channel_id=1, source_target_pairs={{0,24},{1,25},{2,26},{3,27},{4,28},{5,29},{6,30},{7,31},{8,16},{9,... | collective-permute-start | bytes 294920 | tf_op jit(solution)/shard_map/ppermute | solution.py:177
  7.8 13.0 %collective-permute-start = (f32[192,128]{1,0:T(8,128)}, f32[192,128]{1,0:T(8,128)}, u32[]{:S(2)}, u32[]{:S(2)}) collective-permute-start(f32[192,128]{1,0:T(8,128)} %get-tuple-element.27), channel_id=1, source_target_pairs={{0,8},{1,9},{2,10},{3,11},{4,12},{5,13},{6,14},{7,15},{8,0},{9,1},... | collective-permute-start | bytes 294920 | tf_op jit(solution)/shard_map/ppermute | solution.py:177
  8.5 9.6 %collective-permute-start.1 = (f32[192,128]{1,0:T(8,128)}, f32[192,128]{1,0:T(8,128)}, u32[]{:S(2)}, u32[]{:S(2)}) collective-permute-start(f32[192,128]{1,0:T(8,128)} %get-tuple-element.27), channel_id=1, source_target_pairs={{0,24},{1,25},{2,26},{3,27},{4,28},{5,29},{6,30},{7,31},{8,16},{9,... | collective-permute-start | bytes 294920 | tf_op jit(solution)/shard_map/ppermute | solution.py:177
  10.5 6.1 %copy-start.14 = (f32[192,256]{1,0:T(8,128)S(1)}, f32[192,256]{1,0:T(8,128)}, u32[]{:S(2)}) copy-start(f32[192,256]{1,0:T(8,128)} %param.7) | copy-start | bytes 589828
  10.5 24.1 %copy-start.4 = (f32[192,256]{1,0:T(8,128)S(1)}, f32[192,256]{1,0:T(8,128)}, u32[]{:S(2)}) copy-start(f32[192,256]{1,0:T(8,128)} %adjoint.1) | copy-start | bytes 589828
  10.5 27.6 %collective-permute-start.3 = (f32[1,192,256]{1,2,0:T(8,128)S(1)}, f32[1,192,256]{1,2,0:T(8,128)}, u32[]{:S(2)}, u32[]{:S(2)}) collective-permute-start(f32[1,192,256]{1,2,0:T(8,128)S(1)} %bitcast.55), channel_id=1, source_target_pairs={{0,2},{1,3},{2,0},{3,1},{4,6},{5,7},{6,4},{7,5},{8,10},{9,11},{10,... | collective-permute-start | bytes 589832 | tf_op jit(solution)/shard_map/ppermute | solution.py:180
  17.2 13.1 %copy-start.15 = (f32[192,128]{1,0:T(8,128)}, f32[192,128]{1,0:T(8,128)S(1)}, u32[]{:S(2)}) copy-start(f32[192,128]{1,0:T(8,128)S(1)} %collective-permute-done.8) | copy-start | bytes 294916
  17.2 5.1 %collective-permute-start.9 = (f32[192,128]{1,0:T(8,128)S(1)}, f32[192,128]{1,0:T(8,128)S(1)}, u32[]{:S(2)}, u32[]{:S(2)}) collective-permute-start(f32[192,128]{1,0:T(8,128)S(1)} %collective-permute-done.8), channel_id=1, source_target_pairs={{0,8},{1,9},{2,10},{3,11},{4,12},{5,13},{6,14},{7,15},{8,0},{9,1},... | collective-permute-start | bytes 294920 | tf_op jit(solution)/shard_map/ppermute | solution.py:177
  18.1 5.5 %collective-permute-start.2 = (f32[192,128]{1,0:T(8,128)}, f32[192,128]{1,0:T(8,128)S(1)}, u32[]{:S(2)}, u32[]{:S(2)}) collective-permute-start(f32[192,128]{1,0:T(8,128)} %collective-permute-done.1), channel_id=1, source_target_pairs={{0,8},{1,9},{2,10},{3,11},{4,12},{5,13},{6,14},{7,15},{8,0},{9,1},... | collective-permute-start | bytes 294920 | tf_op jit(solution)/shard_map/ppermute | solution.py:177
  22.3 8.0 %copy-start.16 = (f32[192,128]{1,0:T(8,128)}, f32[192,128]{1,0:T(8,128)S(1)}, u32[]{:S(2)}) copy-start(f32[192,128]{1,0:T(8,128)S(1)} %collective-permute-done.9) | copy-start | bytes 294916
  30.3 16.8 %all-to-all-start = ((f32[8,192,128]{2,1,0:T(8,128)}), f32[8,192,128]{2,1,0:T(8,128)}, u32[]{:S(2)}, u32[]{:S(2)}) async-start(f32[8,192,128]{2,1,0:T(8,128)} %bitcast_dynamic-update-slice_fusion.9), calls=%async_computation | async-start | bytes 1572864 | tf_op jit(solution)/shard_map/all_to_all | solution.py:217
  39.9 13.4 %collective-permute-start.4 = (f32[2,192,256]{1,2,0:T(8,128)}, f32[2,192,256]{1,2,0:T(8,128)}, u32[]{:S(2)}, u32[]{:S(2)}) collective-permute-start(f32[2,192,256]{1,2,0:T(8,128)} %pad_maximum_fusion), channel_id=1, source_target_pairs={{0,1},{1,0},{2,3},{3,2},{4,5},{5,4},{6,7},{7,6},{8,9},{9,8},{10,11... | collective-permute-start | bytes 1179656 | tf_op jit(solution)/shard_map/ppermute | solution.py:180
  47.1 19.8 %all-to-all-start.1 = ((f32[8,192,128]{2,1,0:T(8,128)}), f32[8,192,128]{2,1,0:T(8,128)}, u32[]{:S(2)}, u32[]{:S(2)}) async-start(f32[8,192,128]{2,1,0:T(8,128)} %bitcast_dynamic-update-slice_fusion.1), calls=%async_computation.1 | async-start | bytes 1572864 | tf_op jit(solution)/shard_map/all_to_all | solution.py:217
  59.6 30.1 %copy-start.3 = (f32[256,256]{1,0:T(8,128)S(1)}, f32[256,256]{1,0:T(8,128)}, u32[]{:S(2)}) copy-start(f32[256,256]{1,0:T(8,128)} %inverse.5) | copy-start | bytes 786436
  64.2 0.7 copy-start.1
  64.9 0.7 copy-start.9
  65.6 0.7 copy-start.10
  66.2 0.7 copy-start.13
  66.9 1.0 copy-start.2
  67.9 0.9 copy-start.11
  73.3 0.7 copy-start.6
  74.0 0.7 copy-start.8
  74.7 0.7 copy-start.12
  75.4 14.3 %all-to-all-start.2 = ((f32[32,8,256]{2,1,0:T(8,128)}), f32[32,8,256]{2,1,0:T(8,128)S(1)}, u32[]{:S(2)}, u32[]{:S(2)}) async-start(f32[32,8,256]{2,1,0:T(8,128)} %bitcast.51), calls=%async_computation.2 | async-start | bytes 524288 | tf_op jit(solution)/shard_map/all_to_all | solution.py:239
  79.1 16.2 %collective-permute-start.5 = (f32[2,192,128]{2,1,0:T(8,128)}, f32[2,192,128]{2,1,0:T(8,128)S(1)}, u32[]{:S(2)}, u32[]{:S(2)}) collective-permute-start(f32[2,192,128]{2,1,0:T(8,128)} %copy-done.13), channel_id=1, source_target_pairs={{0,2},{1,3},{2,0},{3,1},{4,6},{5,7},{6,4},{7,5},{8,10},{9,11},{10,... | collective-permute-start | bytes 589832 | tf_op jit(solution)/shard_map/ppermute | solution.py:180
  81.1 15.4 %collective-permute-start.10 = (f32[2,192,128]{2,1,0:T(8,128)}, f32[2,192,128]{2,1,0:T(8,128)S(1)}, u32[]{:S(2)}, u32[]{:S(2)}) collective-permute-start(f32[2,192,128]{2,1,0:T(8,128)} %copy-done.12), channel_id=1, source_target_pairs={{0,2},{1,3},{2,0},{3,1},{4,6},{5,7},{6,4},{7,5},{8,10},{9,11},{10,... | collective-permute-start | bytes 589832 | tf_op jit(solution)/shard_map/ppermute | solution.py:180
  89.7 1.0 copy-start.7
  92.8 13.2 %all-to-all-start.3 = ((f32[32,8,256]{2,1,0:T(8,128)}), f32[32,8,256]{2,1,0:T(8,128)S(1)}, u32[]{:S(2)}, u32[]{:S(2)}) async-start(f32[32,8,256]{2,1,0:T(8,128)} %bitcast.23), calls=%async_computation.3 | async-start | bytes 524288 | tf_op jit(solution)/shard_map/all_to_all | solution.py:253
  96.3 1.6 %collective-permute-start.6 = (f32[1,192,128]{2,1,0:T(8,128)S(1)}, f32[1,192,128]{2,1,0:T(8,128)S(1)}, u32[]{:S(2)}, u32[]{:S(2)}) collective-permute-start(f32[1,192,128]{2,1,0:T(8,128)S(1)} %get-tuple-element.22), channel_id=1, source_target_pairs={{0,1},{1,0},{2,3},{3,2},{4,5},{5,4},{6,7},{7,6},{8,9},{9,8},{10,11... | collective-permute-start | bytes 294920 | tf_op jit(solution)/shard_map/ppermute | solution.py:180
  97.5 1.4 %collective-permute-start.11 = (f32[1,192,128]{2,1,0:T(8,128)S(1)}, f32[1,192,128]{2,1,0:T(8,128)S(1)}, u32[]{:S(2)}, u32[]{:S(2)}) collective-permute-start(f32[1,192,128]{2,1,0:T(8,128)S(1)} %get-tuple-element.20), channel_id=1, source_target_pairs={{0,1},{1,0},{2,3},{3,2},{4,5},{5,4},{6,7},{7,6},{8,9},{9,8},{10,11... | collective-permute-start | bytes 294920 | tf_op jit(solution)/shard_map/ppermute | solution.py:180
  98.9 0.9 copy-start.5

commit v3 on v1

v3 whole, which is shorter than its diff:
```python
import functools

import jax
import jax.numpy as jnp
from jax import lax
from jax.experimental import pallas as pl
from jax.experimental.pallas import tpu as pltpu
from jax.sharding import PartitionSpec as P

HIGHEST = lax.Precision.HIGHEST
AXES = ("row", "col")
ANY = pl.BlockSpec(memory_space=pl.ANY)
VMEM = pl.BlockSpec(memory_space=pltpu.VMEM)
LIMIT = 16 * 1024 * 1024


def dot(a, b, precision=HIGHEST):
    return jnp.dot(a, b, precision=precision, preferred_element_type=jnp.float32)


def dot_t(a, b, precision=HIGHEST):
    return lax.dot_general(
        a, b, (((0,), (0,)), ((), ())), precision=precision, preferred_element_type=jnp.float32
    )


def parts(x):
    high = x.astype(jnp.bfloat16)
    return high, (x - high.astype(jnp.float32)).astype(jnp.bfloat16)


def dot_parts(x, high, low):
    rows = x.shape[0]
    x = jnp.concatenate(parts(x), axis=0)
    both = dot(x, high, None) + dot(x, low, None)
    return both[:rows] + both[rows:]


def halve_kernel(h, x, out):
    half = out.shape[1]
    out[...] = x[:, h * half : (h + 1) * half]


def prepare_kernel(cols, order, *refs):
    blocks, rest = refs[:cols], refs[cols:]
    adjoint, factor, inverse, corner, rowt_high, rowt_low, start, base, unit, inv = rest
    height = adjoint.shape[0]
    for d in range(cols):
        high, low = parts(blocks[order.index(d)][...].T)
        rowt_high[:, d * height : (d + 1) * height] = high
        rowt_low[:, d * height : (d + 1) * height] = low
    start[...] = dot_t(blocks[0][...], adjoint[...])
    base[...] = dot_t(corner[...], factor[...])
    high, low = parts(dot(inverse[...], factor[...]))
    unit[0], unit[1] = high, low
    high, low = parts(inverse[...])
    inv[0], inv[1] = high, low


def assemble_kernel(group, cols, *refs):
    pieces, out = refs[:-1], refs[-1]
    for y in range(group):
        for d in range(cols):
            out[y * cols + d] = pieces[d][...]


def trail_kernel(trail, out):
    out[0], out[1] = parts(trail[...])


def choose_kernel(zero, one, two, three, own, other):
    side = lax.axis_index("col") // 2
    mine = side == lax.axis_index("row") // 4
    for ref, take in ((own, mine), (other, jnp.logical_not(mine))):

        @pl.when(take)
        def _():
            ref[0] = zero[...]
            ref[1] = one[...]

        @pl.when(jnp.logical_not(take))
        def _():
            ref[0] = two[...]
            ref[1] = three[...]


def fill_pieces(group, cols, pieces, wide):
    height, half = pieces.shape[1], pieces.shape[2]
    plane = lax.axis_index("row") // group
    for y in range(group):
        for c in range(cols):
            high, low = parts(pieces[y * cols + (plane ^ c)])
            at = pl.ds((y * cols + c) * height, height)
            wide[at, :half] = high
            wide[at, half:] = low


def which_plane():
    return (lax.axis_index("row") // 2 + lax.axis_index("col")) % 2


def pick_kernel(*refs):
    pairs, out = refs[:-1], refs[-1]
    theirs = 1 - which_plane()
    for i, pair in enumerate(pairs):
        out[i] = pair[theirs]


def fill_pairs(pairs, came, wide):
    height, half = pairs[0].shape[1], pairs[0].shape[2]
    which = which_plane()
    place = lax.axis_index("row") % 2 * 4 + lax.axis_index("col")
    for i in range(2 * len(pairs)):
        k, y, x = i // 4, i // 2 % 2, i % 2
        source = place ^ (y * 4 + x * 2 + k)
        high, low = parts(came[i % 4] if k else pairs[i][which])
        at = pl.ds(pl.multiple_of(source * height, height), height)
        wide[at, :half] = high
        wide[at, half:] = low


def product_kernel(group, cols, count, last, *refs):
    pieces, refs = refs[:count], refs[count:]
    if last:
        rowt_high, rowt_low, start, before, trail, keep, send, gram_t, wide, split = refs
    else:
        rowt_high, rowt_low, start, trail, keep, send, gram_t, _, wide, split = refs
    height, half = pieces[0].shape[1], pieces[0].shape[2]
    col = lax.axis_index("col")
    if count == 1:
        fill_pieces(group, cols, pieces[0], wide)
    else:
        fill_pairs(pieces[:-1], pieces[-1], wide)
    for target in range(cols):
        at = pl.ds(target * height, height)
        both = dot(trail[0, at, :], wide[...], None) + dot(trail[1, at, :], wide[...], None)
        block = both[:, :half] + both[:, half:]
        d = target ^ col
        high, low = parts(block)
        at = pl.ds(pl.multiple_of(d * height, height), height)
        split[at, :half] = high
        split[at, half:] = low

        @pl.when(d % 2 == 0)
        def _():
            keep[d // 2] = block

        @pl.when(d % 2 == 1)
        def _():
            send[d // 2] = block

    total = dot(rowt_high[...], split[...], None) + dot(rowt_low[...], split[...], None)
    total = total[:, :half] + total[:, half:]
    if last:
        gram_t[:, :half] = before[...]
        gram_t[:, half:] = start[:, half:] - 2.0 * total
    else:
        gram_t[...] = start[:, :half] - 2.0 * total


def middle_kernel(devices, cols, share, shares, base, unit, inv, out):
    total = shares[pl.ds(0, share), :]
    for i in range(1, devices):
        total = total + shares[pl.ds(i * share, share), :]
    me = lax.axis_index("row") * cols + lax.axis_index("col")
    first = pl.multiple_of(me * share, share)
    inner_t = base[pl.ds(first, share), :] - dot_parts(total, unit[0], unit[1])
    at = lax.broadcasted_iota(jnp.int32, inner_t.shape, 0) + first
    across = lax.broadcasted_iota(jnp.int32, inner_t.shape, 1)
    inner_t = jnp.where(across > at, inner_t, jnp.where(across == at, 0.5 * inner_t, 0.0))
    left_t = dot_parts(inner_t, inv[0], inv[1])
    for i in range(devices):
        out[pl.ds(i * share, share), :] = left_t


def last_kernel(left_t, inv, out):
    full = dot_parts(left_t[...].T, inv[0], inv[1])
    at = lax.broadcasted_iota(jnp.int32, full.shape, 0)
    across = lax.broadcasted_iota(jnp.int32, full.shape, 1)
    out[...] = jnp.where(across < at, full, jnp.where(across == at, 0.5 * full, 0.0))


def add_kernel(count, *refs):
    half, blocks = refs[0].shape[2], refs[0].shape[0]
    mine, theirs = refs[-2:]
    for h in range(count):
        keep, came = refs[2 * h], refs[2 * h + 1]
        at = slice(h * half, (h + 1) * half)
        for i in range(blocks // 2):
            mine[i, :, at] = keep[2 * i] + came[2 * i]
            theirs[i, :, at] = keep[2 * i + 1] + came[2 * i + 1]


def panel_kernel(adjoint, inv, mine, came, out, inv_on):
    inv_on[...] = inv[...]
    out[...] = dot_parts(adjoint[...] - 2.0 * (mine[0] + came[0]), inv[0], inv[1])


def whole(shape):
    return pl.BlockSpec(shape, lambda i: (0,) * len(shape))


def call(kernel, shapes, *args, name, after=(), cost=1000):
    out = [
        s if isinstance(s, jax.ShapeDtypeStruct) else jax.ShapeDtypeStruct(s, jnp.float32)
        for s in shapes
    ]

    def body(*refs):
        kernel(*refs[: len(args)], *refs[len(args) + len(after) :])

    return pl.pallas_call(
        body,
        grid=(1,),
        out_shape=out,
        in_specs=[whole(x.shape) for x in args] + [ANY] * len(after),
        out_specs=[whole(x.shape) for x in out],
        compiler_params=pltpu.CompilerParams(vmem_limit_bytes=LIMIT),
        cost_estimate=pl.CostEstimate(flops=1000, bytes_accessed=cost, transcendentals=0),
        name=name,
    )(*args, *after)


def split_trail(trail):
    rows, width = trail.shape
    blocks = 4
    return pl.pallas_call(
        trail_kernel,
        grid=(blocks,),
        in_specs=[pl.BlockSpec((rows // blocks, width), lambda i: (i, 0))],
        out_specs=pl.BlockSpec((2, rows // blocks, width), lambda i: (0, i, 0)),
        out_shape=jax.ShapeDtypeStruct((2, rows, width), jnp.bfloat16),
        compiler_params=pltpu.CompilerParams(vmem_limit_bytes=2 * LIMIT),
        cost_estimate=pl.CostEstimate(flops=1000, bytes_accessed=8 * rows * width, transcendentals=0),
        name="split_trail",
    )(trail)


def half_product(trail, pieces, rowt, start, before, group, cols, after=()):
    _, rows, width = trail.shape
    height, half = pieces[0].shape[1], pieces[0].shape[2]
    size = rowt[0].shape[0]
    near = cols // 2
    last = before is not None
    out = [
        jax.ShapeDtypeStruct((near, height, half), jnp.float32),
        jax.ShapeDtypeStruct((cols - near, height, half), jnp.float32),
        jax.ShapeDtypeStruct((size, size if last else half), jnp.float32),
    ]
    args = list(pieces) + list(rowt) + [start] + ([before] if last else [])
    count = len(args) + 1
    kernel = functools.partial(product_kernel, group, cols, len(pieces), last)

    def body(*refs):
        kernel(*refs[:count], *refs[count + len(after) :])

    return pl.pallas_call(
        body,
        grid=(1,),
        in_specs=[VMEM] * (len(args) + 1) + [ANY] * len(after),
        out_specs=[whole(x.shape) for x in out] + ([] if last else [VMEM]),
        out_shape=out + ([] if last else [jax.ShapeDtypeStruct(trail.shape, trail.dtype)]),
        scratch_shapes=[
            pltpu.VMEM((width, 2 * half), jnp.bfloat16),
            pltpu.VMEM((rows, 2 * half), jnp.bfloat16),
        ],
        input_output_aliases={} if last else {count - 1: 3},
        compiler_params=pltpu.CompilerParams(vmem_limit_bytes=LIMIT),
        cost_estimate=pl.CostEstimate(flops=1000, bytes_accessed=8 * rows * width, transcendentals=0),
        name="half_product",
    )(*args, trail, *after)


def make_on_device(rows, cols):
    group = rows // cols
    devices = rows * cols

    def index(plane, y, c):
        return (plane * group + y) * cols + c

    def plane_flip(mask):
        return [
            (index(p, y, c), index(p ^ mask, y, c))
            for p in range(cols) for y in range(group) for c in range(cols)
        ]

    def col_flip(mask):
        return [(r * cols + c, r * cols + (c ^ mask)) for r in range(rows) for c in range(cols)]

    planes = [[index(p, y, p ^ d) for y in range(group) for d in range(cols)] for p in range(cols)]

    def flip_plane(x, mask):
        return lax.ppermute(x, AXES, plane_flip(mask))

    def flip_col(x, mask):
        return lax.ppermute(x, AXES, col_flip(mask))

    def flip_y(x, mask):
        pairs = [
            (r * cols + c, (r ^ 1) * cols + (c ^ mask)) for r in range(rows) for c in range(cols)
        ]
        return lax.ppermute(x, AXES, pairs)

    def on_device(trail_adjoint, panel, panel_adjoint, diag_factor, diag_inverse, diag_adjoint):
        height, size = panel.shape
        half = size // 2
        row_place = lax.axis_index("row")
        col_place = lax.axis_index("col")
        me = row_place * cols + col_place

        far = []
        for h in range(2):
            (mine,) = call(
                functools.partial(halve_kernel, h), [(height, half)], panel,
                name="halve", after=(far[0][1],) if h else (),
            )
            pieces = {0: mine}
            for d in range(3, cols, 2):
                pieces[d] = flip_plane(mine, d)
            pieces[1] = flip_plane(mine, 1)
            for d in range(2, cols, 2):
                pieces[d] = flip_plane(pieces[d + 1], 1)
            far.append([pieces[d] for d in range(cols)])

        blocks, order, mask = [panel], [0], cols // 2
        while mask:
            blocks = blocks + [flip_col(x, mask) for x in blocks]
            order = order + [o ^ mask for o in order]
            mask //= 2
        trail = split_trail(trail_adjoint)
        halves = []
        for h in range(2):
            after = () if h else (blocks[1],)
            if cols == 4 and group == 2:
                own, other = call(
                    choose_kernel, [(2, height, half)] * 2, *far[h], name="choose", after=after
                )
                chosen = own
                halves.append([own, flip_col(other, 2), flip_y(own, 0), flip_y(other, 2)])
            else:
                (chosen,) = call(
                    functools.partial(assemble_kernel, group, cols),
                    [(group * cols, height, half)], *far[h], name="assemble", after=after,
                )
                halves.append([
                    lax.all_to_all(chosen, AXES, 0, 0, axis_index_groups=planes, tiled=True)
                ])

        bf16 = lambda *shape: jax.ShapeDtypeStruct(shape, jnp.bfloat16)
        rowt_high, rowt_low, start, base, unit, inv = call(
            functools.partial(prepare_kernel, cols, order),
            [bf16(size, cols * height)] * 2 + [(size, size)] * 2 + [bf16(2, size, size)] * 2,
            *blocks, panel_adjoint, diag_factor, diag_inverse, diag_adjoint,
            name="prepare", after=(chosen,), cost=1 << 22,
        )

        if len(halves[0]) > 1:
            (theirs,) = call(
                pick_kernel, [(4, height, half)], *halves[0], name="pick", after=(trail, start)
            )
            halves[0].append(flip_col(theirs, 1))
        keep, send, gram_t, trail = half_product(
            trail, halves[0], (rowt_high, rowt_low), start, None, group, cols
        )
        sums = [keep, flip_col(send, 1)]
        if len(halves[1]) > 1:
            (theirs,) = call(
                pick_kernel, [(4, height, half)], *halves[1], name="pick", after=(gram_t,)
            )
            halves[1].append(flip_col(theirs, 1))
        keep, send, gram_t = half_product(
            trail, halves[1], (rowt_high, rowt_low), start, gram_t, group, cols
        )
        sums += [keep, flip_col(send, 1)]

        mine, theirs = call(
            functools.partial(add_kernel, 2), [(cols // 4, height, size)] * 2, *sums, name="add"
        )
        mask = 2
        while True:
            came = flip_col(theirs, mask)
            mask *= 2
            if mask >= cols:
                break
            mine, theirs = mine[::2] + came[::2], mine[1::2] + came[1::2]
        share = size // devices
        shares = lax.all_to_all(gram_t, AXES, 0, 0, tiled=True)
        if share % 8 == 0:
            (left_t,) = call(
                functools.partial(middle_kernel, devices, cols, share), [(size, size)],
                shares, base, unit, inv, name="middle", after=(came,),
            )
        else:
            total = jnp.sum(shares.reshape(devices, share, size), axis=0)
            inner_t = dot(
                lax.dynamic_slice_in_dim(diag_adjoint.T, me * share, share, 0)
                - dot(total, diag_inverse),
                diag_factor,
            )
            at = lax.broadcasted_iota(jnp.int32, inner_t.shape, 0) + me * share
            across = lax.broadcasted_iota(jnp.int32, inner_t.shape, 1)
            inner_t = jnp.where(across > at, inner_t, jnp.where(across == at, 0.5 * inner_t, 0.0))
            left_t = jnp.tile(dot(inner_t, diag_inverse), (devices, 1))
        gathered = lax.all_to_all(left_t, AXES, 0, 0, tiled=True)

        panel_grad, inv = call(
            panel_kernel, [panel.shape, bf16(*inv.shape)], panel_adjoint, inv, mine, came,
            name="panel_grad",
        )
        (diag_grad,) = call(last_kernel, [(size, size)], gathered, inv, name="diag_grad")
        return panel_grad, diag_grad

    return on_device


def solution(mesh):
    in_specs = (P("row", "col"), P(("row", "col"), None), P(("row", "col"), None), P(), P(), P())
    out_specs = (P(("row", "col"), None), P())
    return jax.shard_map(
        make_on_device(mesh.shape["row"], mesh.shape["col"]),
        mesh=mesh, in_specs=in_specs, out_specs=out_specs, check_vma=False,
    )
```

time: 90 us -> 82.8 us (0.920)
  Pallas kernels: 0 us -> 15.9 us
  waiting for transfers between devices: 43.2 us -> 29.6 us
  matrix products: 13.4 us -> 0 us
  starting transfers between devices: 20.8 us -> 33.7 us
  local copies, waits for them, and re-layouts: 7.25 us -> 2.41 us
  other arithmetic: 3.98 us -> 0 us
    all_to_all x3 -> x2, waiting for transfers between devices: 28.7 us -> 9.65 us  [the longest x1 9.64 us: on_device(): gathered = lax.all_to_all(left_t, AXES, 0, 0, tiled=True)]
    pallas_call x0 -> x14, Pallas kernels: none -> 15.9 us  [the longest x2 7.9 us: half_product(): pl.pallas_call(body, grid=(1,), in_specs=[VMEM] * (len(args) + 1) + [ANY]...]
    dot_general x8 -> x0, matrix products: 13.4 us -> none  [the longest x5 9.32 us: dot(): jnp.dot(a, b, precision=precision, preferred_element_type=jnp.float32)]
    ppermute x4 -> x10, waiting for transfers between devices: 6.52 us -> 13.1 us  [flip_col(): return lax.ppermute(x, AXES, col_flip(mask))]
    ppermute x0 -> x4, starting transfers between devices: none -> 6.29 us  [flip_y(): return lax.ppermute(x, AXES, pairs)]
    ppermute x3 -> x6, waiting for transfers between devices: 8.06 us -> 2.58 us  [flip_plane(): return lax.ppermute(x, AXES, plane_flip(mask))]
    ppermute x0 -> x4, waiting for transfers between devices: none -> 4.29 us  [flip_y(): return lax.ppermute(x, AXES, pairs)]
    ppermute x3 -> x6, starting transfers between devices: 8.17 us -> 11.8 us  [flip_plane(): return lax.ppermute(x, AXES, plane_flip(mask))]
  transfers between devices with their start and end apart: 10 -> 22, of which waited for: 8 -> 13; matrix products, arithmetic and copies ran while one was open for 12% -> 0% of each run, Pallas kernels for 0% -> 10%
where the time goes in v3:
time: 82.8 us; the launch traced here: 82.4 us
  starting transfers between devices  33.7 us (41%)
  waiting for transfers between devices  29.6 us (36%)
  Pallas kernels  15.9 us (19%)
  local copies, waits for them, and re-layouts  2.41 us (3%)
    ppermute x10, waiting for transfers between devices, flip_col(): return lax.ppermute(x, AXES, col_flip(mask))  13.1 us
    ppermute x6, starting transfers between devices, flip_plane(): return lax.ppermute(x, AXES, plane_flip(mask))  11.8 us
    all_to_all x1, waiting for transfers between devices, on_device(): gathered = lax.all_to_all(left_t, AXES, 0, 0, tiled=True)  9.64 us
    pallas_call x2, Pallas kernels, half_product(): pl.pallas_call(body, grid=(1,), in_specs=[VMEM] * (len(args) + 1) + [ANY]...  7.9 us
    pallas_call x11, Pallas kernels, call(): pl.pallas_call(body, grid=(1,), out_shape=out, in_specs=[whole(x.shape) f...  6.99 us
    ppermute x4, starting transfers between devices, flip_y(): return lax.ppermute(x, AXES, pairs)  6.29 us
    ppermute x10, starting transfers between devices, flip_col(): return lax.ppermute(x, AXES, col_flip(mask))  6.13 us
    all_to_all x1, starting transfers between devices, on_device(): gathered = lax.all_to_all(left_t, AXES, 0, 0, tiled=True)  4.77 us
  transfers between devices with their start and end apart: 22, of which 13 were waited for; matrix products, arithmetic and copies ran while one was open for 0% of the time, Pallas kernels for 10%

profile of v3, /device:TPU:0, one launch (start us, length us, event | category | flops | bytes accessed | tf_op | source)
XLA Modules:
  0.0 82.4 jit_solution(4365480347476173602)
XLA Ops:
  0.6 0.9 %halve.2.refs_0_ = f32[192,128]{1,0:T(8,128)S(1)} custom-call(f32[192,256]{1,0:T(8,128)} %refs_0_.6), custom_call_target="tpu_custom_call" | custom-call | flops 1000 | bytes 1000 | tf_op jit(solution)/shard_map/halve/pallas_call | solution.py:212
  1.6 3.0 %collective-permute-start.3 = (f32[192,128]{1,0:T(8,128)S(1)}, f32[192,128]{1,0:T(8,128)S(1)}, u32[]{:S(2)}, u32[]{:S(2)}) collective-permute-start(f32[192,128]{1,0:T(8,128)S(1)} %halve.2.refs_0_), channel_id=1, source_target_pairs={{0,8},{1,9},{2,10},{3,11},{4,12},{5,13},{6,14},{7,15},{8,0},{9,1},... | collective-permute-start | bytes 294920 | tf_op jit(solution)/shard_map/ppermute | solution.py:293
  4.6 1.5 %collective-permute-start = (f32[192,256]{1,0:T(8,128)}, f32[192,256]{1,0:T(8,128)S(1)}, u32[]{:S(2)}, u32[]{:S(2)}) collective-permute-start(f32[192,256]{1,0:T(8,128)} %refs_0_.6), channel_id=1, source_target_pairs={{0,2},{1,3},{2,0},{3,1},{4,6},{5,7},{6,4},{7,5},{8,10},{9,11},{10,... | collective-permute-start | bytes 589832 | tf_op jit(solution)/shard_map/ppermute | solution.py:296
  6.1 2.5 %collective-permute-start.7 = (f32[192,128]{1,0:T(8,128)S(1)}, f32[192,128]{1,0:T(8,128)S(1)}, u32[]{:S(2)}, u32[]{:S(2)}) collective-permute-start(f32[192,128]{1,0:T(8,128)S(1)} %halve.2.refs_0_), channel_id=1, source_target_pairs={{0,24},{1,25},{2,26},{3,27},{4,28},{5,29},{6,30},{7,31},{8,16},{9,... | collective-permute-start | bytes 294920 | tf_op jit(solution)/shard_map/ppermute | solution.py:293
  8.6 0.0 collective-permute-done.3.refs_1_
  8.6 0.9 %halve.3.refs_0_ = f32[192,128]{1,0:T(8,128)S(1)} custom-call(f32[192,256]{1,0:T(8,128)} %refs_0_.6, f32[192,128]{1,0:T(8,128)S(1)} %collective-permute-done.3.refs_1_), custom_call_target="tpu_custom_call" | custom-call | flops 1000 | bytes 1000 | tf_op jit(solution)/shard_map/halve/pallas_call | solution.py:212
  9.5 2.7 %collective-permute-start.5 = (f32[192,128]{1,0:T(8,128)S(1)}, f32[192,128]{1,0:T(8,128)S(1)}, u32[]{:S(2)}, u32[]{:S(2)}) collective-permute-start(f32[192,128]{1,0:T(8,128)S(1)} %halve.3.refs_0_), channel_id=1, source_target_pairs={{0,24},{1,25},{2,26},{3,27},{4,28},{5,29},{6,30},{7,31},{8,16},{9,... | collective-permute-start | bytes 294920 | tf_op jit(solution)/shard_map/ppermute | solution.py:293
  12.2 0.4 collective-permute-done.7.refs_3_
  12.6 2.8 %collective-permute-start.8 = (f32[192,128]{1,0:T(8,128)S(1)}, f32[192,128]{1,0:T(8,128)S(1)}, u32[]{:S(2)}, u32[]{:S(2)}) collective-permute-start(f32[192,128]{1,0:T(8,128)S(1)} %collective-permute-done.7.refs_3_), channel_id=1, source_target_pairs={{0,8},{1,9},{2,10},{3,11},{4,12},{5,13},{6,14},{7,15},{8,0},{9,1},... | collective-permute-start | bytes 294920 | tf_op jit(solution)/shard_map/ppermute | solution.py:293
  15.4 0.0 collective-permute-start.4
  15.4 1.5 %collective-permute-done.5.refs_3_ = f32[192,128]{1,0:T(8,128)S(1)} collective-permute-done((f32[192,128]{1,0:T(8,128)S(1)}, f32[192,128]{1,0:T(8,128)S(1)}, u32[]{:S(2)}, u32[]{:S(2)}) %collective-permute-start.5) | collective-permute-done | bytes 98336 | tf_op jit(solution)/shard_map/ppermute | solution.py:293
  16.9 0.9 %collective-permute-start.6 = (f32[192,128]{1,0:T(8,128)S(1)}, f32[192,128]{1,0:T(8,128)S(1)}, u32[]{:S(2)}, u32[]{:S(2)}) collective-permute-start(f32[192,128]{1,0:T(8,128)S(1)} %collective-permute-done.5.refs_3_), channel_id=1, source_target_pairs={{0,8},{1,9},{2,10},{3,11},{4,12},{5,13},{6,14},{7,15},{8,0},{9,1},... | collective-permute-start | bytes 294920 | tf_op jit(solution)/shard_map/ppermute | solution.py:293
  17.8 0.0 collective-permute-start.1
  17.8 0.0 collective-permute-done.refs_1_.refs_4_
  17.8 0.5 collective-permute-start.2
  18.3 0.6 collective-permute-done.8.refs_2_
  19.0 1.6 %collective-permute-start.10 = (f32[2,192,128]{2,1,0:T(8,128)S(1)}, f32[2,192,128]{2,1,0:T(8,128)S(1)}, u32[]{:S(2)}, u32[]{:S(2)}) collective-permute-start(f32[2,192,128]{2,1,0:T(8,128)S(1)} %get-tuple-element.25.refs_0_), channel_id=1, source_target_pairs={{0,4},{1,5},{2,6},{3,7},{4,0},{5,1},{6,2},{7,3},{8,12},{9,13},{10,... | collective-permute-start | bytes 589832 | tf_op jit(solution)/shard_map/ppermute | solution.py:302
  20.5 0.0 collective-permute-done.4.refs_1_
  20.6 1.8 %collective-permute-start.11 = (f32[2,192,128]{2,1,0:T(8,128)S(1)}, f32[2,192,128]{2,1,0:T(8,128)S(1)}, u32[]{:S(2)}, u32[]{:S(2)}) collective-permute-start(f32[2,192,128]{2,1,0:T(8,128)S(1)} %get-tuple-element.26), channel_id=1, source_target_pairs={{0,6},{1,7},{2,4},{3,5},{4,2},{5,3},{6,0},{7,1},{8,14},{9,15},{10,... | collective-permute-start | bytes 589832 | tf_op jit(solution)/shard_map/ppermute | solution.py:302
  22.4 0.0 collective-permute-done.6.refs_2_
  22.4 0.9 %collective-permute-start.9 = (f32[2,192,128]{2,1,0:T(8,128)S(1)}, f32[2,192,128]{2,1,0:T(8,128)S(1)}, u32[]{:S(2)}, u32[]{:S(2)}) collective-permute-start(f32[2,192,128]{2,1,0:T(8,128)S(1)} %get-tuple-element.26), channel_id=1, source_target_pairs={{0,2},{1,3},{2,0},{3,1},{4,6},{5,7},{6,4},{7,5},{8,10},{9,11},{10,... | collective-permute-start | bytes 589832 | tf_op jit(solution)/shard_map/ppermute | solution.py:296
  23.3 0.0 copy-start
  23.3 2.3 %copy-done = f32[768,1536]{1,0:T(8,128)S(1)} copy-done((f32[768,1536]{1,0:T(8,128)S(1)}, f32[768,1536]{1,0:T(8,128)}, u32[]{:S(2)}) %copy-start) | copy-done | bytes 4718616
  25.6 0.0 copy-start.1
  25.6 0.0 copy-start.2
  25.6 0.0 copy-start.3
  25.6 0.0 copy-start.4
  25.6 1.0 %split_trail.1.refs_4_.refs_8_ = bf16[2,768,1536]{2,1,0:T(8,128)(2,1)S(1)} custom-call(f32[768,1536]{1,0:T(8,128)S(1)} %copy-done), custom_call_target="tpu_custom_call" | custom-call | flops 1000 | bytes 9437184 | tf_op jit(solution)/shard_map/split_trail/pallas_call | solution.py:227
  26.7 0.1 choose.2
  26.7 0.0 collective-permute-done.1.refs_2_
  26.7 0.0 collective-permute-done.2.refs_3_
  26.7 0.0 copy-done.1
  26.8 0.0 copy-done.2
  26.8 0.0 copy-done.3
  26.8 0.1 copy-done.4
  26.8 1.9 %prepare.1 = (bf16[256,768]{1,0:T(8,128)(2,1)S(1)}, bf16[256,768]{1,0:T(8,128)(2,1)S(1)}, f32[256,256]{1,0:T(8,128)S(1)}, f32[256,256]{1,0:T(8,128)S(1)}, bf16[2...) custom-call(f32[192,256]{1,0:T(8,128)} %refs_0_.6, f32[192,256]{1,0:T(8,128)S(1)} %collective-permute-done.refs_1_.refs_4_, ...), custom_call_target="tpu_custom_call" | custom-call | flops 1000 | bytes 4194304 | tf_op jit(solution)/shard_map/prepare/pallas_call | solution.py:212
  28.7 0.8 collective-permute-done.10.refs_2_
  29.5 0.0 collective-permute-done.11.refs_3_
  29.5 1.2 %collective-permute-done.9.refs_1_ = f32[2,192,128]{2,1,0:T(8,128)S(1)} collective-permute-done((f32[2,192,128]{2,1,0:T(8,128)S(1)}, f32[2,192,128]{2,1,0:T(8,128)S(1)}, u32[]{:S(2)}, u32[]{:S(2)}) %collective-permute-start.9) | collective-permute-done | bytes 196640 | tf_op jit(solution)/shard_map/ppermute | solution.py:296
  30.7 0.1 collective-permute-start.12
  30.8 1.6 %collective-permute-start.15 = (f32[2,192,128]{2,1,0:T(8,128)S(1)}, f32[2,192,128]{2,1,0:T(8,128)S(1)}, u32[]{:S(2)}, u32[]{:S(2)}) collective-permute-start(f32[2,192,128]{2,1,0:T(8,128)S(1)} %get-tuple-element.23.refs_8_.refs_0_), channel_id=1, source_target_pairs={{0,4},{1,5},{2,6},{3,7},{4,0},{5,1},{6,2},{7,3},{8,12},{9,13},{10,... | collective-permute-start | bytes 589832 | tf_op jit(solution)/shard_map/ppermute | solution.py:302
  32.4 0.7 collective-permute-start.14
  33.1 1.3 %collective-permute-start.16 = (f32[2,192,128]{2,1,0:T(8,128)S(1)}, f32[2,192,128]{2,1,0:T(8,128)S(1)}, u32[]{:S(2)}, u32[]{:S(2)}) collective-permute-start(f32[2,192,128]{2,1,0:T(8,128)S(1)} %get-tuple-element.32), channel_id=1, source_target_pairs={{0,6},{1,7},{2,4},{3,5},{4,2},{5,3},{6,0},{7,1},{8,14},{9,15},{10,... | collective-permute-start | bytes 589832 | tf_op jit(solution)/shard_map/ppermute | solution.py:302
  34.4 0.0 collective-permute-done.12.refs_4_
  34.4 3.6 %half_product.2 = (f32[2,192,128]{2,1,0:T(8,128)S(1)}, f32[2,192,128]{2,1,0:T(8,128)S(1)}, f32[256,128]{1,0:T(8,128)S(1)}, bf16[2,768,1536]{2,1,0:T(8,128)(2,1)S(1)}) custom-call(f32[2,192,128]{2,1,0:T(8,128)S(1)} %get-tuple-element.25.refs_0_, f32[2,192,128]{2,1,0:T(8,128)S(1)} %collective-permute-done.9.refs_1_, ...), custom_call_target="tpu_custom_call", output_to_operand_aliasing={{3}: (8, {})} | custom-call | flops 1000 | bytes 9437184 | tf_op jit(solution)/shard_map/half_product/pallas_call | solution.py:257
  38.0 0.2 collective-permute-done.15.refs_2_
  38.1 2.0 %collective-permute-done.14.refs_1_ = f32[2,192,128]{2,1,0:T(8,128)S(1)} collective-permute-done((f32[2,192,128]{2,1,0:T(8,128)S(1)}, f32[2,192,128]{2,1,0:T(8,128)S(1)}, u32[]{:S(2)}, u32[]{:S(2)}) %collective-permute-start.14) | collective-permute-done | bytes 196640 | tf_op jit(solution)/shard_map/ppermute | solution.py:296
  40.1 3.4 %collective-permute-done.16.refs_3_ = f32[2,192,128]{2,1,0:T(8,128)S(1)} collective-permute-done((f32[2,192,128]{2,1,0:T(8,128)S(1)}, f32[2,192,128]{2,1,0:T(8,128)S(1)}, u32[]{:S(2)}, u32[]{:S(2)}) %collective-permute-start.16) | collective-permute-done | bytes 196640 | tf_op jit(solution)/shard_map/ppermute | solution.py:302
  43.5 0.1 collective-permute-start.17
  43.6 1.7 %collective-permute-done.17.refs_4_ = f32[4,192,128]{2,1,0:T(8,128)S(1)} collective-permute-done((f32[4,192,128]{2,1,0:T(8,128)S(1)}, f32[4,192,128]{2,1,0:T(8,128)S(1)}, u32[]{:S(2)}, u32[]{:S(2)}) %collective-permute-start.17) | collective-permute-done | bytes 393248 | tf_op jit(solution)/shard_map/ppermute | solution.py:296
  45.3 4.3 %half_product.3 = (f32[2,192,128]{2,1,0:T(8,128)S(1)}, f32[2,192,128]{2,1,0:T(8,128)S(1)}, f32[256,256]{1,0:T(8,128)}) custom-call(f32[2,192,128]{2,1,0:T(8,128)S(1)} %get-tuple-element.23.refs_8_.refs_0_, f32[2,192,128]{2,1,0:T(8,128)S(1)} %collective-permute-done.14.refs_1_, f32[2,192,128]{2,1,0:T(8,128)S(1)} %collective-permute-done.15.refs_2_, ...), custom_call_target="tpu_custom_call" | custom-call | flops 1000 | bytes 9437184 | tf_op jit(solution)/shard_map/half_product/pallas_call | solution.py:257
  49.6 4.6 %all-to-all-start = ((f32[32,8,256]{2,1,0:T(8,128)}), f32[32,8,256]{2,1,0:T(8,128)S(1)}, u32[]{:S(2)}, u32[]{:S(2)}) async-start(f32[32,8,256]{2,1,0:T(8,128)} %bitcast), calls=%async_computation | async-start | bytes 524288 | tf_op jit(solution)/shard_map/all_to_all | solution.py:387
  54.3 0.3 collective-permute-start.13
  54.6 0.3 collective-permute-start.18
  54.9 0.9 %collective-permute-done.13.refs_1_ = f32[2,192,128]{2,1,0:T(8,128)S(1)} collective-permute-done((f32[2,192,128]{2,1,0:T(8,128)S(1)}, f32[2,192,128]{2,1,0:T(8,128)S(1)}, u32[]{:S(2)}, u32[]{:S(2)}) %collective-permute-start.13) | collective-permute-done | bytes 196640 | tf_op jit(solution)/shard_map/ppermute | solution.py:296
  55.8 0.3 collective-permute-done.18.refs_3_
  56.1 1.8 %collective-permute-start.19 = (f32[1,192,256]{2,1,0:T(8,128)S(1)}, f32[1,192,256]{2,1,0:T(8,128)S(1)}, u32[]{:S(2)}, u32[]{:S(2)}) collective-permute-start(f32[1,192,256]{2,1,0:T(8,128)S(1)} %get-tuple-element.38), channel_id=1, source_target_pairs={{0,2},{1,3},{2,0},{3,1},{4,6},{5,7},{6,4},{7,5},{8,10},{9,11},{10,... | collective-permute-start | bytes 589832 | tf_op jit(solution)/shard_map/ppermute | solution.py:296
  57.9 6.9 %collective-permute-done.19.refs_3_.refs_4_ = f32[1,192,256]{2,1,0:T(8,128)S(1)} collective-permute-done((f32[1,192,256]{2,1,0:T(8,128)S(1)}, f32[1,192,256]{2,1,0:T(8,128)S(1)}, u32[]{:S(2)}, u32[]{:S(2)}) %collective-permute-start.19) | collective-permute-done | bytes 196640 | tf_op jit(solution)/shard_map/ppermute | solution.py:296
  64.9 0.0 all-to-all-done
  64.9 1.1 %middle.1 = f32[256,256]{1,0:T(8,128)} custom-call(f32[256,256]{1,0:T(8,128)S(1)} %bitcast.5, f32[256,256]{1,0:T(8,128)S(1)} %get-tuple-element.41.refs_1_, bf16[2,256,256]{2,1,0:T(8,128)(2,1)S(1)} %get-tuple-element.42.refs_2_, bf16[2,256,256]{2,1,0:T(8,128)(2,1)S(1)} %get-tuple-element.24.refs_1_.refs_3_, ...), custom_call_target="tpu_custom_call" | custom-call | flops 1000 | bytes 1000 | tf_op jit(solution)/shard_map/middle/pallas_call | solution.py:212
  66.0 4.8 %all-to-all-start.1 = ((f32[32,8,256]{2,1,0:T(8,128)}), f32[32,8,256]{2,1,0:T(8,128)S(1)}, u32[]{:S(2)}, u32[]{:S(2)}) async-start(f32[32,8,256]{2,1,0:T(8,128)} %bitcast.2), calls=%async_computation.1 | async-start | bytes 524288 | tf_op jit(solution)/shard_map/all_to_all | solution.py:404
  70.7 1.0 %panel_grad.1 = (f32[192,256]{1,0:T(8,128)}, bf16[2,256,256]{2,1,0:T(8,128)(2,1)S(1)}) custom-call(f32[192,256]{1,0:T(8,128)S(1)} %copy-done.1, bf16[2,256,256]{2,1,0:T(8,128)(2,1)S(1)} %get-tuple-element.24.refs_1_.refs_3_, f32[1,192,256]{2,1,0:T(8,128)S(1)} %get-tuple-element.37.refs_2_, f32[1,192,256]{2,1,0:T(8,128)S(1)} %collective-permute-done.19.refs_3_.refs_4_), custom_call_target="tpu_custom_call" | custom-call | flops 1000 | bytes 1000 | tf_op jit(solution)/shard_map/panel_grad/pallas_call | solution.py:212
  71.7 9.6 %all-to-all-done.1 = f32[32,8,256]{2,1,0:T(8,128)S(1)} async-done(((f32[32,8,256]{2,1,0:T(8,128)}), f32[32,8,256]{2,1,0:T(8,128)S(1)}, u32[]{:S(2)}, u32[]{:S(2)}) %all-to-all-start.1) | async-done | bytes 262176 | tf_op jit(solution)/shard_map/all_to_all | solution.py:404
  81.3 1.1 %diag_grad.1 = f32[256,256]{1,0:T(8,128)} custom-call(f32[256,256]{1,0:T(8,128)S(1)} %bitcast.4, bf16[2,256,256]{2,1,0:T(8,128)(2,1)S(1)} %get-tuple-element.43.refs_1_), custom_call_target="tpu_custom_call" | custom-call | flops 1000 | bytes 1000 | tf_op jit(solution)/shard_map/diag_grad/pallas_call | solution.py:212
  (4 shorter events, 0.1 us)
Async XLA Ops:
  1.6 7.0 %collective-permute-start.3 = (f32[192,128]{1,0:T(8,128)S(1)}, f32[192,128]{1,0:T(8,128)S(1)}, u32[]{:S(2)}, u32[]{:S(2)}) collective-permute-start(f32[192,128]{1,0:T(8,128)S(1)} %halve.2.refs_0_), channel_id=1, source_target_pairs={{0,8},{1,9},{2,10},{3,11},{4,12},{5,13},{6,14},{7,15},{8,0},{9,1},... | collective-permute-start | bytes 294920 | tf_op jit(solution)/shard_map/ppermute | solution.py:293
  4.6 13.2 %collective-permute-start = (f32[192,256]{1,0:T(8,128)}, f32[192,256]{1,0:T(8,128)S(1)}, u32[]{:S(2)}, u32[]{:S(2)}) collective-permute-start(f32[192,256]{1,0:T(8,128)} %refs_0_.6), channel_id=1, source_target_pairs={{0,2},{1,3},{2,0},{3,1},{4,6},{5,7},{6,4},{7,5},{8,10},{9,11},{10,... | collective-permute-start | bytes 589832 | tf_op jit(solution)/shard_map/ppermute | solution.py:296
  6.1 6.5 %collective-permute-start.7 = (f32[192,128]{1,0:T(8,128)S(1)}, f32[192,128]{1,0:T(8,128)S(1)}, u32[]{:S(2)}, u32[]{:S(2)}) collective-permute-start(f32[192,128]{1,0:T(8,128)S(1)} %halve.2.refs_0_), channel_id=1, source_target_pairs={{0,24},{1,25},{2,26},{3,27},{4,28},{5,29},{6,30},{7,31},{8,16},{9,... | collective-permute-start | bytes 294920 | tf_op jit(solution)/shard_map/ppermute | solution.py:293
  9.5 7.4 %collective-permute-start.5 = (f32[192,128]{1,0:T(8,128)S(1)}, f32[192,128]{1,0:T(8,128)S(1)}, u32[]{:S(2)}, u32[]{:S(2)}) collective-permute-start(f32[192,128]{1,0:T(8,128)S(1)} %halve.3.refs_0_), channel_id=1, source_target_pairs={{0,24},{1,25},{2,26},{3,27},{4,28},{5,29},{6,30},{7,31},{8,16},{9,... | collective-permute-start | bytes 294920 | tf_op jit(solution)/shard_map/ppermute | solution.py:293
  12.6 6.3 %collective-permute-start.8 = (f32[192,128]{1,0:T(8,128)S(1)}, f32[192,128]{1,0:T(8,128)S(1)}, u32[]{:S(2)}, u32[]{:S(2)}) collective-permute-start(f32[192,128]{1,0:T(8,128)S(1)} %collective-permute-done.7.refs_3_), channel_id=1, source_target_pairs={{0,8},{1,9},{2,10},{3,11},{4,12},{5,13},{6,14},{7,15},{8,0},{9,1},... | collective-permute-start | bytes 294920 | tf_op jit(solution)/shard_map/ppermute | solution.py:293
  15.4 5.2 %collective-permute-start.4 = (f32[192,128]{1,0:T(8,128)S(1)}, f32[192,128]{1,0:T(8,128)S(1)}, u32[]{:S(2)}, u32[]{:S(2)}) collective-permute-start(f32[192,128]{1,0:T(8,128)S(1)} %halve.3.refs_0_), channel_id=1, source_target_pairs={{0,8},{1,9},{2,10},{3,11},{4,12},{5,13},{6,14},{7,15},{8,0},{9,1},... | collective-permute-start | bytes 294920 | tf_op jit(solution)/shard_map/ppermute | solution.py:293
  16.9 5.4 %collective-permute-start.6 = (f32[192,128]{1,0:T(8,128)S(1)}, f32[192,128]{1,0:T(8,128)S(1)}, u32[]{:S(2)}, u32[]{:S(2)}) collective-permute-start(f32[192,128]{1,0:T(8,128)S(1)} %collective-permute-done.5.refs_3_), channel_id=1, source_target_pairs={{0,8},{1,9},{2,10},{3,11},{4,12},{5,13},{6,14},{7,15},{8,0},{9,1},... | collective-permute-start | bytes 294920 | tf_op jit(solution)/shard_map/ppermute | solution.py:293
  17.8 8.9 %collective-permute-start.1 = (f32[192,256]{1,0:T(8,128)}, f32[192,256]{1,0:T(8,128)S(1)}, u32[]{:S(2)}, u32[]{:S(2)}) collective-permute-start(f32[192,256]{1,0:T(8,128)} %refs_0_.6), channel_id=1, source_target_pairs={{0,1},{1,0},{2,3},{3,2},{4,5},{5,4},{6,7},{7,6},{8,9},{9,8},{10,11... | collective-permute-start | bytes 589832 | tf_op jit(solution)/shard_map/ppermute | solution.py:296
  17.8 8.9 %collective-permute-start.2 = (f32[192,256]{1,0:T(8,128)S(1)}, f32[192,256]{1,0:T(8,128)S(1)}, u32[]{:S(2)}, u32[]{:S(2)}) collective-permute-start(f32[192,256]{1,0:T(8,128)S(1)} %collective-permute-done.refs_1_.refs_4_), channel_id=1, source_target_pairs={{0,1},{1,0},{2,3},{3,2},{4,5},{5,4},{6,7},{7,6},{8,9},{9,8},{10,11... | collective-permute-start | bytes 589832 | tf_op jit(solution)/shard_map/ppermute | solution.py:296
  19.0 10.5 %collective-permute-start.10 = (f32[2,192,128]{2,1,0:T(8,128)S(1)}, f32[2,192,128]{2,1,0:T(8,128)S(1)}, u32[]{:S(2)}, u32[]{:S(2)}) collective-permute-start(f32[2,192,128]{2,1,0:T(8,128)S(1)} %get-tuple-element.25.refs_0_), channel_id=1, source_target_pairs={{0,4},{1,5},{2,6},{3,7},{4,0},{5,1},{6,2},{7,3},{8,12},{9,13},{10,... | collective-permute-start | bytes 589832 | tf_op jit(solution)/shard_map/ppermute | solution.py:302
  20.6 8.9 %collective-permute-start.11 = (f32[2,192,128]{2,1,0:T(8,128)S(1)}, f32[2,192,128]{2,1,0:T(8,128)S(1)}, u32[]{:S(2)}, u32[]{:S(2)}) collective-permute-start(f32[2,192,128]{2,1,0:T(8,128)S(1)} %get-tuple-element.26), channel_id=1, source_target_pairs={{0,6},{1,7},{2,4},{3,5},{4,2},{5,3},{6,0},{7,1},{8,14},{9,15},{10,... | collective-permute-start | bytes 589832 | tf_op jit(solution)/shard_map/ppermute | solution.py:302
  22.4 8.3 %collective-permute-start.9 = (f32[2,192,128]{2,1,0:T(8,128)S(1)}, f32[2,192,128]{2,1,0:T(8,128)S(1)}, u32[]{:S(2)}, u32[]{:S(2)}) collective-permute-start(f32[2,192,128]{2,1,0:T(8,128)S(1)} %get-tuple-element.26), channel_id=1, source_target_pairs={{0,2},{1,3},{2,0},{3,1},{4,6},{5,7},{6,4},{7,5},{8,10},{9,11},{10,... | collective-permute-start | bytes 589832 | tf_op jit(solution)/shard_map/ppermute | solution.py:296
  23.3 2.3 %copy-start = (f32[768,1536]{1,0:T(8,128)S(1)}, f32[768,1536]{1,0:T(8,128)}, u32[]{:S(2)}) copy-start(f32[768,1536]{1,0:T(8,128)} %trail.1) | copy-start | bytes 14155780
  25.6 1.1 %copy-start.1 = (f32[192,256]{1,0:T(8,128)S(1)}, f32[192,256]{1,0:T(8,128)}, u32[]{:S(2)}) copy-start(f32[192,256]{1,0:T(8,128)} %refs_0_.7) | copy-start | bytes 589828
  25.6 1.1 %copy-start.2 = (f32[256,256]{1,0:T(8,128)S(1)}, f32[256,256]{1,0:T(8,128)}, u32[]{:S(2)}) copy-start(f32[256,256]{1,0:T(8,128)} %refs_5_.1) | copy-start | bytes 786436
  25.6 1.1 %copy-start.3 = (f32[256,256]{1,0:T(8,128)S(1)}, f32[256,256]{1,0:T(8,128)}, u32[]{:S(2)}) copy-start(f32[256,256]{1,0:T(8,128)} %refs_6_.1) | copy-start | bytes 786436
  25.6 1.2 %copy-start.4 = (f32[256,256]{1,0:T(8,128)S(1)}, f32[256,256]{1,0:T(8,128)}, u32[]{:S(2)}) copy-start(f32[256,256]{1,0:T(8,128)} %refs_7_.1) | copy-start | bytes 786436
  30.7 3.6 %collective-permute-start.12 = (f32[4,192,128]{2,1,0:T(8,128)S(1)}, f32[4,192,128]{2,1,0:T(8,128)S(1)}, u32[]{:S(2)}, u32[]{:S(2)}) collective-permute-start(f32[4,192,128]{2,1,0:T(8,128)S(1)} %pick.2), channel_id=1, source_target_pairs={{0,1},{1,0},{2,3},{3,2},{4,5},{5,4},{6,7},{7,6},{8,9},{9,8},{10,11... | collective-permute-start | bytes 1179656 | tf_op jit(solution)/shard_map/ppermute | solution.py:296
  30.8 7.3 %collective-permute-start.15 = (f32[2,192,128]{2,1,0:T(8,128)S(1)}, f32[2,192,128]{2,1,0:T(8,128)S(1)}, u32[]{:S(2)}, u32[]{:S(2)}) collective-permute-start(f32[2,192,128]{2,1,0:T(8,128)S(1)} %get-tuple-element.23.refs_8_.refs_0_), channel_id=1, source_target_pairs={{0,4},{1,5},{2,6},{3,7},{4,0},{5,1},{6,2},{7,3},{8,12},{9,13},{10,... | collective-permute-start | bytes 589832 | tf_op jit(solution)/shard_map/ppermute | solution.py:302
  32.4 7.7 %collective-permute-start.14 = (f32[2,192,128]{2,1,0:T(8,128)S(1)}, f32[2,192,128]{2,1,0:T(8,128)S(1)}, u32[]{:S(2)}, u32[]{:S(2)}) collective-permute-start(f32[2,192,128]{2,1,0:T(8,128)S(1)} %get-tuple-element.32), channel_id=1, source_target_pairs={{0,2},{1,3},{2,0},{3,1},{4,6},{5,7},{6,4},{7,5},{8,10},{9,11},{10,... | collective-permute-start | bytes 589832 | tf_op jit(solution)/shard_map/ppermute | solution.py:296
  33.1 10.5 %collective-permute-start.16 = (f32[2,192,128]{2,1,0:T(8,128)S(1)}, f32[2,192,128]{2,1,0:T(8,128)S(1)}, u32[]{:S(2)}, u32[]{:S(2)}) collective-permute-start(f32[2,192,128]{2,1,0:T(8,128)S(1)} %get-tuple-element.32), channel_id=1, source_target_pairs={{0,6},{1,7},{2,4},{3,5},{4,2},{5,3},{6,0},{7,1},{8,14},{9,15},{10,... | collective-permute-start | bytes 589832 | tf_op jit(solution)/shard_map/ppermute | solution.py:302
  43.5 1.8 %collective-permute-start.17 = (f32[4,192,128]{2,1,0:T(8,128)S(1)}, f32[4,192,128]{2,1,0:T(8,128)S(1)}, u32[]{:S(2)}, u32[]{:S(2)}) collective-permute-start(f32[4,192,128]{2,1,0:T(8,128)S(1)} %pick.3), channel_id=1, source_target_pairs={{0,1},{1,0},{2,3},{3,2},{4,5},{5,4},{6,7},{7,6},{8,9},{9,8},{10,11... | collective-permute-start | bytes 1179656 | tf_op jit(solution)/shard_map/ppermute | solution.py:296
  49.6 15.3 %all-to-all-start = ((f32[32,8,256]{2,1,0:T(8,128)}), f32[32,8,256]{2,1,0:T(8,128)S(1)}, u32[]{:S(2)}, u32[]{:S(2)}) async-start(f32[32,8,256]{2,1,0:T(8,128)} %bitcast), calls=%async_computation | async-start | bytes 524288 | tf_op jit(solution)/shard_map/all_to_all | solution.py:387
  54.3 1.5 %collective-permute-start.13 = (f32[2,192,128]{2,1,0:T(8,128)S(1)}, f32[2,192,128]{2,1,0:T(8,128)S(1)}, u32[]{:S(2)}, u32[]{:S(2)}) collective-permute-start(f32[2,192,128]{2,1,0:T(8,128)S(1)} %get-tuple-element.31), channel_id=1, source_target_pairs={{0,1},{1,0},{2,3},{3,2},{4,5},{5,4},{6,7},{7,6},{8,9},{9,8},{10,11... | collective-permute-start | bytes 589832 | tf_op jit(solution)/shard_map/ppermute | solution.py:296
  54.6 1.5 %collective-permute-start.18 = (f32[2,192,128]{2,1,0:T(8,128)S(1)}, f32[2,192,128]{2,1,0:T(8,128)S(1)}, u32[]{:S(2)}, u32[]{:S(2)}) collective-permute-start(f32[2,192,128]{2,1,0:T(8,128)S(1)} %get-tuple-element.36), channel_id=1, source_target_pairs={{0,1},{1,0},{2,3},{3,2},{4,5},{5,4},{6,7},{7,6},{8,9},{9,8},{10,11... | collective-permute-start | bytes 589832 | tf_op jit(solution)/shard_map/ppermute | solution.py:296
  56.1 8.8 %collective-permute-start.19 = (f32[1,192,256]{2,1,0:T(8,128)S(1)}, f32[1,192,256]{2,1,0:T(8,128)S(1)}, u32[]{:S(2)}, u32[]{:S(2)}) collective-permute-start(f32[1,192,256]{2,1,0:T(8,128)S(1)} %get-tuple-element.38), channel_id=1, source_target_pairs={{0,2},{1,3},{2,0},{3,1},{4,6},{5,7},{6,4},{7,5},{8,10},{9,11},{10,... | collective-permute-start | bytes 589832 | tf_op jit(solution)/shard_map/ppermute | solution.py:296
  66.0 15.4 %all-to-all-start.1 = ((f32[32,8,256]{2,1,0:T(8,128)}), f32[32,8,256]{2,1,0:T(8,128)S(1)}, u32[]{:S(2)}, u32[]{:S(2)}) async-start(f32[32,8,256]{2,1,0:T(8,128)} %bitcast.2), calls=%async_computation.1 | async-start | bytes 524288 | tf_op jit(solution)/shard_map/all_to_all | solution.py:404

commit v4 on v0

v4 whole, which is shorter than its diff:
```python
import functools

import jax
import jax.numpy as jnp
from jax import lax
from jax.experimental import pallas as pl
from jax.experimental.pallas import tpu as pltpu
from jax.sharding import PartitionSpec as P

HIGHEST = lax.Precision.HIGHEST
AXES = ("row", "col")
ANY = pl.BlockSpec(memory_space=pl.ANY)
VMEM = pl.BlockSpec(memory_space=pltpu.VMEM)
LIMIT = 16 * 1024 * 1024


def dot(a, b, precision=HIGHEST):
    return jnp.dot(a, b, precision=precision, preferred_element_type=jnp.float32)


def dot_t(a, b, precision=HIGHEST):
    return lax.dot_general(
        a, b, (((0,), (0,)), ((), ())), precision=precision, preferred_element_type=jnp.float32
    )


def parts(x):
    high = x.astype(jnp.bfloat16)
    return high, (x - high.astype(jnp.float32)).astype(jnp.bfloat16)


def dot_parts(x, high, low):
    rows = x.shape[0]
    x = jnp.concatenate(parts(x), axis=0)
    both = dot(x, high, None) + dot(x, low, None)
    return both[:rows] + both[rows:]


def dot_three(a_high, a_low, b_high, b_low):
    return dot(a_high, b_high, None) + dot(a_high, b_low, None) + dot(a_low, b_high, None)


def needs_first():
    return (lax.axis_index("row") // 2 + lax.axis_index("col")) % 2 == 1


def choose_kernel(near, far, own, other):
    mine = lax.axis_index("col") // 2 == lax.axis_index("row") // 4

    @pl.when(mine)
    def _():
        own[...] = near[...]
        other[...] = far[...]

    @pl.when(jnp.logical_not(mine))
    def _():
        own[...] = far[...]
        other[...] = near[...]


def pick_kernel(count, *refs):
    first, second, out = refs[:count], refs[count : 2 * count], refs[-1]

    @pl.when(needs_first())
    def _():
        for i, ref in enumerate(second):
            out[i] = ref[...]

    @pl.when(jnp.logical_not(needs_first()))
    def _():
        for i, ref in enumerate(first):
            out[i] = ref[...]


def prepare_kernel(
    cols, order, blocks, *refs,
):
    rows_of, rest = refs[:cols], refs[cols:]
    (
        adjoint, factor, inverse, corner, trail,
        rowt, start, base, unit, inv, trail_parts, landing, sems,
    ) = rest
    rows = trail.shape[0] // blocks
    copies = []
    for i in range(blocks):
        at = pl.ds(i * rows, rows)
        copies.append(pltpu.make_async_copy(trail.at[at], landing.at[at], sems.at[i]))
        copies[-1].start()
    height = adjoint.shape[0]
    for d in range(cols):
        high, low = parts(rows_of[order.index(d)][...].T)
        rowt[0, :, d * height : (d + 1) * height] = high
        rowt[1, :, d * height : (d + 1) * height] = low
    start[...] = dot_t(rows_of[0][...], adjoint[...])
    base[...] = dot_t(corner[...], factor[...])
    high, low = parts(dot(inverse[...], factor[...]))
    unit[0], unit[1] = high, low
    high, low = parts(inverse[...])
    inv[0], inv[1] = high, low
    for i in range(blocks):
        copies[i].wait()
        at = pl.ds(i * rows, rows)
        trail_parts[0, at, :], trail_parts[1, at, :] = parts(landing[at, :])


def fill_all(group, cols, pieces, wide):
    height = pieces.shape[1]
    plane = lax.axis_index("row") // group
    for y in range(group):
        for c in range(cols):
            at = pl.ds((y * cols + c) * height, height)
            wide[0, at, :], wide[1, at, :] = parts(pieces[y * cols + (plane ^ c)])


def fill_sets(first, second, came, wide):
    height = came.shape[1]
    place = lax.axis_index("row") % 2 * 4 + lax.axis_index("col")

    def put(source, value):
        at = pl.ds(pl.multiple_of(source * height, height), height)
        wide[0, at, :], wide[1, at, :] = parts(value)

    @pl.when(needs_first())
    def _():
        for i, ref in enumerate(first):
            put(place ^ (2 * i), ref[...])

    @pl.when(jnp.logical_not(needs_first()))
    def _():
        for i, ref in enumerate(second):
            put(place ^ (2 * i), ref[...])

    for i in range(came.shape[0]):
        put(place ^ (2 * i) ^ 1, came[i])


def product_kernel(group, cols, count, *refs):
    pieces, (rowt, start, trail, keep, send, gram_t, wide, split) = refs[:count], refs[count:]
    if count == 1:
        fill_all(group, cols, pieces[0], wide)
    else:
        fill_sets(pieces[0:4], pieces[4:8], pieces[8], wide)
    height = split.shape[1] // cols
    col = lax.axis_index("col")
    for target in range(cols):
        at = pl.ds(target * height, height)
        block = dot_three(trail[0, at, :], trail[1, at, :], wide[0], wide[1])
        d = target ^ col
        at = pl.ds(pl.multiple_of(d * height, height), height)
        split[0, at, :], split[1, at, :] = parts(block)

        @pl.when(d % 2 == 0)
        def _():
            keep[d // 2] = block

        @pl.when(d % 2 == 1)
        def _():
            send[d // 2] = block

    gram_t[...] = start[...] - 2.0 * dot_three(rowt[0], rowt[1], split[0], split[1])


def middle_kernel(devices, cols, share, shares, base, unit, inv, out):
    total = shares[pl.ds(0, share), :]
    for i in range(1, devices):
        total = total + shares[pl.ds(i * share, share), :]
    me = lax.axis_index("row") * cols + lax.axis_index("col")
    first = pl.multiple_of(me * share, share)
    inner_t = base[pl.ds(first, share), :] - dot_parts(total, unit[0], unit[1])
    at = lax.broadcasted_iota(jnp.int32, inner_t.shape, 0) + first
    across = lax.broadcasted_iota(jnp.int32, inner_t.shape, 1)
    inner_t = jnp.where(across > at, inner_t, jnp.where(across == at, 0.5 * inner_t, 0.0))
    left_t = dot_parts(inner_t, inv[0], inv[1])
    for i in range(devices):
        out[pl.ds(i * share, share), :] = left_t


def last_kernel(left_t, inv, out):
    full = dot_parts(left_t[...].T, inv[0], inv[1])
    at = lax.broadcasted_iota(jnp.int32, full.shape, 0)
    across = lax.broadcasted_iota(jnp.int32, full.shape, 1)
    out[...] = jnp.where(across < at, full, jnp.where(across == at, 0.5 * full, 0.0))


def add_kernel(keep, came, mine, theirs):
    for i in range(keep.shape[0] // 2):
        mine[i] = keep[2 * i] + came[2 * i]
        theirs[i] = keep[2 * i + 1] + came[2 * i + 1]


def panel_kernel(adjoint, inv, mine, came, out, inv_on):
    inv_on[...] = inv[...]
    out[...] = dot_parts(adjoint[...] - 2.0 * (mine[0] + came[0]), inv[0], inv[1])


def whole(shape):
    return pl.BlockSpec(shape, lambda i: (0,) * len(shape))


def f32(*shape):
    return jax.ShapeDtypeStruct(shape, jnp.float32)


def bf16(*shape):
    return jax.ShapeDtypeStruct(shape, jnp.bfloat16)


def call(
    kernel, out, *args, name, after=(), in_specs=None, out_specs=None, scratch=(), aliases=None
):
    def body(*refs):
        kernel(*refs[: len(args)], *refs[len(args) + len(after) :])

    return pl.pallas_call(
        body,
        grid=(1,),
        out_shape=out,
        in_specs=(in_specs or [whole(x.shape) for x in args]) + [ANY] * len(after),
        out_specs=out_specs or [whole(x.shape) for x in out],
        scratch_shapes=list(scratch),
        input_output_aliases=aliases or {},
        compiler_params=pltpu.CompilerParams(vmem_limit_bytes=LIMIT),
        cost_estimate=pl.CostEstimate(flops=1000, bytes_accessed=1000, transcendentals=0),
        name=name,
    )(*args, *after)


def make_on_device(rows, cols):
    group = rows // cols
    devices = rows * cols
    paired = cols == 4 and group == 2

    def index(plane, y, c):
        return (plane * group + y) * cols + c

    planes = [[index(p, y, p ^ d) for y in range(group) for d in range(cols)] for p in range(cols)]

    def flip(x, plane=0, y=0, col=0):
        pairs = [
            (index(p, v, c), index(p ^ plane, v ^ y, c ^ col))
            for p in range(cols) for v in range(group) for c in range(cols)
        ]
        return lax.ppermute(x, AXES, pairs)

    def on_device(trail_adjoint, panel, panel_adjoint, diag_factor, diag_inverse, diag_adjoint):
        height, size = panel.shape
        width = trail_adjoint.shape[1]
        me = lax.axis_index("row") * cols + lax.axis_index("col")

        pieces = {0: panel}
        for d in range(3, cols, 2):
            pieces[d] = flip(panel, plane=d)
        pieces[1] = flip(panel, plane=1)
        for d in range(2, cols, 2):
            pieces[d] = flip(pieces[d + 1], plane=1)

        row_blocks, order, mask = [panel], [0], cols // 2
        while mask:
            row_blocks = row_blocks + [flip(x, col=mask) for x in row_blocks]
            order = order + [o ^ mask for o in order]
            mask //= 2

        if paired:
            sets = []
            for near, far in ((1, 3), (0, 2)):
                own, other = call(
                    choose_kernel, [f32(height, size)] * 2, pieces[near], pieces[far],
                    name="choose", after=(row_blocks[1],) if near else (),
                )
                sets.append([own, flip(other, col=2), flip(own, y=1), flip(other, y=1, col=2)])
            chosen = own
        else:
            chosen = jnp.stack([pieces[d] for d in range(cols)] * group)

        blocks = 4
        rowt, start, base, unit, inv, trail = call(
            functools.partial(prepare_kernel, cols, order, blocks),
            [bf16(2, size, cols * height), f32(size, size), f32(size, size)]
            + [bf16(2, size, size)] * 2 + [bf16(2, *trail_adjoint.shape)],
            *row_blocks, panel_adjoint, diag_factor, diag_inverse, diag_adjoint, trail_adjoint,
            name="prepare", after=(chosen,),
            in_specs=[whole(panel.shape)] * (cols + 1) + [whole((size, size))] * 3 + [ANY],
            out_specs=[VMEM] * 6,
            scratch=[
                pltpu.VMEM(trail_adjoint.shape, jnp.float32), pltpu.SemaphoreType.DMA((blocks,)),
            ],
        )

        if paired:
            args = sets[0] + sets[1]
            theirs = call(
                functools.partial(pick_kernel, 4), [f32(4, height, size)], *args,
                name="pick", after=(trail,),
            )[0]
            args = args + [flip(theirs, col=1)]
        else:
            args = [lax.all_to_all(chosen, AXES, 0, 0, axis_index_groups=planes, tiled=True)]
        keep, send, gram_t = call(
            functools.partial(product_kernel, group, cols, len(args)),
            [f32(cols // 2, height, size)] * 2 + [f32(size, size)],
            *args, rowt, start, trail, name="product", in_specs=[VMEM] * (len(args) + 3),
            scratch=[
                pltpu.VMEM((2, width, size), jnp.bfloat16),
                pltpu.VMEM((2, cols * height, size), jnp.bfloat16),
            ],
        )

        mine, theirs = call(
            add_kernel, [f32(cols // 4, height, size)] * 2, keep, flip(send, col=1), name="add"
        )
        mask = 2
        while True:
            came = flip(theirs, col=mask)
            mask *= 2
            if mask >= cols:
                break
            mine, theirs = mine[::2] + came[::2], mine[1::2] + came[1::2]

        share = size // devices
        shares = lax.all_to_all(gram_t, AXES, 0, 0, tiled=True)
        if share % 8 == 0:
            (left_t,) = call(
                functools.partial(middle_kernel, devices, cols, share), [f32(size, size)],
                shares, base, unit, inv, name="middle", after=(theirs,),
            )
        else:
            total = jnp.sum(shares.reshape(devices, share, size), axis=0)
            inner_t = dot(
                lax.dynamic_slice_in_dim(diag_adjoint.T, me * share, share, 0)
                - dot(total, diag_inverse),
                diag_factor,
            )
            at = lax.broadcasted_iota(jnp.int32, inner_t.shape, 0) + me * share
            across = lax.broadcasted_iota(jnp.int32, inner_t.shape, 1)
            inner_t = jnp.where(across > at, inner_t, jnp.where(across == at, 0.5 * inner_t, 0.0))
            left_t = jnp.tile(dot(inner_t, diag_inverse), (devices, 1))
        gathered = lax.all_to_all(left_t, AXES, 0, 0, tiled=True)

        panel_grad, inv = call(
            panel_kernel, [f32(*panel.shape), bf16(*inv.shape)], panel_adjoint, inv, mine, came,
            name="panel_grad",
        )
        (diag_grad,) = call(last_kernel, [f32(size, size)], gathered, inv, name="diag_grad")
        return panel_grad, diag_grad

    return on_device


def solution(mesh):
    in_specs = (P("row", "col"), P(("row", "col"), None), P(("row", "col"), None), P(), P(), P())
    out_specs = (P(("row", "col"), None), P())
    return jax.shard_map(
        make_on_device(mesh.shape["row"], mesh.shape["col"]),
        mesh=mesh, in_specs=in_specs, out_specs=out_specs, check_vma=False,
    )
```

time: 295 us -> 75.1 us (0.25)
  waiting for transfers between devices: 250 us -> 27.7 us
  starting transfers between devices: 0.12 us -> 27.6 us
  between operations: 13.9 us -> 0.74 us
  matrix products: 12.7 us -> 0 us
  blocking collectives: 11.8 us -> 0 us
  Pallas kernels: 0 us -> 11.5 us
    psum x1 -> x0, waiting for transfers between devices: 129 us -> none  [on_device(): gram = lax.psum(local_gram, ('row', 'col'))]
    all_gather x1 -> x0, waiting for transfers between devices: 99.5 us -> none  [on_device(): full_panel = lax.all_gather(row_block, 'row', axis=0, tiled=True)]
    reduce_scatter x1 -> x0, waiting for transfers between devices: 21.6 us -> none  [on_device(): lax.psum_scatter(jnp.dot(trail_adjoint, column_panel, precision=highest,...]
    ppermute x0 -> x15, starting transfers between devices: none -> 20.4 us  [flip(): return lax.ppermute(x, AXES, pairs)]
    ppermute x0 -> x15, waiting for transfers between devices: none -> 19 us  [flip(): return lax.ppermute(x, AXES, pairs)]
    dot_general x6 -> x0, matrix products: 12.7 us -> none  [the longest x1 7.57 us: on_device(): jnp.dot(trail_adjoint, column_panel, precision=highest, preferred_element...]
    all_gather x1 -> x0, blocking collectives: 11.8 us -> none  [on_device(): row_block = lax.all_gather(panel, 'col', axis=0, tiled=True)]
    pallas_call x0 -> x9, Pallas kernels: none -> 11.5 us  [call(): pl.pallas_call(body, grid=(1,), out_shape=out, in_specs=(in_specs or [who...]
  transfers between devices with their start and end apart: 3 -> 17, of which waited for: 3 -> 9; matrix products, arithmetic and copies ran while one was open for 0% -> 0% of each run, Pallas kernels for 0% -> 5%
where the time goes in v4:
time: 75.1 us; the launch traced here: 74.6 us
  waiting for transfers between devices  27.7 us (37%)
  starting transfers between devices  27.6 us (37%)
  Pallas kernels  11.5 us (15%)
  local copies, waits for them, and re-layouts  7.04 us (9%)
    ppermute x15, starting transfers between devices, flip(): return lax.ppermute(x, AXES, pairs)  20.4 us
    ppermute x15, waiting for transfers between devices, flip(): return lax.ppermute(x, AXES, pairs)  19 us
    pallas_call x9, Pallas kernels, call(): pl.pallas_call(body, grid=(1,), out_shape=out, in_specs=(in_specs or [who...  11.5 us
    all_to_all x1, waiting for transfers between devices, on_device(): shares = lax.all_to_all(gram_t, AXES, 0, 0, tiled=True)  8.76 us
    unnamed x14, local copies, waits for them, and re-layouts  7.04 us
    all_to_all x1, starting transfers between devices, on_device(): shares = lax.all_to_all(gram_t, AXES, 0, 0, tiled=True)  4.63 us
    all_to_all x1, starting transfers between devices, on_device(): gathered = lax.all_to_all(left_t, AXES, 0, 0, tiled=True)  2.59 us
  transfers between devices with their start and end apart: 17, of which 9 were waited for; matrix products, arithmetic and copies ran while one was open for 0% of the time, Pallas kernels for 5%

profile of v4, /device:TPU:0, one launch (start us, length us, event | category | flops | bytes accessed | tf_op | source)
XLA Modules:
  0.0 74.6 jit_solution(4552758714811522265)
XLA Ops:
  0.6 5.1 %collective-permute-start.3 = (f32[192,256]{1,0:T(8,128)}, f32[192,256]{1,0:T(8,128)S(1)}, u32[]{:S(2)}, u32[]{:S(2)}) collective-permute-start(f32[192,256]{1,0:T(8,128)} %refs_0_.4), channel_id=1, source_target_pairs={{0,24},{1,25},{2,26},{3,27},{4,28},{5,29},{6,30},{7,31},{8,16},{9,... | collective-permute-start | bytes 589832 | tf_op jit(solution)/shard_map/ppermute | solution.py:243
  5.7 1.5 %collective-permute-start = (f32[192,256]{1,0:T(8,128)}, f32[192,256]{1,0:T(8,128)S(1)}, u32[]{:S(2)}, u32[]{:S(2)}) collective-permute-start(f32[192,256]{1,0:T(8,128)} %refs_0_.4), channel_id=1, source_target_pairs={{0,2},{1,3},{2,0},{3,1},{4,6},{5,7},{6,4},{7,5},{8,10},{9,11},{10,... | collective-permute-start | bytes 589832 | tf_op jit(solution)/shard_map/ppermute | solution.py:243
  7.2 0.0 collective-permute-start.5
  7.2 4.5 %collective-permute-done.3.refs_1_ = f32[192,256]{1,0:T(8,128)S(1)} collective-permute-done((f32[192,256]{1,0:T(8,128)}, f32[192,256]{1,0:T(8,128)S(1)}, u32[]{:S(2)}, u32[]{:S(2)}) %collective-permute-start.3) | collective-permute-done | bytes 196640 | tf_op jit(solution)/shard_map/ppermute | solution.py:243
  11.7 3.0 %collective-permute-start.4 = (f32[192,256]{1,0:T(8,128)S(1)}, f32[192,256]{1,0:T(8,128)S(1)}, u32[]{:S(2)}, u32[]{:S(2)}) collective-permute-start(f32[192,256]{1,0:T(8,128)S(1)} %collective-permute-done.3.refs_1_), channel_id=1, source_target_pairs={{0,8},{1,9},{2,10},{3,11},{4,12},{5,13},{6,14},{7,15},{8,0},{9,1},... | collective-permute-start | bytes 589832 | tf_op jit(solution)/shard_map/ppermute | solution.py:243
  14.8 0.0 collective-permute-start.1
  14.8 0.0 collective-permute-done.refs_1_.refs_2_
  14.8 0.5 collective-permute-start.2
  15.3 0.2 collective-permute-done.5.refs_0_
  15.5 2.3 %collective-permute-start.8 = (f32[192,256]{1,0:T(8,128)S(1)}, f32[192,256]{1,0:T(8,128)S(1)}, u32[]{:S(2)}, u32[]{:S(2)}) collective-permute-start(f32[192,256]{1,0:T(8,128)S(1)} %get-tuple-element.22), channel_id=1, source_target_pairs={{0,6},{1,7},{2,4},{3,5},{4,2},{5,3},{6,0},{7,1},{8,14},{9,15},{10,... | collective-permute-start | bytes 589832 | tf_op jit(solution)/shard_map/ppermute | solution.py:243
  17.8 0.7 collective-permute-start.6
  18.6 0.8 %collective-permute-done.4.refs_1_ = f32[192,256]{1,0:T(8,128)S(1)} collective-permute-done((f32[192,256]{1,0:T(8,128)S(1)}, f32[192,256]{1,0:T(8,128)S(1)}, u32[]{:S(2)}, u32[]{:S(2)}) %collective-permute-start.4) | collective-permute-done | bytes 196640 | tf_op jit(solution)/shard_map/ppermute | solution.py:243
  19.4 1.5 %collective-permute-start.7 = (f32[192,256]{1,0:T(8,128)S(1)}, f32[192,256]{1,0:T(8,128)S(1)}, u32[]{:S(2)}, u32[]{:S(2)}) collective-permute-start(f32[192,256]{1,0:T(8,128)S(1)} %get-tuple-element.21.refs_0_), channel_id=1, source_target_pairs={{0,4},{1,5},{2,6},{3,7},{4,0},{5,1},{6,2},{7,3},{8,12},{9,13},{10,... | collective-permute-start | bytes 589832 | tf_op jit(solution)/shard_map/ppermute | solution.py:243
  20.9 0.0 copy-start.1
  20.9 0.9 %copy-done.1 = f32[192,256]{1,0:T(8,128)S(1)} copy-done((f32[192,256]{1,0:T(8,128)S(1)}, f32[192,256]{1,0:T(8,128)}, u32[]{:S(2)}) %copy-start.1) | copy-done | bytes 196632
  21.9 0.0 collective-permute-done.1.refs_2_
  21.9 1.5 %collective-permute-start.11 = (f32[192,256]{1,0:T(8,128)S(1)}, f32[192,256]{1,0:T(8,128)S(1)}, u32[]{:S(2)}, u32[]{:S(2)}) collective-permute-start(f32[192,256]{1,0:T(8,128)S(1)} %get-tuple-element.23), channel_id=1, source_target_pairs={{0,6},{1,7},{2,4},{3,5},{4,2},{5,3},{6,0},{7,1},{8,14},{9,15},{10,... | collective-permute-start | bytes 589832 | tf_op jit(solution)/shard_map/ppermute | solution.py:243
  23.4 0.0 collective-permute-done.2.refs_3_
  23.4 0.5 collective-permute-start.9
  23.9 0.4 collective-permute-done.8.refs_3_
  24.3 1.5 %collective-permute-start.10 = (f32[192,256]{1,0:T(8,128)S(1)}, f32[192,256]{1,0:T(8,128)S(1)}, u32[]{:S(2)}, u32[]{:S(2)}) collective-permute-start(f32[192,256]{1,0:T(8,128)S(1)} %get-tuple-element.19.refs_9_.refs_4_), channel_id=1, source_target_pairs={{0,4},{1,5},{2,6},{3,7},{4,0},{5,1},{6,2},{7,3},{8,12},{9,13},{10,... | collective-permute-start | bytes 589832 | tf_op jit(solution)/shard_map/ppermute | solution.py:243
  25.8 0.0 copy-start
  25.8 2.3 %copy-done = f32[768,1536]{1,0:T(8,128)S(1)} copy-done((f32[768,1536]{1,0:T(8,128)S(1)}, f32[768,1536]{1,0:T(8,128)}, u32[]{:S(2)}) %copy-start) | copy-done | bytes 4718616
  28.2 0.0 copy-start.2
  28.2 0.9 %copy-done.2 = f32[192,256]{1,0:T(8,128)S(1)} copy-done((f32[192,256]{1,0:T(8,128)S(1)}, f32[192,256]{1,0:T(8,128)}, u32[]{:S(2)}) %copy-start.2) | copy-done | bytes 196632
  29.1 0.0 copy-start.4
  29.1 0.9 %copy-done.4 = f32[256,256]{1,0:T(8,128)S(1)} copy-done((f32[256,256]{1,0:T(8,128)S(1)}, f32[256,256]{1,0:T(8,128)}, u32[]{:S(2)}) %copy-start.4) | copy-done | bytes 262168
  30.0 0.0 copy-start.5
  30.0 0.9 %copy-done.5 = f32[256,256]{1,0:T(8,128)S(1)} copy-done((f32[256,256]{1,0:T(8,128)S(1)}, f32[256,256]{1,0:T(8,128)}, u32[]{:S(2)}) %copy-start.5) | copy-done | bytes 262168
  31.0 0.0 copy-start.6
  31.0 0.9 %copy-done.6 = f32[256,256]{1,0:T(8,128)S(1)} copy-done((f32[256,256]{1,0:T(8,128)S(1)}, f32[256,256]{1,0:T(8,128)}, u32[]{:S(2)}) %copy-start.6) | copy-done | bytes 262168
  31.9 2.5 %prepare.1 = (bf16[2,256,768]{2,1,0:T(8,128)(2,1)S(1)}, f32[256,256]{1,0:T(8,128)S(1)}, f32[256,256]{1,0:T(8,128)S(1)}, bf16[2,256,256]{2,1,0:T(8,128)(2,1)S(1)}...) custom-call(f32[192,256]{1,0:T(8,128)S(1)} %copy-done.1, ...), custom_call_target="tpu_custom_call" | custom-call | flops 1000 | bytes 1000 | tf_op jit(solution)/shard_map/prepare/pallas_call | solution.py:214
  34.5 0.0 collective-permute-done.6.refs_1_
  34.5 0.0 collective-permute-done.7.refs_2_
  34.5 0.0 collective-permute-done.11.refs_7_
  34.5 1.4 %collective-permute-done.9.refs_5_ = f32[192,256]{1,0:T(8,128)S(1)} collective-permute-done((f32[192,256]{1,0:T(8,128)S(1)}, f32[192,256]{1,0:T(8,128)S(1)}, u32[]{:S(2)}, u32[]{:S(2)}) %collective-permute-start.9) | collective-permute-done | bytes 196640 | tf_op jit(solution)/shard_map/ppermute | solution.py:243
  35.9 0.0 collective-permute-done.10.refs_6_
  35.9 0.1 pick.1
  35.9 0.1 collective-permute-start.12
  36.0 2.3 %collective-permute-done.12.refs_8_ = f32[4,192,256]{2,1,0:T(8,128)S(1)} collective-permute-done((f32[4,192,256]{2,1,0:T(8,128)S(1)}, f32[4,192,256]{2,1,0:T(8,128)S(1)}, u32[]{:S(2)}, u32[]{:S(2)}) %collective-permute-start.12) | collective-permute-done | bytes 786464 | tf_op jit(solution)/shard_map/ppermute | solution.py:243
  38.3 0.0 copy-start.3
  38.3 5.8 %product.1 = (f32[2,192,256]{2,1,0:T(8,128)S(1)}, f32[2,192,256]{2,1,0:T(8,128)S(1)}, f32[256,256]{1,0:T(8,128)}) custom-call(f32[192,256]{1,0:T(8,128)S(1)} %get-tuple-element.21.refs_0_, f32[192,256]{1,0:T(8,128)S(1)} %collective-permute-done.6.refs_1_, f32[192,256]{1,0:T(8,128)S(1)} %collective-permute-done.7.refs_2_, ...), custom_call_target="tpu_custom_call" | custom-call | flops 1000 | bytes 1000 | tf_op jit(solution)/shard_map/product/pallas_call | solution.py:214
  44.1 4.6 %all-to-all-start = ((f32[32,8,256]{2,1,0:T(8,128)}), f32[32,8,256]{2,1,0:T(8,128)S(1)}, u32[]{:S(2)}, u32[]{:S(2)}) async-start(f32[32,8,256]{2,1,0:T(8,128)} %bitcast), calls=%async_computation | async-start | bytes 524288 | tf_op jit(solution)/shard_map/all_to_all | solution.py:320
  48.7 0.3 collective-permute-start.13
  49.0 1.5 %collective-permute-done.13.refs_1_ = f32[2,192,256]{2,1,0:T(8,128)S(1)} collective-permute-done((f32[2,192,256]{2,1,0:T(8,128)S(1)}, f32[2,192,256]{2,1,0:T(8,128)S(1)}, u32[]{:S(2)}, u32[]{:S(2)}) %collective-permute-start.13) | collective-permute-done | bytes 393248 | tf_op jit(solution)/shard_map/ppermute | solution.py:243
  50.5 8.8 %all-to-all-done = f32[32,8,256]{2,1,0:T(8,128)S(1)} async-done(((f32[32,8,256]{2,1,0:T(8,128)}), f32[32,8,256]{2,1,0:T(8,128)S(1)}, u32[]{:S(2)}, u32[]{:S(2)}) %all-to-all-start) | async-done | bytes 262176 | tf_op jit(solution)/shard_map/all_to_all | solution.py:320
  59.3 1.1 %middle.1 = f32[256,256]{1,0:T(8,128)} custom-call(f32[256,256]{1,0:T(8,128)S(1)} %bitcast.5, f32[256,256]{1,0:T(8,128)S(1)} %get-tuple-element.33.refs_1_, bf16[2,256,256]{2,1,0:T(8,128)(2,1)S(1)} %get-tuple-element.34.refs_2_, bf16[2,256,256]{2,1,0:T(8,128)(2,1)S(1)} %get-tuple-element.20.refs_1_.refs_3_, f32[1,192,256]{2,1,0:T(8,128)S(1)} %get-tuple-element.30.refs_4_), custom_call_target="tpu_custom_call" | custom-call | flops 1000 | bytes 1000 | tf_op jit(solution)/shard_map/middle/pallas_call | solution.py:214
  60.4 2.6 %all-to-all-start.1 = ((f32[32,8,256]{2,1,0:T(8,128)}), f32[32,8,256]{2,1,0:T(8,128)S(1)}, u32[]{:S(2)}, u32[]{:S(2)}) async-start(f32[32,8,256]{2,1,0:T(8,128)} %bitcast.2), calls=%async_computation.1 | async-start | bytes 524288 | tf_op jit(solution)/shard_map/all_to_all | solution.py:337
  63.0 1.7 %collective-permute-start.14 = (f32[1,192,256]{2,1,0:T(8,128)S(1)}, f32[1,192,256]{2,1,0:T(8,128)S(1)}, u32[]{:S(2)}, u32[]{:S(2)}) collective-permute-start(f32[1,192,256]{2,1,0:T(8,128)S(1)} %get-tuple-element.30.refs_4_), channel_id=1, source_target_pairs={{0,2},{1,3},{2,0},{3,1},{4,6},{5,7},{6,4},{7,5},{8,10},{9,11},{10,... | collective-permute-start | bytes 589832 | tf_op jit(solution)/shard_map/ppermute | solution.py:243
  64.7 8.0 %collective-permute-done.14.refs_3_ = f32[1,192,256]{2,1,0:T(8,128)S(1)} collective-permute-done((f32[1,192,256]{2,1,0:T(8,128)S(1)}, f32[1,192,256]{2,1,0:T(8,128)S(1)}, u32[]{:S(2)}, u32[]{:S(2)}) %collective-permute-start.14) | collective-permute-done | bytes 196640 | tf_op jit(solution)/shard_map/ppermute | solution.py:243
  72.6 0.0 copy-done.3
  72.6 1.0 %panel_grad.1 = (f32[192,256]{1,0:T(8,128)}, bf16[2,256,256]{2,1,0:T(8,128)(2,1)S(1)}) custom-call(f32[192,256]{1,0:T(8,128)S(1)} %copy-done.3, bf16[2,256,256]{2,1,0:T(8,128)(2,1)S(1)} %get-tuple-element.20.refs_1_.refs_3_, f32[1,192,256]{2,1,0:T(8,128)S(1)} %get-tuple-element.29.refs_2_, f32[1,192,256]{2,1,0:T(8,128)S(1)} %collective-permute-done.14.refs_3_), custom_call_target="tpu_custom_call" | custom-call | flops 1000 | bytes 1000 | tf_op jit(solution)/shard_map/panel_grad/pallas_call | solution.py:214
  73.6 0.0 all-to-all-done.1
  73.6 1.1 %diag_grad.1 = f32[256,256]{1,0:T(8,128)} custom-call(f32[256,256]{1,0:T(8,128)S(1)} %bitcast.4, bf16[2,256,256]{2,1,0:T(8,128)(2,1)S(1)} %get-tuple-element.35.refs_1_), custom_call_target="tpu_custom_call" | custom-call | flops 1000 | bytes 1000 | tf_op jit(solution)/shard_map/diag_grad/pallas_call | solution.py:214
  (3 shorter events, 0.1 us)
Async XLA Ops:
  0.6 11.1 %collective-permute-start.3 = (f32[192,256]{1,0:T(8,128)}, f32[192,256]{1,0:T(8,128)S(1)}, u32[]{:S(2)}, u32[]{:S(2)}) collective-permute-start(f32[192,256]{1,0:T(8,128)} %refs_0_.4), channel_id=1, source_target_pairs={{0,24},{1,25},{2,26},{3,27},{4,28},{5,29},{6,30},{7,31},{8,16},{9,... | collective-permute-start | bytes 589832 | tf_op jit(solution)/shard_map/ppermute | solution.py:243
  5.7 9.0 %collective-permute-start = (f32[192,256]{1,0:T(8,128)}, f32[192,256]{1,0:T(8,128)S(1)}, u32[]{:S(2)}, u32[]{:S(2)}) collective-permute-start(f32[192,256]{1,0:T(8,128)} %refs_0_.4), channel_id=1, source_target_pairs={{0,2},{1,3},{2,0},{3,1},{4,6},{5,7},{6,4},{7,5},{8,10},{9,11},{10,... | collective-permute-start | bytes 589832 | tf_op jit(solution)/shard_map/ppermute | solution.py:243
  7.2 8.3 %collective-permute-start.5 = (f32[192,256]{1,0:T(8,128)}, f32[192,256]{1,0:T(8,128)S(1)}, u32[]{:S(2)}, u32[]{:S(2)}) collective-permute-start(f32[192,256]{1,0:T(8,128)} %refs_0_.4), channel_id=1, source_target_pairs={{0,8},{1,9},{2,10},{3,11},{4,12},{5,13},{6,14},{7,15},{8,0},{9,1},... | collective-permute-start | bytes 589832 | tf_op jit(solution)/shard_map/ppermute | solution.py:243
  11.7 7.7 %collective-permute-start.4 = (f32[192,256]{1,0:T(8,128)S(1)}, f32[192,256]{1,0:T(8,128)S(1)}, u32[]{:S(2)}, u32[]{:S(2)}) collective-permute-start(f32[192,256]{1,0:T(8,128)S(1)} %collective-permute-done.3.refs_1_), channel_id=1, source_target_pairs={{0,8},{1,9},{2,10},{3,11},{4,12},{5,13},{6,14},{7,15},{8,0},{9,1},... | collective-permute-start | bytes 589832 | tf_op jit(solution)/shard_map/ppermute | solution.py:243
  14.8 7.1 %collective-permute-start.1 = (f32[192,256]{1,0:T(8,128)}, f32[192,256]{1,0:T(8,128)S(1)}, u32[]{:S(2)}, u32[]{:S(2)}) collective-permute-start(f32[192,256]{1,0:T(8,128)} %refs_0_.4), channel_id=1, source_target_pairs={{0,1},{1,0},{2,3},{3,2},{4,5},{5,4},{6,7},{7,6},{8,9},{9,8},{10,11... | collective-permute-start | bytes 589832 | tf_op jit(solution)/shard_map/ppermute | solution.py:243
  14.8 8.6 %collective-permute-start.2 = (f32[192,256]{1,0:T(8,128)S(1)}, f32[192,256]{1,0:T(8,128)S(1)}, u32[]{:S(2)}, u32[]{:S(2)}) collective-permute-start(f32[192,256]{1,0:T(8,128)S(1)} %collective-permute-done.refs_1_.refs_2_), channel_id=1, source_target_pairs={{0,1},{1,0},{2,3},{3,2},{4,5},{5,4},{6,7},{7,6},{8,9},{9,8},{10,11... | collective-permute-start | bytes 589832 | tf_op jit(solution)/shard_map/ppermute | solution.py:243
  15.5 8.8 %collective-permute-start.8 = (f32[192,256]{1,0:T(8,128)S(1)}, f32[192,256]{1,0:T(8,128)S(1)}, u32[]{:S(2)}, u32[]{:S(2)}) collective-permute-start(f32[192,256]{1,0:T(8,128)S(1)} %get-tuple-element.22), channel_id=1, source_target_pairs={{0,6},{1,7},{2,4},{3,5},{4,2},{5,3},{6,0},{7,1},{8,14},{9,15},{10,... | collective-permute-start | bytes 589832 | tf_op jit(solution)/shard_map/ppermute | solution.py:243
  17.8 16.6 %collective-permute-start.6 = (f32[192,256]{1,0:T(8,128)S(1)}, f32[192,256]{1,0:T(8,128)S(1)}, u32[]{:S(2)}, u32[]{:S(2)}) collective-permute-start(f32[192,256]{1,0:T(8,128)S(1)} %get-tuple-element.22), channel_id=1, source_target_pairs={{0,2},{1,3},{2,0},{3,1},{4,6},{5,7},{6,4},{7,5},{8,10},{9,11},{10,... | collective-permute-start | bytes 589832 | tf_op jit(solution)/shard_map/ppermute | solution.py:243
  19.4 15.1 %collective-permute-start.7 = (f32[192,256]{1,0:T(8,128)S(1)}, f32[192,256]{1,0:T(8,128)S(1)}, u32[]{:S(2)}, u32[]{:S(2)}) collective-permute-start(f32[192,256]{1,0:T(8,128)S(1)} %get-tuple-element.21.refs_0_), channel_id=1, source_target_pairs={{0,4},{1,5},{2,6},{3,7},{4,0},{5,1},{6,2},{7,3},{8,12},{9,13},{10,... | collective-permute-start | bytes 589832 | tf_op jit(solution)/shard_map/ppermute | solution.py:243
  20.9 0.9 %copy-start.1 = (f32[192,256]{1,0:T(8,128)S(1)}, f32[192,256]{1,0:T(8,128)}, u32[]{:S(2)}) copy-start(f32[192,256]{1,0:T(8,128)} %refs_0_.4) | copy-start | bytes 589828
  21.9 12.6 %collective-permute-start.11 = (f32[192,256]{1,0:T(8,128)S(1)}, f32[192,256]{1,0:T(8,128)S(1)}, u32[]{:S(2)}, u32[]{:S(2)}) collective-permute-start(f32[192,256]{1,0:T(8,128)S(1)} %get-tuple-element.23), channel_id=1, source_target_pairs={{0,6},{1,7},{2,4},{3,5},{4,2},{5,3},{6,0},{7,1},{8,14},{9,15},{10,... | collective-permute-start | bytes 589832 | tf_op jit(solution)/shard_map/ppermute | solution.py:243
  23.4 12.5 %collective-permute-start.9 = (f32[192,256]{1,0:T(8,128)S(1)}, f32[192,256]{1,0:T(8,128)S(1)}, u32[]{:S(2)}, u32[]{:S(2)}) collective-permute-start(f32[192,256]{1,0:T(8,128)S(1)} %get-tuple-element.23), channel_id=1, source_target_pairs={{0,2},{1,3},{2,0},{3,1},{4,6},{5,7},{6,4},{7,5},{8,10},{9,11},{10,... | collective-permute-start | bytes 589832 | tf_op jit(solution)/shard_map/ppermute | solution.py:243
  24.3 11.6 %collective-permute-start.10 = (f32[192,256]{1,0:T(8,128)S(1)}, f32[192,256]{1,0:T(8,128)S(1)}, u32[]{:S(2)}, u32[]{:S(2)}) collective-permute-start(f32[192,256]{1,0:T(8,128)S(1)} %get-tuple-element.19.refs_9_.refs_4_), channel_id=1, source_target_pairs={{0,4},{1,5},{2,6},{3,7},{4,0},{5,1},{6,2},{7,3},{8,12},{9,13},{10,... | collective-permute-start | bytes 589832 | tf_op jit(solution)/shard_map/ppermute | solution.py:243
  25.8 2.3 %copy-start = (f32[768,1536]{1,0:T(8,128)S(1)}, f32[768,1536]{1,0:T(8,128)}, u32[]{:S(2)}) copy-start(f32[768,1536]{1,0:T(8,128)} %refs_8_.1) | copy-start | bytes 14155780
  28.2 0.9 %copy-start.2 = (f32[192,256]{1,0:T(8,128)S(1)}, f32[192,256]{1,0:T(8,128)}, u32[]{:S(2)}) copy-start(f32[192,256]{1,0:T(8,128)} %refs_0_.5) | copy-start | bytes 589828
  29.1 0.9 %copy-start.4 = (f32[256,256]{1,0:T(8,128)S(1)}, f32[256,256]{1,0:T(8,128)}, u32[]{:S(2)}) copy-start(f32[256,256]{1,0:T(8,128)} %refs_5_.1) | copy-start | bytes 786436
  30.0 0.9 %copy-start.5 = (f32[256,256]{1,0:T(8,128)S(1)}, f32[256,256]{1,0:T(8,128)}, u32[]{:S(2)}) copy-start(f32[256,256]{1,0:T(8,128)} %refs_6_.1) | copy-start | bytes 786436
  31.0 0.9 %copy-start.6 = (f32[256,256]{1,0:T(8,128)S(1)}, f32[256,256]{1,0:T(8,128)}, u32[]{:S(2)}) copy-start(f32[256,256]{1,0:T(8,128)} %refs_7_.1) | copy-start | bytes 786436
  35.9 2.4 %collective-permute-start.12 = (f32[4,192,256]{2,1,0:T(8,128)S(1)}, f32[4,192,256]{2,1,0:T(8,128)S(1)}, u32[]{:S(2)}, u32[]{:S(2)}) collective-permute-start(f32[4,192,256]{2,1,0:T(8,128)S(1)} %pick.1), channel_id=1, source_target_pairs={{0,1},{1,0},{2,3},{3,2},{4,5},{5,4},{6,7},{7,6},{8,9},{9,8},{10,11... | collective-permute-start | bytes 2359304 | tf_op jit(solution)/shard_map/ppermute | solution.py:243
  38.3 34.3 %copy-start.3 = (f32[192,256]{1,0:T(8,128)S(1)}, f32[192,256]{1,0:T(8,128)}, u32[]{:S(2)}) copy-start(f32[192,256]{1,0:T(8,128)} %refs_0_.5) | copy-start | bytes 589828
  44.1 15.2 %all-to-all-start = ((f32[32,8,256]{2,1,0:T(8,128)}), f32[32,8,256]{2,1,0:T(8,128)S(1)}, u32[]{:S(2)}, u32[]{:S(2)}) async-start(f32[32,8,256]{2,1,0:T(8,128)} %bitcast), calls=%async_computation | async-start | bytes 524288 | tf_op jit(solution)/shard_map/all_to_all | solution.py:320
  48.7 1.8 %collective-permute-start.13 = (f32[2,192,256]{2,1,0:T(8,128)S(1)}, f32[2,192,256]{2,1,0:T(8,128)S(1)}, u32[]{:S(2)}, u32[]{:S(2)}) collective-permute-start(f32[2,192,256]{2,1,0:T(8,128)S(1)} %get-tuple-element.28), channel_id=1, source_target_pairs={{0,1},{1,0},{2,3},{3,2},{4,5},{5,4},{6,7},{7,6},{8,9},{9,8},{10,11... | collective-permute-start | bytes 1179656 | tf_op jit(solution)/shard_map/ppermute | solution.py:243
  60.4 13.2 %all-to-all-start.1 = ((f32[32,8,256]{2,1,0:T(8,128)}), f32[32,8,256]{2,1,0:T(8,128)S(1)}, u32[]{:S(2)}, u32[]{:S(2)}) async-start(f32[32,8,256]{2,1,0:T(8,128)} %bitcast.2), calls=%async_computation.1 | async-start | bytes 524288 | tf_op jit(solution)/shard_map/all_to_all | solution.py:337
  63.0 9.7 %collective-permute-start.14 = (f32[1,192,256]{2,1,0:T(8,128)S(1)}, f32[1,192,256]{2,1,0:T(8,128)S(1)}, u32[]{:S(2)}, u32[]{:S(2)}) collective-permute-start(f32[1,192,256]{2,1,0:T(8,128)S(1)} %get-tuple-element.30.refs_4_), channel_id=1, source_target_pairs={{0,2},{1,3},{2,0},{3,1},{4,6},{5,7},{6,4},{7,5},{8,10},{9,11},{10,... | collective-permute-start | bytes 589832 | tf_op jit(solution)/shard_map/ppermute | solution.py:243

commit v5 on v4

--- a/solution.py
+++ b/solution.py
@@ -72,33 +72,36 @@
             out[i] = ref[...]
 
 
-def prepare_kernel(
-    cols, order, blocks, *refs,
-):
-    rows_of, rest = refs[:cols], refs[cols:]
-    (
-        adjoint, factor, inverse, corner, trail,
-        rowt, start, base, unit, inv, trail_parts, landing, sems,
-    ) = rest
+def prepare_kernel(blocks, places, *refs):
+    rows_of, refs = refs[: len(places)], refs[len(places) :]
+    panel, adjoint, factor, inverse, corner, trail = refs[:6]
+    rowt, start, base, unit, inv, trail_parts = refs[6:12]
+    landing, here, sems = refs[12], refs[13:-1], refs[-1]
     rows = trail.shape[0] // blocks
-    copies = []
+    small = [
+        pltpu.make_async_copy(ref, to, sems.at[blocks + i])
+        for i, (ref, to) in enumerate(zip((panel, adjoint, factor, inverse, corner), here))
+    ]
+    large = []
     for i in range(blocks):
         at = pl.ds(i * rows, rows)
-        copies.append(pltpu.make_async_copy(trail.at[at], landing.at[at], sems.at[i]))
-        copies[-1].start()
+        large.append(pltpu.make_async_copy(trail.at[at], landing.at[at], sems.at[i]))
+    for copy in small + large:
+        copy.start()
+    for copy in small:
+        copy.wait()
+    panel, adjoint, factor, inverse, corner = here
     height = adjoint.shape[0]
-    for d in range(cols):
-        high, low = parts(rows_of[order.index(d)][...].T)
+    for d, block in enumerate([panel] + [rows_of[i] for i in places]):
+        high, low = parts(block[...].T)
         rowt[0, :, d * height : (d + 1) * height] = high
         rowt[1, :, d * height : (d + 1) * height] = low
-    start[...] = dot_t(rows_of[0][...], adjoint[...])
+    start[...] = dot_t(panel[...], adjoint[...])
     base[...] = dot_t(corner[...], factor[...])
-    high, low = parts(dot(inverse[...], factor[...]))
-    unit[0], unit[1] = high, low
-    high, low = parts(inverse[...])
-    inv[0], inv[1] = high, low
+    unit[0], unit[1] = parts(dot(inverse[...], factor[...]))
+    inv[0], inv[1] = parts(inverse[...])
     for i in range(blocks):
-        copies[i].wait()
+        large[i].wait()
         at = pl.ds(i * rows, rows)
         trail_parts[0, at, :], trail_parts[1, at, :] = parts(landing[at, :])
 
@@ -135,28 +138,21 @@
 
 
 def product_kernel(group, cols, count, *refs):
-    pieces, (rowt, start, trail, keep, send, gram_t, wide, split) = refs[:count], refs[count:]
+    pieces, (rowt, start, trail, keep, send, gram_t, wide, split, image) = refs[:count], refs[count:]
     if count == 1:
         fill_all(group, cols, pieces[0], wide)
     else:
         fill_sets(pieces[0:4], pieces[4:8], pieces[8], wide)
-    height = split.shape[1] // cols
+    height = image.shape[0] // cols
+    for i in range(cols):
+        at = pl.ds(i * height, height)
+        image[at, :] = dot_three(trail[0, at, :], trail[1, at, :], wide[0], wide[1])
     col = lax.axis_index("col")
-    for target in range(cols):
-        at = pl.ds(target * height, height)
-        block = dot_three(trail[0, at, :], trail[1, at, :], wide[0], wide[1])
-        d = target ^ col
-        at = pl.ds(pl.multiple_of(d * height, height), height)
+    for d in range(cols):
+        block = image[pl.ds(pl.multiple_of((d ^ col) * height, height), height), :]
+        at = pl.ds(d * height, height)
         split[0, at, :], split[1, at, :] = parts(block)
-
-        @pl.when(d % 2 == 0)
-        def _():
-            keep[d // 2] = block
-
-        @pl.when(d % 2 == 1)
-        def _():
-            send[d // 2] = block
-
+        (send if d % 2 else keep)[d // 2] = block
     gram_t[...] = start[...] - 2.0 * dot_three(rowt[0], rowt[1], split[0], split[1])
 
 
@@ -182,15 +178,16 @@
     out[...] = jnp.where(across < at, full, jnp.where(across == at, 0.5 * full, 0.0))
 
 
-def add_kernel(keep, came, mine, theirs):
+def add_kernel(keep, came, adjoint, inv, mine, theirs):
     for i in range(keep.shape[0] // 2):
-        mine[i] = keep[2 * i] + came[2 * i]
-        theirs[i] = keep[2 * i + 1] + came[2 * i + 1]
-
-
-def panel_kernel(adjoint, inv, mine, came, out, inv_on):
+        own = -2.0 * (keep[2 * i] + came[2 * i])
+        mine[i] = dot_parts(own if i else adjoint[...] + own, inv[0], inv[1])
+        theirs[i] = dot_parts(-2.0 * (keep[2 * i + 1] + came[2 * i + 1]), inv[0], inv[1])
+
+
+def panel_kernel(mine, came, inv, out, inv_on):
     inv_on[...] = inv[...]
-    out[...] = dot_parts(adjoint[...] - 2.0 * (mine[0] + came[0]), inv[0], inv[1])
+    out[...] = mine[0] + came[0]
 
 
 def whole(shape):
@@ -267,23 +264,30 @@
                     choose_kernel, [f32(height, size)] * 2, pieces[near], pieces[far],
                     name="choose", after=(row_blocks[1],) if near else (),
                 )
-                sets.append([own, flip(other, col=2), flip(own, y=1), flip(other, y=1, col=2)])
+                diagonal = flip(sets[0][3], plane=1) if sets else flip(other, y=1, col=2)
+                sets.append([own, flip(other, col=2), flip(own, y=1), diagonal])
             chosen = own
         else:
             chosen = jnp.stack([pieces[d] for d in range(cols)] * group)
 
         blocks = 4
+        params = [
+            pltpu.with_memory_space_constraint(x, pltpu.HBM)
+            for x in (panel, panel_adjoint, diag_factor, diag_inverse, diag_adjoint, trail_adjoint)
+        ]
         rowt, start, base, unit, inv, trail = call(
-            functools.partial(prepare_kernel, cols, order, blocks),
+            functools.partial(
+                prepare_kernel, blocks, [order.index(d) - 1 for d in range(1, cols)]
+            ),
             [bf16(2, size, cols * height), f32(size, size), f32(size, size)]
             + [bf16(2, size, size)] * 2 + [bf16(2, *trail_adjoint.shape)],
-            *row_blocks, panel_adjoint, diag_factor, diag_inverse, diag_adjoint, trail_adjoint,
-            name="prepare", after=(chosen,),
-            in_specs=[whole(panel.shape)] * (cols + 1) + [whole((size, size))] * 3 + [ANY],
+            *row_blocks[1:], *params, name="prepare", after=(chosen,),
+            in_specs=[whole(panel.shape)] * (cols - 1) + [pl.BlockSpec(memory_space=pltpu.HBM)] * 6,
             out_specs=[VMEM] * 6,
-            scratch=[
-                pltpu.VMEM(trail_adjoint.shape, jnp.float32), pltpu.SemaphoreType.DMA((blocks,)),
-            ],
+            scratch=[pltpu.VMEM(trail_adjoint.shape, jnp.float32)]
+            + [pltpu.VMEM((height, size), jnp.float32)] * 2
+            + [pltpu.VMEM((size, size), jnp.float32)] * 3
+            + [pltpu.SemaphoreType.DMA((blocks + 5,))],
         )
 
         if paired:
@@ -302,11 +306,13 @@
             scratch=[
                 pltpu.VMEM((2, width, size), jnp.bfloat16),
                 pltpu.VMEM((2, cols * height, size), jnp.bfloat16),
+                pltpu.VMEM((cols * height, size), jnp.float32),
             ],
         )
 
         mine, theirs = call(
-            add_kernel, [f32(cols // 4, height, size)] * 2, keep, flip(send, col=1), name="add"
+            add_kernel, [f32(cols // 4, height, size)] * 2,
+            keep, flip(send, col=1), panel_adjoint, inv, name="add",
         )
         mask = 2
         while True:
@@ -337,8 +343,7 @@
         gathered = lax.all_to_all(left_t, AXES, 0, 0, tiled=True)
 
         panel_grad, inv = call(
-            panel_kernel, [f32(*panel.shape), bf16(*inv.shape)], panel_adjoint, inv, mine, came,
-            name="panel_grad",
+            panel_kernel, [f32(*panel.shape), bf16(*inv.shape)], mine, came, inv, name="panel_grad",
         )
         (diag_grad,) = call(last_kernel, [f32(size, size)], gathered, inv, name="diag_grad")
         return panel_grad, diag_grad

time: 75.1 us -> 68.5 us (0.912)
  local copies, waits for them, and re-layouts: 7.04 us -> 0.93 us
  Pallas kernels: 11.5 us -> 9.92 us
  waiting for transfers between devices: 27.7 us -> 28.8 us
    unnamed x14 -> x4, local copies, waits for them, and re-layouts: 7.04 us -> 0.93 us
    pallas_call x9, Pallas kernels: 11.5 us -> 9.92 us  [call(): pl.pallas_call(body, grid=(1,), out_shape=out, in_specs=(in_specs or [who...]
    ppermute x15, waiting for transfers between devices: 19 us -> 20.2 us  [flip(): return lax.ppermute(x, AXES, pairs)]
  transfers between devices with their start and end apart: 17 -> 17, of which waited for: 9 -> 10; matrix products, arithmetic and copies ran while one was open for 0% -> 0% of each run, Pallas kernels for 5% -> 6%
where the time goes in v5:
time: 68.5 us; the launch traced here: 68.2 us
  waiting for transfers between devices  28.8 us (42%)
  starting transfers between devices  27.8 us (41%)
  Pallas kernels  9.92 us (14%)
  local copies, waits for them, and re-layouts  0.93 us (1%)
  between operations  0.74 us (1%)
    ppermute x15, starting transfers between devices, flip(): return lax.ppermute(x, AXES, pairs)  20.5 us
    ppermute x15, waiting for transfers between devices, flip(): return lax.ppermute(x, AXES, pairs)  20.2 us
    pallas_call x9, Pallas kernels, call(): pl.pallas_call(body, grid=(1,), out_shape=out, in_specs=(in_specs or [who...  9.92 us
    all_to_all x1, waiting for transfers between devices, on_device(): shares = lax.all_to_all(gram_t, AXES, 0, 0, tiled=True)  8.42 us
    all_to_all x1, starting transfers between devices, on_device(): shares = lax.all_to_all(gram_t, AXES, 0, 0, tiled=True)  4.66 us
    all_to_all x1, starting transfers between devices, on_device(): gathered = lax.all_to_all(left_t, AXES, 0, 0, tiled=True)  2.59 us
  transfers between devices with their start and end apart: 17, of which 10 were waited for; matrix products, arithmetic and copies ran while one was open for 0% of the time, Pallas kernels for 6%

profile of v5, /device:TPU:0, one launch (start us, length us, event | category | flops | bytes accessed | tf_op | source)
XLA Modules:
  0.0 68.2 jit_solution(15781230945112279430)
XLA Ops:
  0.6 5.1 %collective-permute-start.1 = (f32[192,256]{1,0:T(8,128)}, f32[192,256]{1,0:T(8,128)S(1)}, u32[]{:S(2)}, u32[]{:S(2)}) collective-permute-start(f32[192,256]{1,0:T(8,128)} %refs_3_.1), channel_id=1, source_target_pairs={{0,24},{1,25},{2,26},{3,27},{4,28},{5,29},{6,30},{7,31},{8,16},{9,... | collective-permute-start | bytes 589832 | tf_op jit(solution)/shard_map/ppermute | solution.py:240
  5.7 1.5 %collective-permute-start.2 = (f32[192,256]{1,0:T(8,128)}, f32[192,256]{1,0:T(8,128)S(1)}, u32[]{:S(2)}, u32[]{:S(2)}) collective-permute-start(f32[192,256]{1,0:T(8,128)} %refs_3_.1), channel_id=1, source_target_pairs={{0,2},{1,3},{2,0},{3,1},{4,6},{5,7},{6,4},{7,5},{8,10},{9,11},{10,... | collective-permute-start | bytes 589832 | tf_op jit(solution)/shard_map/ppermute | solution.py:240
  7.2 0.0 collective-permute-start
  7.2 4.5 %collective-permute-done.1.refs_1_ = f32[192,256]{1,0:T(8,128)S(1)} collective-permute-done((f32[192,256]{1,0:T(8,128)}, f32[192,256]{1,0:T(8,128)S(1)}, u32[]{:S(2)}, u32[]{:S(2)}) %collective-permute-start.1) | collective-permute-done | bytes 196640 | tf_op jit(solution)/shard_map/ppermute | solution.py:240
  11.7 3.0 %collective-permute-start.6 = (f32[192,256]{1,0:T(8,128)S(1)}, f32[192,256]{1,0:T(8,128)S(1)}, u32[]{:S(2)}, u32[]{:S(2)}) collective-permute-start(f32[192,256]{1,0:T(8,128)S(1)} %collective-permute-done.1.refs_1_), channel_id=1, source_target_pairs={{0,8},{1,9},{2,10},{3,11},{4,12},{5,13},{6,14},{7,15},{8,0},{9,1},... | collective-permute-start | bytes 589832 | tf_op jit(solution)/shard_map/ppermute | solution.py:240
  14.8 0.0 collective-permute-start.10
  14.8 0.0 collective-permute-done.2.refs_2_.refs_0_
  14.8 0.5 collective-permute-start.11
  15.3 0.2 collective-permute-done.refs_0_
  15.5 2.3 %collective-permute-start.5 = (f32[192,256]{1,0:T(8,128)S(1)}, f32[192,256]{1,0:T(8,128)S(1)}, u32[]{:S(2)}, u32[]{:S(2)}) collective-permute-start(f32[192,256]{1,0:T(8,128)S(1)} %get-tuple-element.20), channel_id=1, source_target_pairs={{0,6},{1,7},{2,4},{3,5},{4,2},{5,3},{6,0},{7,1},{8,14},{9,15},{10,... | collective-permute-start | bytes 589832 | tf_op jit(solution)/shard_map/ppermute | solution.py:240
  17.8 0.7 %collective-permute-start.3 = (f32[192,256]{1,0:T(8,128)S(1)}, f32[192,256]{1,0:T(8,128)S(1)}, u32[]{:S(2)}, u32[]{:S(2)}) collective-permute-start(f32[192,256]{1,0:T(8,128)S(1)} %get-tuple-element.20), channel_id=1, source_target_pairs={{0,2},{1,3},{2,0},{3,1},{4,6},{5,7},{6,4},{7,5},{8,10},{9,11},{10,... | collective-permute-start | bytes 589832 | tf_op jit(solution)/shard_map/ppermute | solution.py:240
  18.6 0.8 %collective-permute-done.6.refs_1_ = f32[192,256]{1,0:T(8,128)S(1)} collective-permute-done((f32[192,256]{1,0:T(8,128)S(1)}, f32[192,256]{1,0:T(8,128)S(1)}, u32[]{:S(2)}, u32[]{:S(2)}) %collective-permute-start.6) | collective-permute-done | bytes 196640 | tf_op jit(solution)/shard_map/ppermute | solution.py:240
  19.4 1.5 %collective-permute-start.4 = (f32[192,256]{1,0:T(8,128)S(1)}, f32[192,256]{1,0:T(8,128)S(1)}, u32[]{:S(2)}, u32[]{:S(2)}) collective-permute-start(f32[192,256]{1,0:T(8,128)S(1)} %get-tuple-element.19.refs_0_), channel_id=1, source_target_pairs={{0,4},{1,5},{2,6},{3,7},{4,0},{5,1},{6,2},{7,3},{8,12},{9,13},{10,... | collective-permute-start | bytes 589832 | tf_op jit(solution)/shard_map/ppermute | solution.py:240
  20.9 0.0 copy-start.1
  20.9 0.9 %copy-done.1 = f32[192,256]{1,0:T(8,128)S(1)} copy-done((f32[192,256]{1,0:T(8,128)S(1)}, f32[192,256]{1,0:T(8,128)}, u32[]{:S(2)}) %copy-start.1) | copy-done | bytes 196632
  21.9 0.0 collective-permute-done.10.refs_1_
  21.9 1.6 %collective-permute-start.7 = (f32[192,256]{1,0:T(8,128)S(1)}, f32[192,256]{1,0:T(8,128)S(1)}, u32[]{:S(2)}, u32[]{:S(2)}) collective-permute-start(f32[192,256]{1,0:T(8,128)S(1)} %get-tuple-element.22), channel_id=1, source_target_pairs={{0,2},{1,3},{2,0},{3,1},{4,6},{5,7},{6,4},{7,5},{8,10},{9,11},{10,... | collective-permute-start | bytes 589832 | tf_op jit(solution)/shard_map/ppermute | solution.py:240
  23.4 0.0 collective-permute-done.11.refs_2_
  23.4 0.5 collective-permute-start.8
  23.9 0.4 collective-permute-done.5.refs_3_
  24.3 1.7 %collective-permute-start.9 = (f32[192,256]{1,0:T(8,128)S(1)}, f32[192,256]{1,0:T(8,128)S(1)}, u32[]{:S(2)}, u32[]{:S(2)}) collective-permute-start(f32[192,256]{1,0:T(8,128)S(1)} %collective-permute-done.5.refs_3_), channel_id=1, source_target_pairs={{0,8},{1,9},{2,10},{3,11},{4,12},{5,13},{6,14},{7,15},{8,0},{9,1},... | collective-permute-start | bytes 589832 | tf_op jit(solution)/shard_map/ppermute | solution.py:240
  26.0 3.0 %prepare.1 = (bf16[2,256,768]{2,1,0:T(8,128)(2,1)S(1)}, f32[256,256]{1,0:T(8,128)S(1)}, f32[256,256]{1,0:T(8,128)S(1)}, bf16[2,256,256]{2,1,0:T(8,128)(2,1)S(1)}...) custom-call(f32[192,256]{1,0:T(8,128)S(1)} %collective-permute-done.2.refs_2_.refs_0_, ...), custom_call_target="tpu_custom_call" | custom-call | flops 1000 | bytes 1000 | tf_op jit(solution)/shard_map/prepare/pallas_call | solution.py:211
  29.0 0.0 collective-permute-done.3.refs_1_
  29.0 0.0 collective-permute-done.4.refs_2_
  29.0 2.6 %collective-permute-done.7.refs_5_ = f32[192,256]{1,0:T(8,128)S(1)} collective-permute-done((f32[192,256]{1,0:T(8,128)S(1)}, f32[192,256]{1,0:T(8,128)S(1)}, u32[]{:S(2)}, u32[]{:S(2)}) %collective-permute-start.7) | collective-permute-done | bytes 196640 | tf_op jit(solution)/shard_map/ppermute | solution.py:240
  31.6 0.0 collective-permute-done.8.refs_6_
  31.6 0.0 collective-permute-done.9.refs_7_
  31.6 0.1 pick.1
  31.7 0.0 copy-start
  31.7 0.1 collective-permute-start.12
  31.8 2.3 %collective-permute-done.12.refs_8_ = f32[4,192,256]{2,1,0:T(8,128)S(1)} collective-permute-done((f32[4,192,256]{2,1,0:T(8,128)S(1)}, f32[4,192,256]{2,1,0:T(8,128)S(1)}, u32[]{:S(2)}, u32[]{:S(2)}) %collective-permute-start.12) | collective-permute-done | bytes 786464 | tf_op jit(solution)/shard_map/ppermute | solution.py:240
  34.0 3.6 %product.1 = (f32[2,192,256]{2,1,0:T(8,128)S(1)}, f32[2,192,256]{2,1,0:T(8,128)S(1)}, f32[256,256]{1,0:T(8,128)}) custom-call(f32[192,256]{1,0:T(8,128)S(1)} %get-tuple-element.19.refs_0_, f32[192,256]{1,0:T(8,128)S(1)} %collective-permute-done.3.refs_1_, f32[192,256]{1,0:T(8,128)S(1)} %collective-permute-done.4.refs_2_, ...), custom_call_target="tpu_custom_call" | custom-call | flops 1000 | bytes 1000 | tf_op jit(solution)/shard_map/product/pallas_call | solution.py:211
  37.6 4.7 %all-to-all-start = ((f32[32,8,256]{2,1,0:T(8,128)}), f32[32,8,256]{2,1,0:T(8,128)S(1)}, u32[]{:S(2)}, u32[]{:S(2)}) async-start(f32[32,8,256]{2,1,0:T(8,128)} %bitcast), calls=%async_computation | async-start | bytes 524288 | tf_op jit(solution)/shard_map/all_to_all | solution.py:326
  42.3 0.3 collective-permute-start.13
  42.6 1.5 %collective-permute-done.13.refs_1_ = f32[2,192,256]{2,1,0:T(8,128)S(1)} collective-permute-done((f32[2,192,256]{2,1,0:T(8,128)S(1)}, f32[2,192,256]{2,1,0:T(8,128)S(1)}, u32[]{:S(2)}, u32[]{:S(2)}) %collective-permute-start.13) | collective-permute-done | bytes 393248 | tf_op jit(solution)/shard_map/ppermute | solution.py:240
  44.1 0.0 copy-done
  44.1 0.4 add.1
  44.5 8.4 %all-to-all-done = f32[32,8,256]{2,1,0:T(8,128)S(1)} async-done(((f32[32,8,256]{2,1,0:T(8,128)}), f32[32,8,256]{2,1,0:T(8,128)S(1)}, u32[]{:S(2)}, u32[]{:S(2)}) %all-to-all-start) | async-done | bytes 262176 | tf_op jit(solution)/shard_map/all_to_all | solution.py:326
  52.9 1.1 %middle.1 = f32[256,256]{1,0:T(8,128)} custom-call(f32[256,256]{1,0:T(8,128)S(1)} %bitcast.5, f32[256,256]{1,0:T(8,128)S(1)} %get-tuple-element.33.refs_1_, bf16[2,256,256]{2,1,0:T(8,128)(2,1)S(1)} %get-tuple-element.34.refs_2_, bf16[2,256,256]{2,1,0:T(8,128)(2,1)S(1)} %get-tuple-element.28.refs_3_.refs_2_, f32[1,192,256]{2,1,0:T(8,128)S(1)} %get-tuple-element.30.refs_4_), custom_call_target="tpu_custom_call" | custom-call | flops 1000 | bytes 1000 | tf_op jit(solution)/shard_map/middle/pallas_call | solution.py:211
  54.0 2.6 %all-to-all-start.1 = ((f32[32,8,256]{2,1,0:T(8,128)}), f32[32,8,256]{2,1,0:T(8,128)S(1)}, u32[]{:S(2)}, u32[]{:S(2)}) async-start(f32[32,8,256]{2,1,0:T(8,128)} %bitcast.2), calls=%async_computation.1 | async-start | bytes 524288 | tf_op jit(solution)/shard_map/all_to_all | solution.py:343
  56.6 1.7 %collective-permute-start.14 = (f32[1,192,256]{2,1,0:T(8,128)S(1)}, f32[1,192,256]{2,1,0:T(8,128)S(1)}, u32[]{:S(2)}, u32[]{:S(2)}) collective-permute-start(f32[1,192,256]{2,1,0:T(8,128)S(1)} %get-tuple-element.30.refs_4_), channel_id=1, source_target_pairs={{0,2},{1,3},{2,0},{3,1},{4,6},{5,7},{6,4},{7,5},{8,10},{9,11},{10,... | collective-permute-start | bytes 589832 | tf_op jit(solution)/shard_map/ppermute | solution.py:240
  58.3 8.0 %collective-permute-done.14.refs_1_ = f32[1,192,256]{2,1,0:T(8,128)S(1)} collective-permute-done((f32[1,192,256]{2,1,0:T(8,128)S(1)}, f32[1,192,256]{2,1,0:T(8,128)S(1)}, u32[]{:S(2)}, u32[]{:S(2)}) %collective-permute-start.14) | collective-permute-done | bytes 196640 | tf_op jit(solution)/shard_map/ppermute | solution.py:240
  66.2 0.7 %panel_grad.1 = (f32[192,256]{1,0:T(8,128)}, bf16[2,256,256]{2,1,0:T(8,128)(2,1)S(1)}) custom-call(f32[1,192,256]{2,1,0:T(8,128)S(1)} %get-tuple-element.29.refs_0_, f32[1,192,256]{2,1,0:T(8,128)S(1)} %collective-permute-done.14.refs_1_, bf16[2,256,256]{2,1,0:T(8,128)(2,1)S(1)} %get-tuple-element.28.refs_3_.refs_2_), custom_call_target="tpu_custom_call" | custom-call | flops 1000 | bytes 1000 | tf_op jit(solution)/shard_map/panel_grad/pallas_call | solution.py:211
  66.9 0.2 all-to-all-done.1
  67.2 1.1 %diag_grad.1 = f32[256,256]{1,0:T(8,128)} custom-call(f32[256,256]{1,0:T(8,128)S(1)} %bitcast.4, bf16[2,256,256]{2,1,0:T(8,128)(2,1)S(1)} %get-tuple-element.35.refs_1_), custom_call_target="tpu_custom_call" | custom-call | flops 1000 | bytes 1000 | tf_op jit(solution)/shard_map/diag_grad/pallas_call | solution.py:211
  (2 shorter events, 0.1 us)
Async XLA Ops:
  0.6 11.1 %collective-permute-start.1 = (f32[192,256]{1,0:T(8,128)}, f32[192,256]{1,0:T(8,128)S(1)}, u32[]{:S(2)}, u32[]{:S(2)}) collective-permute-start(f32[192,256]{1,0:T(8,128)} %refs_3_.1), channel_id=1, source_target_pairs={{0,24},{1,25},{2,26},{3,27},{4,28},{5,29},{6,30},{7,31},{8,16},{9,... | collective-permute-start | bytes 589832 | tf_op jit(solution)/shard_map/ppermute | solution.py:240
  5.7 9.0 %collective-permute-start.2 = (f32[192,256]{1,0:T(8,128)}, f32[192,256]{1,0:T(8,128)S(1)}, u32[]{:S(2)}, u32[]{:S(2)}) collective-permute-start(f32[192,256]{1,0:T(8,128)} %refs_3_.1), channel_id=1, source_target_pairs={{0,2},{1,3},{2,0},{3,1},{4,6},{5,7},{6,4},{7,5},{8,10},{9,11},{10,... | collective-permute-start | bytes 589832 | tf_op jit(solution)/shard_map/ppermute | solution.py:240
  7.2 8.3 %collective-permute-start = (f32[192,256]{1,0:T(8,128)}, f32[192,256]{1,0:T(8,128)S(1)}, u32[]{:S(2)}, u32[]{:S(2)}) collective-permute-start(f32[192,256]{1,0:T(8,128)} %refs_3_.1), channel_id=1, source_target_pairs={{0,8},{1,9},{2,10},{3,11},{4,12},{5,13},{6,14},{7,15},{8,0},{9,1},... | collective-permute-start | bytes 589832 | tf_op jit(solution)/shard_map/ppermute | solution.py:240
  11.7 7.7 %collective-permute-start.6 = (f32[192,256]{1,0:T(8,128)S(1)}, f32[192,256]{1,0:T(8,128)S(1)}, u32[]{:S(2)}, u32[]{:S(2)}) collective-permute-start(f32[192,256]{1,0:T(8,128)S(1)} %collective-permute-done.1.refs_1_), channel_id=1, source_target_pairs={{0,8},{1,9},{2,10},{3,11},{4,12},{5,13},{6,14},{7,15},{8,0},{9,1},... | collective-permute-start | bytes 589832 | tf_op jit(solution)/shard_map/ppermute | solution.py:240
  14.8 7.1 %collective-permute-start.10 = (f32[192,256]{1,0:T(8,128)}, f32[192,256]{1,0:T(8,128)S(1)}, u32[]{:S(2)}, u32[]{:S(2)}) collective-permute-start(f32[192,256]{1,0:T(8,128)} %refs_3_.1), channel_id=1, source_target_pairs={{0,1},{1,0},{2,3},{3,2},{4,5},{5,4},{6,7},{7,6},{8,9},{9,8},{10,11... | collective-permute-start | bytes 589832 | tf_op jit(solution)/shard_map/ppermute | solution.py:240
  14.8 8.6 %collective-permute-start.11 = (f32[192,256]{1,0:T(8,128)S(1)}, f32[192,256]{1,0:T(8,128)S(1)}, u32[]{:S(2)}, u32[]{:S(2)}) collective-permute-start(f32[192,256]{1,0:T(8,128)S(1)} %collective-permute-done.2.refs_2_.refs_0_), channel_id=1, source_target_pairs={{0,1},{1,0},{2,3},{3,2},{4,5},{5,4},{6,7},{7,6},{8,9},{9,8},{10,11... | collective-permute-start | bytes 589832 | tf_op jit(solution)/shard_map/ppermute | solution.py:240
  15.5 8.8 %collective-permute-start.5 = (f32[192,256]{1,0:T(8,128)S(1)}, f32[192,256]{1,0:T(8,128)S(1)}, u32[]{:S(2)}, u32[]{:S(2)}) collective-permute-start(f32[192,256]{1,0:T(8,128)S(1)} %get-tuple-element.20), channel_id=1, source_target_pairs={{0,6},{1,7},{2,4},{3,5},{4,2},{5,3},{6,0},{7,1},{8,14},{9,15},{10,... | collective-permute-start | bytes 589832 | tf_op jit(solution)/shard_map/ppermute | solution.py:240
  17.8 11.1 %collective-permute-start.3 = (f32[192,256]{1,0:T(8,128)S(1)}, f32[192,256]{1,0:T(8,128)S(1)}, u32[]{:S(2)}, u32[]{:S(2)}) collective-permute-start(f32[192,256]{1,0:T(8,128)S(1)} %get-tuple-element.20), channel_id=1, source_target_pairs={{0,2},{1,3},{2,0},{3,1},{4,6},{5,7},{6,4},{7,5},{8,10},{9,11},{10,... | collective-permute-start | bytes 589832 | tf_op jit(solution)/shard_map/ppermute | solution.py:240
  19.4 9.6 %collective-permute-start.4 = (f32[192,256]{1,0:T(8,128)S(1)}, f32[192,256]{1,0:T(8,128)S(1)}, u32[]{:S(2)}, u32[]{:S(2)}) collective-permute-start(f32[192,256]{1,0:T(8,128)S(1)} %get-tuple-element.19.refs_0_), channel_id=1, source_target_pairs={{0,4},{1,5},{2,6},{3,7},{4,0},{5,1},{6,2},{7,3},{8,12},{9,13},{10,... | collective-permute-start | bytes 589832 | tf_op jit(solution)/shard_map/ppermute | solution.py:240
  20.9 0.9 %copy-start.1 = (f32[192,256]{1,0:T(8,128)S(1)}, f32[192,256]{1,0:T(8,128)}, u32[]{:S(2)}) copy-start(f32[192,256]{1,0:T(8,128)} %refs_3_.1) | copy-start | bytes 589828
  21.9 9.7 %collective-permute-start.7 = (f32[192,256]{1,0:T(8,128)S(1)}, f32[192,256]{1,0:T(8,128)S(1)}, u32[]{:S(2)}, u32[]{:S(2)}) collective-permute-start(f32[192,256]{1,0:T(8,128)S(1)} %get-tuple-element.22), channel_id=1, source_target_pairs={{0,2},{1,3},{2,0},{3,1},{4,6},{5,7},{6,4},{7,5},{8,10},{9,11},{10,... | collective-permute-start | bytes 589832 | tf_op jit(solution)/shard_map/ppermute | solution.py:240
  23.4 8.2 %collective-permute-start.8 = (f32[192,256]{1,0:T(8,128)S(1)}, f32[192,256]{1,0:T(8,128)S(1)}, u32[]{:S(2)}, u32[]{:S(2)}) collective-permute-start(f32[192,256]{1,0:T(8,128)S(1)} %get-tuple-element.21.refs_9_.refs_4_), channel_id=1, source_target_pairs={{0,4},{1,5},{2,6},{3,7},{4,0},{5,1},{6,2},{7,3},{8,12},{9,13},{10,... | collective-permute-start | bytes 589832 | tf_op jit(solution)/shard_map/ppermute | solution.py:240
  24.3 7.3 %collective-permute-start.9 = (f32[192,256]{1,0:T(8,128)S(1)}, f32[192,256]{1,0:T(8,128)S(1)}, u32[]{:S(2)}, u32[]{:S(2)}) collective-permute-start(f32[192,256]{1,0:T(8,128)S(1)} %collective-permute-done.5.refs_3_), channel_id=1, source_target_pairs={{0,8},{1,9},{2,10},{3,11},{4,12},{5,13},{6,14},{7,15},{8,0},{9,1},... | collective-permute-start | bytes 589832 | tf_op jit(solution)/shard_map/ppermute | solution.py:240
  31.7 12.4 %copy-start = (f32[192,256]{1,0:T(8,128)S(1)}, f32[192,256]{1,0:T(8,128)}, u32[]{:S(2)}) copy-start(f32[192,256]{1,0:T(8,128)} %refs_2_.1) | copy-start | bytes 589828
  31.7 2.4 %collective-permute-start.12 = (f32[4,192,256]{2,1,0:T(8,128)S(1)}, f32[4,192,256]{2,1,0:T(8,128)S(1)}, u32[]{:S(2)}, u32[]{:S(2)}) collective-permute-start(f32[4,192,256]{2,1,0:T(8,128)S(1)} %pick.1), channel_id=1, source_target_pairs={{0,1},{1,0},{2,3},{3,2},{4,5},{5,4},{6,7},{7,6},{8,9},{9,8},{10,11... | collective-permute-start | bytes 2359304 | tf_op jit(solution)/shard_map/ppermute | solution.py:240
  37.6 15.3 %all-to-all-start = ((f32[32,8,256]{2,1,0:T(8,128)}), f32[32,8,256]{2,1,0:T(8,128)S(1)}, u32[]{:S(2)}, u32[]{:S(2)}) async-start(f32[32,8,256]{2,1,0:T(8,128)} %bitcast), calls=%async_computation | async-start | bytes 524288 | tf_op jit(solution)/shard_map/all_to_all | solution.py:326
  42.3 1.8 %collective-permute-start.13 = (f32[2,192,256]{2,1,0:T(8,128)S(1)}, f32[2,192,256]{2,1,0:T(8,128)S(1)}, u32[]{:S(2)}, u32[]{:S(2)}) collective-permute-start(f32[2,192,256]{2,1,0:T(8,128)S(1)} %get-tuple-element.27), channel_id=1, source_target_pairs={{0,1},{1,0},{2,3},{3,2},{4,5},{5,4},{6,7},{7,6},{8,9},{9,8},{10,11... | collective-permute-start | bytes 1179656 | tf_op jit(solution)/shard_map/ppermute | solution.py:240
  54.0 13.2 %all-to-all-start.1 = ((f32[32,8,256]{2,1,0:T(8,128)}), f32[32,8,256]{2,1,0:T(8,128)S(1)}, u32[]{:S(2)}, u32[]{:S(2)}) async-start(f32[32,8,256]{2,1,0:T(8,128)} %bitcast.2), calls=%async_computation.1 | async-start | bytes 524288 | tf_op jit(solution)/shard_map/all_to_all | solution.py:343
  56.6 9.7 %collective-permute-start.14 = (f32[1,192,256]{2,1,0:T(8,128)S(1)}, f32[1,192,256]{2,1,0:T(8,128)S(1)}, u32[]{:S(2)}, u32[]{:S(2)}) collective-permute-start(f32[1,192,256]{2,1,0:T(8,128)S(1)} %get-tuple-element.30.refs_4_), channel_id=1, source_target_pairs={{0,2},{1,3},{2,0},{3,1},{4,6},{5,7},{6,4},{7,5},{8,10},{9,11},{10,... | collective-permute-start | bytes 589832 | tf_op jit(solution)/shard_map/ppermute | solution.py:240

commit v6 on v5

--- a/solution.py
+++ b/solution.py
@@ -103,50 +103,68 @@
     for i in range(blocks):
         large[i].wait()
         at = pl.ds(i * rows, rows)
-        trail_parts[0, at, :], trail_parts[1, at, :] = parts(landing[at, :])
-
-
-def fill_all(group, cols, pieces, wide):
+        for piece in range(trail.shape[1] // height):
+            high, low = parts(landing[at, piece * height : (piece + 1) * height])
+            to = slice(piece // 2 * height, (piece // 2 + 1) * height)
+            trail_parts[0, piece % 2, at, to] = high
+            trail_parts[1, piece % 2, at, to] = low
+
+
+def fill_all(group, cols, core, pieces, wide):
     height = pieces.shape[1]
     plane = lax.axis_index("row") // group
     for y in range(group):
-        for c in range(cols):
-            at = pl.ds((y * cols + c) * height, height)
+        for c in range(core, cols, 2):
+            at = pl.ds((y * cols + c) // 2 * height, height)
             wide[0, at, :], wide[1, at, :] = parts(pieces[y * cols + (plane ^ c)])
 
 
-def fill_sets(first, second, came, wide):
-    height = came.shape[1]
-    place = lax.axis_index("row") % 2 * 4 + lax.axis_index("col")
-
-    def put(source, value):
-        at = pl.ds(pl.multiple_of(source * height, height), height)
-        wide[0, at, :], wide[1, at, :] = parts(value)
-
-    @pl.when(needs_first())
-    def _():
-        for i, ref in enumerate(first):
-            put(place ^ (2 * i), ref[...])
-
-    @pl.when(jnp.logical_not(needs_first()))
-    def _():
-        for i, ref in enumerate(second):
-            put(place ^ (2 * i), ref[...])
-
-    for i in range(came.shape[0]):
-        put(place ^ (2 * i) ^ 1, came[i])
-
-
-def product_kernel(group, cols, count, *refs):
-    pieces, (rowt, start, trail, keep, send, gram_t, wide, split, image) = refs[:count], refs[count:]
-    if count == 1:
-        fill_all(group, cols, pieces[0], wide)
+def fill_four(pieces, wide):
+    place = lax.axis_index("row") % 2 * 2 + lax.axis_index("col") // 2
+    for i, piece in enumerate(pieces):
+        height = piece.shape[0]
+        at = pl.ds(pl.multiple_of((place ^ i) * height, height), height)
+        wide[0, at, :], wide[1, at, :] = parts(piece[...])
+
+
+def first_kernel(group, cols, *refs):
+    pieces, (trail, out, wide) = refs[:-3], refs[-3:]
+    core = 0
+    if len(pieces) == 1:
+        fill_all(group, cols, core, pieces[0], wide)
     else:
-        fill_sets(pieces[0:4], pieces[4:8], pieces[8], wide)
+        core = lax.axis_index("col") % 2
+
+        @pl.when(needs_first())
+        def _():
+            fill_four(pieces[:4], wide)
+
+        @pl.when(jnp.logical_not(needs_first()))
+        def _():
+            fill_four(pieces[4:], wide)
+
+    height = out.shape[0] // cols
+    for i in range(cols):
+        at = pl.ds(i * height, height)
+        out[at, :] = dot_three(trail[0, core, at, :], trail[1, core, at, :], wide[0], wide[1])
+
+
+def second_kernel(
+    group, cols, paired,
+    came, before, rowt, start, trail, keep, send, gram_t, wide, split, image,
+):
+    core = 1
+    if paired:
+        core = 1 - lax.axis_index("col") % 2
+        fill_four([came.at[i] for i in range(4)], wide)
+    else:
+        fill_all(group, cols, core, came, wide)
     height = image.shape[0] // cols
     for i in range(cols):
         at = pl.ds(i * height, height)
-        image[at, :] = dot_three(trail[0, at, :], trail[1, at, :], wide[0], wide[1])
+        image[at, :] = before[at, :] + dot_three(
+            trail[0, core, at, :], trail[1, core, at, :], wide[0], wide[1]
+        )
     col = lax.axis_index("col")
     for d in range(cols):
         block = image[pl.ds(pl.multiple_of((d ^ col) * height, height), height), :]
@@ -280,7 +298,7 @@
                 prepare_kernel, blocks, [order.index(d) - 1 for d in range(1, cols)]
             ),
             [bf16(2, size, cols * height), f32(size, size), f32(size, size)]
-            + [bf16(2, size, size)] * 2 + [bf16(2, *trail_adjoint.shape)],
+            + [bf16(2, size, size)] * 2 + [bf16(2, 2, cols * height, width // 2)],
             *row_blocks[1:], *params, name="prepare", after=(chosen,),
             in_specs=[whole(panel.shape)] * (cols - 1) + [pl.BlockSpec(memory_space=pltpu.HBM)] * 6,
             out_specs=[VMEM] * 6,
@@ -296,15 +314,21 @@
                 functools.partial(pick_kernel, 4), [f32(4, height, size)], *args,
                 name="pick", after=(trail,),
             )[0]
-            args = args + [flip(theirs, col=1)]
+            came = flip(theirs, col=1)
         else:
-            args = [lax.all_to_all(chosen, AXES, 0, 0, axis_index_groups=planes, tiled=True)]
+            came = lax.all_to_all(chosen, AXES, 0, 0, axis_index_groups=planes, tiled=True)
+            args = [came]
+        (before,) = call(
+            functools.partial(first_kernel, group, cols), [f32(cols * height, size)],
+            *args, trail, name="product_first", in_specs=[VMEM] * (len(args) + 1),
+            scratch=[pltpu.VMEM((2, width // 2, size), jnp.bfloat16)],
+        )
         keep, send, gram_t = call(
-            functools.partial(product_kernel, group, cols, len(args)),
+            functools.partial(second_kernel, group, cols, paired),
             [f32(cols // 2, height, size)] * 2 + [f32(size, size)],
-            *args, rowt, start, trail, name="product", in_specs=[VMEM] * (len(args) + 3),
+            came, before, rowt, start, trail, name="product_second", in_specs=[VMEM] * 5,
             scratch=[
-                pltpu.VMEM((2, width, size), jnp.bfloat16),
+                pltpu.VMEM((2, width // 2, size), jnp.bfloat16),
                 pltpu.VMEM((2, cols * height, size), jnp.bfloat16),
                 pltpu.VMEM((cols * height, size), jnp.float32),
             ],

time: 68.5 us -> 67.5 us (0.985)
  waiting for transfers between devices: 28.8 us -> 27 us
  Pallas kernels: 9.92 us -> 10.8 us
    ppermute x15, waiting for transfers between devices: 20.2 us -> 18.3 us  [flip(): return lax.ppermute(x, AXES, pairs)]
    pallas_call x9 -> x10, Pallas kernels: 9.92 us -> 10.8 us  [call(): pl.pallas_call(body, grid=(1,), out_shape=out, in_specs=(in_specs or [who...]
  transfers between devices with their start and end apart: 17 -> 17, of which waited for: 10 -> 10; matrix products, arithmetic and copies ran while one was open for 0% -> 0% of each run, Pallas kernels for 6% -> 9%
where the time goes in v6:
time: 67.5 us; the launch traced here: 67.2 us
  starting transfers between devices  27.8 us (41%)
  waiting for transfers between devices  27 us (40%)
  Pallas kernels  10.8 us (16%)
  local copies, waits for them, and re-layouts  0.93 us (1%)
  between operations  0.75 us (1%)
    ppermute x15, starting transfers between devices, flip(): return lax.ppermute(x, AXES, pairs)  20.5 us
    ppermute x15, waiting for transfers between devices, flip(): return lax.ppermute(x, AXES, pairs)  18.3 us
    pallas_call x10, Pallas kernels, call(): pl.pallas_call(body, grid=(1,), out_shape=out, in_specs=(in_specs or [who...  10.8 us
    all_to_all x1, waiting for transfers between devices, on_device(): shares = lax.all_to_all(gram_t, AXES, 0, 0, tiled=True)  8.42 us
    all_to_all x1, starting transfers between devices, on_device(): shares = lax.all_to_all(gram_t, AXES, 0, 0, tiled=True)  4.67 us
    all_to_all x1, starting transfers between devices, on_device(): gathered = lax.all_to_all(left_t, AXES, 0, 0, tiled=True)  2.59 us
  transfers between devices with their start and end apart: 17, of which 10 were waited for; matrix products, arithmetic and copies ran while one was open for 0% of the time, Pallas kernels for 9%

profile of v6, /device:TPU:0, one launch (start us, length us, event | category | flops | bytes accessed | tf_op | source)
XLA Modules:
  0.0 67.2 jit_solution(2353620895501780988)
XLA Ops:
  0.6 5.1 %collective-permute-start.1 = (f32[192,256]{1,0:T(8,128)}, f32[192,256]{1,0:T(8,128)S(1)}, u32[]{:S(2)}, u32[]{:S(2)}) collective-permute-start(f32[192,256]{1,0:T(8,128)} %refs_3_.1), channel_id=1, source_target_pairs={{0,24},{1,25},{2,26},{3,27},{4,28},{5,29},{6,30},{7,31},{8,16},{9,... | collective-permute-start | bytes 589832 | tf_op jit(solution)/shard_map/ppermute | solution.py:258
  5.7 1.5 %collective-permute-start.2 = (f32[192,256]{1,0:T(8,128)}, f32[192,256]{1,0:T(8,128)S(1)}, u32[]{:S(2)}, u32[]{:S(2)}) collective-permute-start(f32[192,256]{1,0:T(8,128)} %refs_3_.1), channel_id=1, source_target_pairs={{0,2},{1,3},{2,0},{3,1},{4,6},{5,7},{6,4},{7,5},{8,10},{9,11},{10,... | collective-permute-start | bytes 589832 | tf_op jit(solution)/shard_map/ppermute | solution.py:258
  7.2 0.0 collective-permute-start
  7.2 4.5 %collective-permute-done.1.refs_1_ = f32[192,256]{1,0:T(8,128)S(1)} collective-permute-done((f32[192,256]{1,0:T(8,128)}, f32[192,256]{1,0:T(8,128)S(1)}, u32[]{:S(2)}, u32[]{:S(2)}) %collective-permute-start.1) | collective-permute-done | bytes 196640 | tf_op jit(solution)/shard_map/ppermute | solution.py:258
  11.7 3.0 %collective-permute-start.6 = (f32[192,256]{1,0:T(8,128)S(1)}, f32[192,256]{1,0:T(8,128)S(1)}, u32[]{:S(2)}, u32[]{:S(2)}) collective-permute-start(f32[192,256]{1,0:T(8,128)S(1)} %collective-permute-done.1.refs_1_), channel_id=1, source_target_pairs={{0,8},{1,9},{2,10},{3,11},{4,12},{5,13},{6,14},{7,15},{8,0},{9,1},... | collective-permute-start | bytes 589832 | tf_op jit(solution)/shard_map/ppermute | solution.py:258
  14.8 0.0 collective-permute-start.10
  14.8 0.0 collective-permute-done.2.refs_2_.refs_0_
  14.8 0.5 collective-permute-start.11
  15.3 0.2 collective-permute-done.refs_0_
  15.5 2.3 %collective-permute-start.5 = (f32[192,256]{1,0:T(8,128)S(1)}, f32[192,256]{1,0:T(8,128)S(1)}, u32[]{:S(2)}, u32[]{:S(2)}) collective-permute-start(f32[192,256]{1,0:T(8,128)S(1)} %get-tuple-element.20), channel_id=1, source_target_pairs={{0,6},{1,7},{2,4},{3,5},{4,2},{5,3},{6,0},{7,1},{8,14},{9,15},{10,... | collective-permute-start | bytes 589832 | tf_op jit(solution)/shard_map/ppermute | solution.py:258
  17.8 0.7 %collective-permute-start.3 = (f32[192,256]{1,0:T(8,128)S(1)}, f32[192,256]{1,0:T(8,128)S(1)}, u32[]{:S(2)}, u32[]{:S(2)}) collective-permute-start(f32[192,256]{1,0:T(8,128)S(1)} %get-tuple-element.20), channel_id=1, source_target_pairs={{0,2},{1,3},{2,0},{3,1},{4,6},{5,7},{6,4},{7,5},{8,10},{9,11},{10,... | collective-permute-start | bytes 589832 | tf_op jit(solution)/shard_map/ppermute | solution.py:258
  18.6 0.8 %collective-permute-done.6.refs_1_ = f32[192,256]{1,0:T(8,128)S(1)} collective-permute-done((f32[192,256]{1,0:T(8,128)S(1)}, f32[192,256]{1,0:T(8,128)S(1)}, u32[]{:S(2)}, u32[]{:S(2)}) %collective-permute-start.6) | collective-permute-done | bytes 196640 | tf_op jit(solution)/shard_map/ppermute | solution.py:258
  19.4 1.5 %collective-permute-start.4 = (f32[192,256]{1,0:T(8,128)S(1)}, f32[192,256]{1,0:T(8,128)S(1)}, u32[]{:S(2)}, u32[]{:S(2)}) collective-permute-start(f32[192,256]{1,0:T(8,128)S(1)} %get-tuple-element.19.refs_0_), channel_id=1, source_target_pairs={{0,4},{1,5},{2,6},{3,7},{4,0},{5,1},{6,2},{7,3},{8,12},{9,13},{10,... | collective-permute-start | bytes 589832 | tf_op jit(solution)/shard_map/ppermute | solution.py:258
  20.9 0.0 copy-start.1
  20.9 0.9 %copy-done.1 = f32[192,256]{1,0:T(8,128)S(1)} copy-done((f32[192,256]{1,0:T(8,128)S(1)}, f32[192,256]{1,0:T(8,128)}, u32[]{:S(2)}) %copy-start.1) | copy-done | bytes 196632
  21.9 0.0 collective-permute-done.10.refs_1_
  21.9 1.6 %collective-permute-start.7 = (f32[192,256]{1,0:T(8,128)S(1)}, f32[192,256]{1,0:T(8,128)S(1)}, u32[]{:S(2)}, u32[]{:S(2)}) collective-permute-start(f32[192,256]{1,0:T(8,128)S(1)} %get-tuple-element.22), channel_id=1, source_target_pairs={{0,2},{1,3},{2,0},{3,1},{4,6},{5,7},{6,4},{7,5},{8,10},{9,11},{10,... | collective-permute-start | bytes 589832 | tf_op jit(solution)/shard_map/ppermute | solution.py:258
  23.4 0.0 collective-permute-done.11.refs_2_
  23.4 0.5 collective-permute-start.8
  23.9 0.4 collective-permute-done.5.refs_3_
  24.3 1.7 %collective-permute-start.9 = (f32[192,256]{1,0:T(8,128)S(1)}, f32[192,256]{1,0:T(8,128)S(1)}, u32[]{:S(2)}, u32[]{:S(2)}) collective-permute-start(f32[192,256]{1,0:T(8,128)S(1)} %collective-permute-done.5.refs_3_), channel_id=1, source_target_pairs={{0,8},{1,9},{2,10},{3,11},{4,12},{5,13},{6,14},{7,15},{8,0},{9,1},... | collective-permute-start | bytes 589832 | tf_op jit(solution)/shard_map/ppermute | solution.py:258
  26.0 3.7 %prepare.1 = (bf16[2,256,768]{2,1,0:T(8,128)(2,1)S(1)}, f32[256,256]{1,0:T(8,128)S(1)}, f32[256,256]{1,0:T(8,128)S(1)}, bf16[2,256,256]{2,1,0:T(8,128)(2,1)S(1)}...) custom-call(f32[192,256]{1,0:T(8,128)S(1)} %collective-permute-done.2.refs_2_.refs_0_, ...), custom_call_target="tpu_custom_call" | custom-call | flops 1000 | bytes 1000 | tf_op jit(solution)/shard_map/prepare/pallas_call | solution.py:229
  29.6 0.0 collective-permute-done.3.refs_1_
  29.6 0.0 collective-permute-done.4.refs_2_
  29.6 2.0 %collective-permute-done.7.refs_5_ = f32[192,256]{1,0:T(8,128)S(1)} collective-permute-done((f32[192,256]{1,0:T(8,128)S(1)}, f32[192,256]{1,0:T(8,128)S(1)}, u32[]{:S(2)}, u32[]{:S(2)}) %collective-permute-start.7) | collective-permute-done | bytes 196640 | tf_op jit(solution)/shard_map/ppermute | solution.py:258
  31.6 0.0 collective-permute-done.8.refs_6_
  31.6 0.0 collective-permute-done.9.refs_7_
  31.6 0.1 pick.1
  31.7 0.1 collective-permute-start.12
  31.8 1.2 %product_first.1.refs_1_ = f32[768,256]{1,0:T(8,128)S(1)} custom-call(f32[192,256]{1,0:T(8,128)S(1)} %get-tuple-element.19.refs_0_, f32[192,256]{1,0:T(8,128)S(1)} %collective-permute-done.3.refs_1_, f32[192,256]{1,0:T(8,128)S(1)} %collective-permute-done.4.refs_2_, f32[192,256]{1,0:T(8,128)S(1)} %collective-permute-done.5.refs_3_, ...), custom_call_target="tpu_custom_call" | custom-call | flops 1000 | bytes 1000 | tf_op jit(solution)/shard_map/product_first/pallas_call | solution.py:229
  33.0 0.0 copy-start
  33.0 1.0 %collective-permute-done.12.refs_0_ = f32[4,192,256]{2,1,0:T(8,128)S(1)} collective-permute-done((f32[4,192,256]{2,1,0:T(8,128)S(1)}, f32[4,192,256]{2,1,0:T(8,128)S(1)}, u32[]{:S(2)}, u32[]{:S(2)}) %collective-permute-start.12) | collective-permute-done | bytes 786464 | tf_op jit(solution)/shard_map/ppermute | solution.py:258
  34.0 2.6 %product_second.1 = (f32[2,192,256]{2,1,0:T(8,128)S(1)}, f32[2,192,256]{2,1,0:T(8,128)S(1)}, f32[256,256]{1,0:T(8,128)}) custom-call(f32[4,192,256]{2,1,0:T(8,128)S(1)} %collective-permute-done.12.refs_0_, f32[768,256]{1,0:T(8,128)S(1)} %product_first.1.refs_1_, bf16[2,256,768]{2,1,0:T(8,128)(2,1)S(1)} %get-tuple-element.24.refs_2_, ...), custom_call_target="tpu_custom_call" | custom-call | flops 1000 | bytes 1000 | tf_op jit(solution)/shard_map/product_second/pallas_call | solution.py:229
  36.6 4.7 %all-to-all-start = ((f32[32,8,256]{2,1,0:T(8,128)}), f32[32,8,256]{2,1,0:T(8,128)S(1)}, u32[]{:S(2)}, u32[]{:S(2)}) async-start(f32[32,8,256]{2,1,0:T(8,128)} %bitcast), calls=%async_computation | async-start | bytes 524288 | tf_op jit(solution)/shard_map/all_to_all | solution.py:350
  41.3 0.3 collective-permute-start.13
  41.6 1.5 %collective-permute-done.13.refs_1_ = f32[2,192,256]{2,1,0:T(8,128)S(1)} collective-permute-done((f32[2,192,256]{2,1,0:T(8,128)S(1)}, f32[2,192,256]{2,1,0:T(8,128)S(1)}, u32[]{:S(2)}, u32[]{:S(2)}) %collective-permute-start.13) | collective-permute-done | bytes 393248 | tf_op jit(solution)/shard_map/ppermute | solution.py:258
  43.1 0.0 copy-done
  43.1 0.4 add.1
  43.5 8.4 %all-to-all-done = f32[32,8,256]{2,1,0:T(8,128)S(1)} async-done(((f32[32,8,256]{2,1,0:T(8,128)}), f32[32,8,256]{2,1,0:T(8,128)S(1)}, u32[]{:S(2)}, u32[]{:S(2)}) %all-to-all-start) | async-done | bytes 262176 | tf_op jit(solution)/shard_map/all_to_all | solution.py:350
  51.9 1.1 %middle.1 = f32[256,256]{1,0:T(8,128)} custom-call(f32[256,256]{1,0:T(8,128)S(1)} %bitcast.5, f32[256,256]{1,0:T(8,128)S(1)} %get-tuple-element.33.refs_1_, bf16[2,256,256]{2,1,0:T(8,128)(2,1)S(1)} %get-tuple-element.34.refs_2_, bf16[2,256,256]{2,1,0:T(8,128)(2,1)S(1)} %get-tuple-element.28.refs_3_.refs_2_, f32[1,192,256]{2,1,0:T(8,128)S(1)} %get-tuple-element.30.refs_4_), custom_call_target="tpu_custom_call" | custom-call | flops 1000 | bytes 1000 | tf_op jit(solution)/shard_map/middle/pallas_call | solution.py:229
  53.0 2.6 %all-to-all-start.1 = ((f32[32,8,256]{2,1,0:T(8,128)}), f32[32,8,256]{2,1,0:T(8,128)S(1)}, u32[]{:S(2)}, u32[]{:S(2)}) async-start(f32[32,8,256]{2,1,0:T(8,128)} %bitcast.2), calls=%async_computation.1 | async-start | bytes 524288 | tf_op jit(solution)/shard_map/all_to_all | solution.py:367
  55.6 1.7 %collective-permute-start.14 = (f32[1,192,256]{2,1,0:T(8,128)S(1)}, f32[1,192,256]{2,1,0:T(8,128)S(1)}, u32[]{:S(2)}, u32[]{:S(2)}) collective-permute-start(f32[1,192,256]{2,1,0:T(8,128)S(1)} %get-tuple-element.30.refs_4_), channel_id=1, source_target_pairs={{0,2},{1,3},{2,0},{3,1},{4,6},{5,7},{6,4},{7,5},{8,10},{9,11},{10,... | collective-permute-start | bytes 589832 | tf_op jit(solution)/shard_map/ppermute | solution.py:258
  57.3 8.0 %collective-permute-done.14.refs_1_ = f32[1,192,256]{2,1,0:T(8,128)S(1)} collective-permute-done((f32[1,192,256]{2,1,0:T(8,128)S(1)}, f32[1,192,256]{2,1,0:T(8,128)S(1)}, u32[]{:S(2)}, u32[]{:S(2)}) %collective-permute-start.14) | collective-permute-done | bytes 196640 | tf_op jit(solution)/shard_map/ppermute | solution.py:258
  65.2 0.7 %panel_grad.1 = (f32[192,256]{1,0:T(8,128)}, bf16[2,256,256]{2,1,0:T(8,128)(2,1)S(1)}) custom-call(f32[1,192,256]{2,1,0:T(8,128)S(1)} %get-tuple-element.29.refs_0_, f32[1,192,256]{2,1,0:T(8,128)S(1)} %collective-permute-done.14.refs_1_, bf16[2,256,256]{2,1,0:T(8,128)(2,1)S(1)} %get-tuple-element.28.refs_3_.refs_2_), custom_call_target="tpu_custom_call" | custom-call | flops 1000 | bytes 1000 | tf_op jit(solution)/shard_map/panel_grad/pallas_call | solution.py:229
  65.9 0.2 all-to-all-done.1
  66.2 1.1 %diag_grad.1 = f32[256,256]{1,0:T(8,128)} custom-call(f32[256,256]{1,0:T(8,128)S(1)} %bitcast.4, bf16[2,256,256]{2,1,0:T(8,128)(2,1)S(1)} %get-tuple-element.35.refs_1_), custom_call_target="tpu_custom_call" | custom-call | flops 1000 | bytes 1000 | tf_op jit(solution)/shard_map/diag_grad/pallas_call | solution.py:229
  (2 shorter events, 0.1 us)
Async XLA Ops:
  0.6 11.1 %collective-permute-start.1 = (f32[192,256]{1,0:T(8,128)}, f32[192,256]{1,0:T(8,128)S(1)}, u32[]{:S(2)}, u32[]{:S(2)}) collective-permute-start(f32[192,256]{1,0:T(8,128)} %refs_3_.1), channel_id=1, source_target_pairs={{0,24},{1,25},{2,26},{3,27},{4,28},{5,29},{6,30},{7,31},{8,16},{9,... | collective-permute-start | bytes 589832 | tf_op jit(solution)/shard_map/ppermute | solution.py:258
  5.7 9.0 %collective-permute-start.2 = (f32[192,256]{1,0:T(8,128)}, f32[192,256]{1,0:T(8,128)S(1)}, u32[]{:S(2)}, u32[]{:S(2)}) collective-permute-start(f32[192,256]{1,0:T(8,128)} %refs_3_.1), channel_id=1, source_target_pairs={{0,2},{1,3},{2,0},{3,1},{4,6},{5,7},{6,4},{7,5},{8,10},{9,11},{10,... | collective-permute-start | bytes 589832 | tf_op jit(solution)/shard_map/ppermute | solution.py:258
  7.2 8.3 %collective-permute-start = (f32[192,256]{1,0:T(8,128)}, f32[192,256]{1,0:T(8,128)S(1)}, u32[]{:S(2)}, u32[]{:S(2)}) collective-permute-start(f32[192,256]{1,0:T(8,128)} %refs_3_.1), channel_id=1, source_target_pairs={{0,8},{1,9},{2,10},{3,11},{4,12},{5,13},{6,14},{7,15},{8,0},{9,1},... | collective-permute-start | bytes 589832 | tf_op jit(solution)/shard_map/ppermute | solution.py:258
  11.7 7.7 %collective-permute-start.6 = (f32[192,256]{1,0:T(8,128)S(1)}, f32[192,256]{1,0:T(8,128)S(1)}, u32[]{:S(2)}, u32[]{:S(2)}) collective-permute-start(f32[192,256]{1,0:T(8,128)S(1)} %collective-permute-done.1.refs_1_), channel_id=1, source_target_pairs={{0,8},{1,9},{2,10},{3,11},{4,12},{5,13},{6,14},{7,15},{8,0},{9,1},... | collective-permute-start | bytes 589832 | tf_op jit(solution)/shard_map/ppermute | solution.py:258
  14.8 7.1 %collective-permute-start.10 = (f32[192,256]{1,0:T(8,128)}, f32[192,256]{1,0:T(8,128)S(1)}, u32[]{:S(2)}, u32[]{:S(2)}) collective-permute-start(f32[192,256]{1,0:T(8,128)} %refs_3_.1), channel_id=1, source_target_pairs={{0,1},{1,0},{2,3},{3,2},{4,5},{5,4},{6,7},{7,6},{8,9},{9,8},{10,11... | collective-permute-start | bytes 589832 | tf_op jit(solution)/shard_map/ppermute | solution.py:258
  14.8 8.6 %collective-permute-start.11 = (f32[192,256]{1,0:T(8,128)S(1)}, f32[192,256]{1,0:T(8,128)S(1)}, u32[]{:S(2)}, u32[]{:S(2)}) collective-permute-start(f32[192,256]{1,0:T(8,128)S(1)} %collective-permute-done.2.refs_2_.refs_0_), channel_id=1, source_target_pairs={{0,1},{1,0},{2,3},{3,2},{4,5},{5,4},{6,7},{7,6},{8,9},{9,8},{10,11... | collective-permute-start | bytes 589832 | tf_op jit(solution)/shard_map/ppermute | solution.py:258
  15.5 8.8 %collective-permute-start.5 = (f32[192,256]{1,0:T(8,128)S(1)}, f32[192,256]{1,0:T(8,128)S(1)}, u32[]{:S(2)}, u32[]{:S(2)}) collective-permute-start(f32[192,256]{1,0:T(8,128)S(1)} %get-tuple-element.20), channel_id=1, source_target_pairs={{0,6},{1,7},{2,4},{3,5},{4,2},{5,3},{6,0},{7,1},{8,14},{9,15},{10,... | collective-permute-start | bytes 589832 | tf_op jit(solution)/shard_map/ppermute | solution.py:258
  17.8 11.8 %collective-permute-start.3 = (f32[192,256]{1,0:T(8,128)S(1)}, f32[192,256]{1,0:T(8,128)S(1)}, u32[]{:S(2)}, u32[]{:S(2)}) collective-permute-start(f32[192,256]{1,0:T(8,128)S(1)} %get-tuple-element.20), channel_id=1, source_target_pairs={{0,2},{1,3},{2,0},{3,1},{4,6},{5,7},{6,4},{7,5},{8,10},{9,11},{10,... | collective-permute-start | bytes 589832 | tf_op jit(solution)/shard_map/ppermute | solution.py:258
  19.4 10.2 %collective-permute-start.4 = (f32[192,256]{1,0:T(8,128)S(1)}, f32[192,256]{1,0:T(8,128)S(1)}, u32[]{:S(2)}, u32[]{:S(2)}) collective-permute-start(f32[192,256]{1,0:T(8,128)S(1)} %get-tuple-element.19.refs_0_), channel_id=1, source_target_pairs={{0,4},{1,5},{2,6},{3,7},{4,0},{5,1},{6,2},{7,3},{8,12},{9,13},{10,... | collective-permute-start | bytes 589832 | tf_op jit(solution)/shard_map/ppermute | solution.py:258
  20.9 0.9 %copy-start.1 = (f32[192,256]{1,0:T(8,128)S(1)}, f32[192,256]{1,0:T(8,128)}, u32[]{:S(2)}) copy-start(f32[192,256]{1,0:T(8,128)} %refs_3_.1) | copy-start | bytes 589828
  21.9 9.7 %collective-permute-start.7 = (f32[192,256]{1,0:T(8,128)S(1)}, f32[192,256]{1,0:T(8,128)S(1)}, u32[]{:S(2)}, u32[]{:S(2)}) collective-permute-start(f32[192,256]{1,0:T(8,128)S(1)} %get-tuple-element.22), channel_id=1, source_target_pairs={{0,2},{1,3},{2,0},{3,1},{4,6},{5,7},{6,4},{7,5},{8,10},{9,11},{10,... | collective-permute-start | bytes 589832 | tf_op jit(solution)/shard_map/ppermute | solution.py:258
  23.4 8.2 %collective-permute-start.8 = (f32[192,256]{1,0:T(8,128)S(1)}, f32[192,256]{1,0:T(8,128)S(1)}, u32[]{:S(2)}, u32[]{:S(2)}) collective-permute-start(f32[192,256]{1,0:T(8,128)S(1)} %get-tuple-element.21.refs_9_.refs_4_), channel_id=1, source_target_pairs={{0,4},{1,5},{2,6},{3,7},{4,0},{5,1},{6,2},{7,3},{8,12},{9,13},{10,... | collective-permute-start | bytes 589832 | tf_op jit(solution)/shard_map/ppermute | solution.py:258
  24.3 7.3 %collective-permute-start.9 = (f32[192,256]{1,0:T(8,128)S(1)}, f32[192,256]{1,0:T(8,128)S(1)}, u32[]{:S(2)}, u32[]{:S(2)}) collective-permute-start(f32[192,256]{1,0:T(8,128)S(1)} %collective-permute-done.5.refs_3_), channel_id=1, source_target_pairs={{0,8},{1,9},{2,10},{3,11},{4,12},{5,13},{6,14},{7,15},{8,0},{9,1},... | collective-permute-start | bytes 589832 | tf_op jit(solution)/shard_map/ppermute | solution.py:258
  31.7 2.4 %collective-permute-start.12 = (f32[4,192,256]{2,1,0:T(8,128)S(1)}, f32[4,192,256]{2,1,0:T(8,128)S(1)}, u32[]{:S(2)}, u32[]{:S(2)}) collective-permute-start(f32[4,192,256]{2,1,0:T(8,128)S(1)} %pick.1), channel_id=1, source_target_pairs={{0,1},{1,0},{2,3},{3,2},{4,5},{5,4},{6,7},{7,6},{8,9},{9,8},{10,11... | collective-permute-start | bytes 2359304 | tf_op jit(solution)/shard_map/ppermute | solution.py:258
  33.0 10.1 %copy-start = (f32[192,256]{1,0:T(8,128)S(1)}, f32[192,256]{1,0:T(8,128)}, u32[]{:S(2)}) copy-start(f32[192,256]{1,0:T(8,128)} %refs_2_.1) | copy-start | bytes 589828
  36.6 15.3 %all-to-all-start = ((f32[32,8,256]{2,1,0:T(8,128)}), f32[32,8,256]{2,1,0:T(8,128)S(1)}, u32[]{:S(2)}, u32[]{:S(2)}) async-start(f32[32,8,256]{2,1,0:T(8,128)} %bitcast), calls=%async_computation | async-start | bytes 524288 | tf_op jit(solution)/shard_map/all_to_all | solution.py:350
  41.3 1.8 %collective-permute-start.13 = (f32[2,192,256]{2,1,0:T(8,128)S(1)}, f32[2,192,256]{2,1,0:T(8,128)S(1)}, u32[]{:S(2)}, u32[]{:S(2)}) collective-permute-start(f32[2,192,256]{2,1,0:T(8,128)S(1)} %get-tuple-element.27), channel_id=1, source_target_pairs={{0,1},{1,0},{2,3},{3,2},{4,5},{5,4},{6,7},{7,6},{8,9},{9,8},{10,11... | collective-permute-start | bytes 1179656 | tf_op jit(solution)/shard_map/ppermute | solution.py:258
  53.0 13.2 %all-to-all-start.1 = ((f32[32,8,256]{2,1,0:T(8,128)}), f32[32,8,256]{2,1,0:T(8,128)S(1)}, u32[]{:S(2)}, u32[]{:S(2)}) async-start(f32[32,8,256]{2,1,0:T(8,128)} %bitcast.2), calls=%async_computation.1 | async-start | bytes 524288 | tf_op jit(solution)/shard_map/all_to_all | solution.py:367
  55.6 9.7 %collective-permute-start.14 = (f32[1,192,256]{2,1,0:T(8,128)S(1)}, f32[1,192,256]{2,1,0:T(8,128)S(1)}, u32[]{:S(2)}, u32[]{:S(2)}) collective-permute-start(f32[1,192,256]{2,1,0:T(8,128)S(1)} %get-tuple-element.30.refs_4_), channel_id=1, source_target_pairs={{0,2},{1,3},{2,0},{3,1},{4,6},{5,7},{6,4},{7,5},{8,10},{9,11},{10,... | collective-permute-start | bytes 589832 | tf_op jit(solution)/shard_map/ppermute | solution.py:258

commit v7 on v6

--- a/solution.py
+++ b/solution.py
@@ -74,13 +74,12 @@
 
 def prepare_kernel(blocks, places, *refs):
     rows_of, refs = refs[: len(places)], refs[len(places) :]
-    panel, adjoint, factor, inverse, corner, trail = refs[:6]
-    rowt, start, base, unit, inv, trail_parts = refs[6:12]
-    landing, here, sems = refs[12], refs[13:-1], refs[-1]
+    panel, adjoint, trail, start, trail_parts, reduced, landing, panel_here, adjoint_here = refs[:9]
+    rows_here, sems = refs[9:]
     rows = trail.shape[0] // blocks
     small = [
-        pltpu.make_async_copy(ref, to, sems.at[blocks + i])
-        for i, (ref, to) in enumerate(zip((panel, adjoint, factor, inverse, corner), here))
+        pltpu.make_async_copy(panel, panel_here, sems.at[blocks]),
+        pltpu.make_async_copy(adjoint, adjoint_here, sems.at[blocks + 1]),
     ]
     large = []
     for i in range(blocks):
@@ -90,16 +89,12 @@
         copy.start()
     for copy in small:
         copy.wait()
-    panel, adjoint, factor, inverse, corner = here
     height = adjoint.shape[0]
-    for d, block in enumerate([panel] + [rows_of[i] for i in places]):
-        high, low = parts(block[...].T)
-        rowt[0, :, d * height : (d + 1) * height] = high
-        rowt[1, :, d * height : (d + 1) * height] = low
-    start[...] = dot_t(panel[...], adjoint[...])
-    base[...] = dot_t(corner[...], factor[...])
-    unit[0], unit[1] = parts(dot(inverse[...], factor[...]))
-    inv[0], inv[1] = parts(inverse[...])
+    col = lax.axis_index("col")
+    for d, block in enumerate([panel_here] + [rows_of[i] for i in places]):
+        rows_here[pl.ds(pl.multiple_of((d ^ col) * height, height), height), :] = block[...]
+    row_high, row_low = parts(rows_here[...].T)
+    start[...] = dot_t(panel_here[...], adjoint_here[...])
     for i in range(blocks):
         large[i].wait()
         at = pl.ds(i * rows, rows)
@@ -108,6 +103,16 @@
             to = slice(piece // 2 * height, (piece // 2 + 1) * height)
             trail_parts[0, piece % 2, at, to] = high
             trail_parts[1, piece % 2, at, to] = low
+    for core in range(2):
+        reduced[0, core], reduced[1, core] = parts(
+            dot_three(row_high, row_low, trail_parts[0, core], trail_parts[1, core])
+        )
+
+
+def tail_kernel(factor, inverse, corner, base, unit, inv):
+    base[...] = dot_t(corner[...], factor[...])
+    unit[0], unit[1] = parts(dot(inverse[...], factor[...]))
+    inv[0], inv[1] = parts(inverse[...])
 
 
 def fill_all(group, cols, core, pieces, wide):
@@ -127,13 +132,15 @@
         wide[0, at, :], wide[1, at, :] = parts(piece[...])
 
 
+def own_core(paired):
+    return lax.axis_index("col") % 2 if paired else 0
+
+
 def first_kernel(group, cols, *refs):
-    pieces, (trail, out, wide) = refs[:-3], refs[-3:]
-    core = 0
-    if len(pieces) == 1:
-        fill_all(group, cols, core, pieces[0], wide)
-    else:
-        core = lax.axis_index("col") % 2
+    pieces, (start, trail, reduced, out, gram_t, wide) = refs[:-6], refs[-6:]
+    paired = len(pieces) > 1
+    core = own_core(paired)
+    if paired:
 
         @pl.when(needs_first())
         def _():
@@ -143,22 +150,35 @@
         def _():
             fill_four(pieces[4:], wide)
 
+    else:
+        fill_all(group, cols, core, pieces[0], wide)
+    gram_t[...] = start[...] - 2.0 * dot_three(
+        reduced[0, core], reduced[1, core], wide[0], wide[1]
+    )
     height = out.shape[0] // cols
     for i in range(cols):
         at = pl.ds(i * height, height)
         out[at, :] = dot_three(trail[0, core, at, :], trail[1, core, at, :], wide[0], wide[1])
 
 
-def second_kernel(
-    group, cols, paired,
-    came, before, rowt, start, trail, keep, send, gram_t, wide, split, image,
-):
-    core = 1
+def fill_rest(group, cols, paired, came, wide):
     if paired:
-        core = 1 - lax.axis_index("col") % 2
         fill_four([came.at[i] for i in range(4)], wide)
     else:
-        fill_all(group, cols, core, came, wide)
+        fill_all(group, cols, 1, came, wide)
+
+
+def gram_kernel(group, cols, paired, came, before, reduced, gram_t, wide):
+    core = 1 - own_core(paired)
+    fill_rest(group, cols, paired, came, wide)
+    gram_t[...] = before[...] - 2.0 * dot_three(
+        reduced[0, core], reduced[1, core], wide[0], wide[1]
+    )
+
+
+def image_kernel(group, cols, paired, came, before, trail, keep, send, wide, image):
+    core = 1 - own_core(paired)
+    fill_rest(group, cols, paired, came, wide)
     height = image.shape[0] // cols
     for i in range(cols):
         at = pl.ds(i * height, height)
@@ -168,10 +188,7 @@
     col = lax.axis_index("col")
     for d in range(cols):
         block = image[pl.ds(pl.multiple_of((d ^ col) * height, height), height), :]
-        at = pl.ds(d * height, height)
-        split[0, at, :], split[1, at, :] = parts(block)
         (send if d % 2 else keep)[d // 2] = block
-    gram_t[...] = start[...] - 2.0 * dot_three(rowt[0], rowt[1], split[0], split[1])
 
 
 def middle_kernel(devices, cols, share, shares, base, unit, inv, out):
@@ -230,8 +247,8 @@
         body,
         grid=(1,),
         out_shape=out,
-        in_specs=(in_specs or [whole(x.shape) for x in args]) + [ANY] * len(after),
-        out_specs=out_specs or [whole(x.shape) for x in out],
+        in_specs=(in_specs or [VMEM] * len(args)) + [ANY] * len(after),
+        out_specs=out_specs or [VMEM] * len(out),
         scratch_shapes=list(scratch),
         input_output_aliases=aliases or {},
         compiler_params=pltpu.CompilerParams(vmem_limit_bytes=LIMIT),
@@ -280,7 +297,7 @@
             for near, far in ((1, 3), (0, 2)):
                 own, other = call(
                     choose_kernel, [f32(height, size)] * 2, pieces[near], pieces[far],
-                    name="choose", after=(row_blocks[1],) if near else (),
+                    name="choose", after=(row_blocks[1],) if near else (row_blocks[2], row_blocks[3]),
                 )
                 diagonal = flip(sets[0][3], plane=1) if sets else flip(other, y=1, col=2)
                 sets.append([own, flip(other, col=2), flip(own, y=1), diagonal])
@@ -291,21 +308,19 @@
         blocks = 4
         params = [
             pltpu.with_memory_space_constraint(x, pltpu.HBM)
-            for x in (panel, panel_adjoint, diag_factor, diag_inverse, diag_adjoint, trail_adjoint)
+            for x in (panel, panel_adjoint, trail_adjoint)
         ]
-        rowt, start, base, unit, inv, trail = call(
+        rows, half = cols * height, width // 2
+        start, trail, reduced = call(
             functools.partial(
                 prepare_kernel, blocks, [order.index(d) - 1 for d in range(1, cols)]
             ),
-            [bf16(2, size, cols * height), f32(size, size), f32(size, size)]
-            + [bf16(2, size, size)] * 2 + [bf16(2, 2, cols * height, width // 2)],
+            [f32(size, size), bf16(2, 2, rows, half), bf16(2, 2, size, half)],
             *row_blocks[1:], *params, name="prepare", after=(chosen,),
-            in_specs=[whole(panel.shape)] * (cols - 1) + [pl.BlockSpec(memory_space=pltpu.HBM)] * 6,
-            out_specs=[VMEM] * 6,
+            in_specs=[VMEM] * (cols - 1) + [pl.BlockSpec(memory_space=pltpu.HBM)] * 3,
             scratch=[pltpu.VMEM(trail_adjoint.shape, jnp.float32)]
             + [pltpu.VMEM((height, size), jnp.float32)] * 2
-            + [pltpu.VMEM((size, size), jnp.float32)] * 3
-            + [pltpu.SemaphoreType.DMA((blocks + 5,))],
+            + [pltpu.VMEM((rows, size), jnp.float32), pltpu.SemaphoreType.DMA((blocks + 2,))],
         )
 
         if paired:
@@ -318,20 +333,23 @@
         else:
             came = lax.all_to_all(chosen, AXES, 0, 0, axis_index_groups=planes, tiled=True)
             args = [came]
-        (before,) = call(
-            functools.partial(first_kernel, group, cols), [f32(cols * height, size)],
-            *args, trail, name="product_first", in_specs=[VMEM] * (len(args) + 1),
-            scratch=[pltpu.VMEM((2, width // 2, size), jnp.bfloat16)],
-        )
-        keep, send, gram_t = call(
-            functools.partial(second_kernel, group, cols, paired),
-            [f32(cols // 2, height, size)] * 2 + [f32(size, size)],
-            came, before, rowt, start, trail, name="product_second", in_specs=[VMEM] * 5,
-            scratch=[
-                pltpu.VMEM((2, width // 2, size), jnp.bfloat16),
-                pltpu.VMEM((2, cols * height, size), jnp.bfloat16),
-                pltpu.VMEM((cols * height, size), jnp.float32),
-            ],
+        wide = pltpu.VMEM((2, half, size), jnp.bfloat16)
+        before, gram_t = call(
+            functools.partial(first_kernel, group, cols), [f32(rows, size), f32(size, size)],
+            *args, start, trail, reduced, name="product_first", scratch=[wide],
+        )
+        (gram_t,) = call(
+            functools.partial(gram_kernel, group, cols, paired), [f32(size, size)],
+            came, gram_t, reduced, name="gram", scratch=[wide],
+        )
+        keep, send = call(
+            functools.partial(image_kernel, group, cols, paired),
+            [f32(cols // 2, height, size)] * 2, came, before, trail, name="product_second",
+            scratch=[wide, pltpu.VMEM((rows, size), jnp.float32)], after=(gram_t,),
+        )
+        base, unit, inv = call(
+            tail_kernel, [f32(size, size)] + [bf16(2, size, size)] * 2,
+            diag_factor, diag_inverse, diag_adjoint, name="tail", after=(keep,),
         )
 
         mine, theirs = call(

time: 67.5 us -> 65.5 us (0.970)
  starting transfers between devices: 27.8 us -> 23.5 us
  local copies, waits for them, and re-layouts: 0.93 us -> 3.28 us
  waiting for transfers between devices: 27 us -> 24.8 us
  Pallas kernels: 10.8 us -> 12.8 us
    all_to_all x1, waiting for transfers between devices: 8.42 us -> 4.75 us  [on_device(): shares = lax.all_to_all(gram_t, AXES, 0, 0, tiled=True)]
    unnamed x4 -> x14, local copies, waits for them, and re-layouts: 0.93 us -> 3.28 us
    ppermute x15, starting transfers between devices: 20.5 us -> 18.2 us  [flip(): return lax.ppermute(x, AXES, pairs)]
    pallas_call x10 -> x12, Pallas kernels: 10.8 us -> 12.8 us  [call(): pl.pallas_call(body, grid=(1,), out_shape=out, in_specs=(in_specs or [VME...]
    all_to_all x1, starting transfers between devices: 4.67 us -> 2.72 us  [on_device(): shares = lax.all_to_all(gram_t, AXES, 0, 0, tiled=True)]
    ppermute x15, waiting for transfers between devices: 18.3 us -> 19.8 us  [flip(): return lax.ppermute(x, AXES, pairs)]
  transfers between devices with their start and end apart: 17 -> 17, of which waited for: 10 -> 12; matrix products, arithmetic and copies ran while one was open for 0% -> 0% of each run, Pallas kernels for 9% -> 14%
where the time goes in v7:
time: 65.5 us; the launch traced here: 65.2 us
  waiting for transfers between devices  24.8 us (38%)
  starting transfers between devices  23.5 us (36%)
  Pallas kernels  12.8 us (20%)
  local copies, waits for them, and re-layouts  3.28 us (5%)
  between operations  0.77 us (1%)
    ppermute x15, waiting for transfers between devices, flip(): return lax.ppermute(x, AXES, pairs)  19.8 us
    ppermute x15, starting transfers between devices, flip(): return lax.ppermute(x, AXES, pairs)  18.2 us
    pallas_call x12, Pallas kernels, call(): pl.pallas_call(body, grid=(1,), out_shape=out, in_specs=(in_specs or [VME...  12.8 us
    all_to_all x1, waiting for transfers between devices, on_device(): shares = lax.all_to_all(gram_t, AXES, 0, 0, tiled=True)  4.75 us
    unnamed x14, local copies, waits for them, and re-layouts  3.28 us
    all_to_all x1, starting transfers between devices, on_device(): shares = lax.all_to_all(gram_t, AXES, 0, 0, tiled=True)  2.72 us
    all_to_all x1, starting transfers between devices, on_device(): gathered = lax.all_to_all(left_t, AXES, 0, 0, tiled=True)  2.59 us
  transfers between devices with their start and end apart: 17, of which 12 were waited for; matrix products, arithmetic and copies ran while one was open for 0% of the time, Pallas kernels for 14%

profile of v7, /device:TPU:0, one launch (start us, length us, event | category | flops | bytes accessed | tf_op | source)
XLA Modules:
  0.0 65.2 jit_solution(13010053076265574975)
XLA Ops:
  0.6 3.0 %collective-permute-start.2 = (f32[192,256]{1,0:T(8,128)}, f32[192,256]{1,0:T(8,128)S(1)}, u32[]{:S(2)}, u32[]{:S(2)}) collective-permute-start(f32[192,256]{1,0:T(8,128)} %refs_3_.1), channel_id=1, source_target_pairs={{0,2},{1,3},{2,0},{3,1},{4,6},{5,7},{6,4},{7,5},{8,10},{9,11},{10,... | collective-permute-start | bytes 589832 | tf_op jit(solution)/shard_map/ppermute | solution.py:275
  3.6 3.6 %collective-permute-start.1 = (f32[192,256]{1,0:T(8,128)}, f32[192,256]{1,0:T(8,128)S(1)}, u32[]{:S(2)}, u32[]{:S(2)}) collective-permute-start(f32[192,256]{1,0:T(8,128)} %refs_3_.1), channel_id=1, source_target_pairs={{0,24},{1,25},{2,26},{3,27},{4,28},{5,29},{6,30},{7,31},{8,16},{9,... | collective-permute-start | bytes 589832 | tf_op jit(solution)/shard_map/ppermute | solution.py:275
  7.2 0.0 collective-permute-start
  7.2 0.0 collective-permute-start.7
  7.2 1.5 %collective-permute-done.2.refs_2_.refs_0_ = f32[192,256]{1,0:T(8,128)S(1)} collective-permute-done((f32[192,256]{1,0:T(8,128)}, f32[192,256]{1,0:T(8,128)S(1)}, u32[]{:S(2)}, u32[]{:S(2)}) %collective-permute-start.2) | collective-permute-done | bytes 196640 | tf_op jit(solution)/shard_map/ppermute | solution.py:275
  8.7 0.0 collective-permute-start.8
  8.8 4.7 %collective-permute-done.1.refs_1_ = f32[192,256]{1,0:T(8,128)S(1)} collective-permute-done((f32[192,256]{1,0:T(8,128)}, f32[192,256]{1,0:T(8,128)S(1)}, u32[]{:S(2)}, u32[]{:S(2)}) %collective-permute-start.1) | collective-permute-done | bytes 196640 | tf_op jit(solution)/shard_map/ppermute | solution.py:275
  13.5 2.5 %collective-permute-start.6 = (f32[192,256]{1,0:T(8,128)S(1)}, f32[192,256]{1,0:T(8,128)S(1)}, u32[]{:S(2)}, u32[]{:S(2)}) collective-permute-start(f32[192,256]{1,0:T(8,128)S(1)} %collective-permute-done.1.refs_1_), channel_id=1, source_target_pairs={{0,8},{1,9},{2,10},{3,11},{4,12},{5,13},{6,14},{7,15},{8,0},{9,1},... | collective-permute-start | bytes 589832 | tf_op jit(solution)/shard_map/ppermute | solution.py:275
  16.0 0.5 collective-permute-done.refs_0_
  16.5 1.6 %collective-permute-start.5 = (f32[192,256]{1,0:T(8,128)S(1)}, f32[192,256]{1,0:T(8,128)S(1)}, u32[]{:S(2)}, u32[]{:S(2)}) collective-permute-start(f32[192,256]{1,0:T(8,128)S(1)} %get-tuple-element.21), channel_id=1, source_target_pairs={{0,6},{1,7},{2,4},{3,5},{4,2},{5,3},{6,0},{7,1},{8,14},{9,15},{10,... | collective-permute-start | bytes 589832 | tf_op jit(solution)/shard_map/ppermute | solution.py:275
  18.1 1.5 %collective-permute-start.3 = (f32[192,256]{1,0:T(8,128)S(1)}, f32[192,256]{1,0:T(8,128)S(1)}, u32[]{:S(2)}, u32[]{:S(2)}) collective-permute-start(f32[192,256]{1,0:T(8,128)S(1)} %get-tuple-element.21), channel_id=1, source_target_pairs={{0,2},{1,3},{2,0},{3,1},{4,6},{5,7},{6,4},{7,5},{8,10},{9,11},{10,... | collective-permute-start | bytes 589832 | tf_op jit(solution)/shard_map/ppermute | solution.py:275
  19.6 0.0 collective-permute-done.7.refs_2_.refs_1_
  19.6 0.5 collective-permute-start.4
  20.1 0.0 collective-permute-done.8.refs_3_.refs_2_
  20.1 0.5 collective-permute-done.6.refs_1_
  20.6 0.0 copy-start.3
  20.6 0.9 %copy-done.3 = f32[192,256]{1,0:T(8,128)S(1)} copy-done((f32[192,256]{1,0:T(8,128)S(1)}, f32[192,256]{1,0:T(8,128)}, u32[]{:S(2)}) %copy-start.3) | copy-done | bytes 196632
  21.6 1.6 %collective-permute-start.10 = (f32[192,256]{1,0:T(8,128)S(1)}, f32[192,256]{1,0:T(8,128)S(1)}, u32[]{:S(2)}, u32[]{:S(2)}) collective-permute-start(f32[192,256]{1,0:T(8,128)S(1)} %get-tuple-element.22.refs_6_.refs_4_), channel_id=1, source_target_pairs={{0,4},{1,5},{2,6},{3,7},{4,0},{5,1},{6,2},{7,3},{8,12},{9,13},{10,... | collective-permute-start | bytes 589832 | tf_op jit(solution)/shard_map/ppermute | solution.py:275
  23.2 2.1 %collective-permute-done.5.refs_3_ = f32[192,256]{1,0:T(8,128)S(1)} collective-permute-done((f32[192,256]{1,0:T(8,128)S(1)}, f32[192,256]{1,0:T(8,128)S(1)}, u32[]{:S(2)}, u32[]{:S(2)}) %collective-permute-start.5) | collective-permute-done | bytes 196640 | tf_op jit(solution)/shard_map/ppermute | solution.py:275
  25.3 1.5 %collective-permute-start.11 = (f32[192,256]{1,0:T(8,128)S(1)}, f32[192,256]{1,0:T(8,128)S(1)}, u32[]{:S(2)}, u32[]{:S(2)}) collective-permute-start(f32[192,256]{1,0:T(8,128)S(1)} %collective-permute-done.5.refs_3_), channel_id=1, source_target_pairs={{0,8},{1,9},{2,10},{3,11},{4,12},{5,13},{6,14},{7,15},{8,0},{9,1},... | collective-permute-start | bytes 589832 | tf_op jit(solution)/shard_map/ppermute | solution.py:275
  26.8 0.5 collective-permute-start.9
  27.3 4.6 %prepare.1 = (f32[256,256]{1,0:T(8,128)S(1)}, bf16[2,2,768,768]{3,2,1,0:T(8,128)(2,1)S(1)}, bf16[2,2,256,768]{3,2,1,0:T(8,128)(2,1)S(1)}) custom-call(f32[192,256]{1,0:T(8,128)S(1)} %collective-permute-done.2.refs_2_.refs_0_, f32[192,256]{1,0:T(8,128)S(1)} %collective-permute-done.7.refs_2_.refs_1_, f32[192,256]{1,0:T(8,128)S(1)} %collective-permute-done.8.refs_3_.refs_2_, ...), custom_call_target="tpu_custom_call" | custom-call | flops 1000 | bytes 1000 | tf_op jit(solution)/shard_map/prepare/pallas_call | solution.py:246
  31.9 0.0 copy-start
  31.9 0.0 collective-permute-done.4.refs_2_
  32.0 0.0 collective-permute-done.3.refs_1_
  32.0 0.7 %collective-permute-done.10.refs_6_ = f32[192,256]{1,0:T(8,128)S(1)} collective-permute-done((f32[192,256]{1,0:T(8,128)S(1)}, f32[192,256]{1,0:T(8,128)S(1)}, u32[]{:S(2)}, u32[]{:S(2)}) %collective-permute-start.10) | collective-permute-done | bytes 196640 | tf_op jit(solution)/shard_map/ppermute | solution.py:275
  32.7 0.0 collective-permute-done.11.refs_7_
  32.7 0.1 collective-permute-done.9.refs_5_
  32.8 0.1 pick.1
  32.8 0.1 collective-permute-start.12
  32.9 1.5 %product_first.1 = (f32[768,256]{1,0:T(8,128)S(1)}, f32[256,256]{1,0:T(8,128)S(1)}) custom-call(f32[192,256]{1,0:T(8,128)S(1)} %get-tuple-element.20.refs_0_, f32[192,256]{1,0:T(8,128)S(1)} %collective-permute-done.3.refs_1_, f32[192,256]{1,0:T(8,128)S(1)} %collective-permute-done.4.refs_2_, f32[192,256]{1,0:T(8,128)S(1)} %collective-permute-done.5.refs_3_, ...), custom_call_target="tpu_custom_call" | custom-call | flops 1000 | bytes 1000 | tf_op jit(solution)/shard_map/product_first/pallas_call | solution.py:246
  34.4 0.0 copy-done
  34.4 0.7 %collective-permute-done.12.refs_0_ = f32[4,192,256]{2,1,0:T(8,128)S(1)} collective-permute-done((f32[4,192,256]{2,1,0:T(8,128)S(1)}, f32[4,192,256]{2,1,0:T(8,128)S(1)}, u32[]{:S(2)}, u32[]{:S(2)}) %collective-permute-start.12) | collective-permute-done | bytes 786464 | tf_op jit(solution)/shard_map/ppermute | solution.py:275
  35.2 0.0 copy-start.4
  35.2 0.0 copy-start.5
  35.2 0.0 copy-start.6
  35.2 1.4 %gram.1.refs_3_ = f32[256,256]{1,0:T(8,128)} custom-call(f32[4,192,256]{2,1,0:T(8,128)S(1)} %collective-permute-done.12.refs_0_, f32[256,256]{1,0:T(8,128)S(1)} %get-tuple-element.28.refs_1_, bf16[2,2,256,768]{3,2,1,0:T(8,128)(2,1)S(1)} %get-tuple-element.26.refs_10_.refs_2_), custom_call_target="tpu_custom_call" | custom-call | flops 1000 | bytes 1000 | tf_op jit(solution)/shard_map/gram/pallas_call | solution.py:246
  36.5 0.0 copy-start.2
  36.5 2.7 %all-to-all-start = ((f32[32,8,256]{2,1,0:T(8,128)}), f32[32,8,256]{2,1,0:T(8,128)S(1)}, u32[]{:S(2)}, u32[]{:S(2)}) async-start(f32[32,8,256]{2,1,0:T(8,128)} %bitcast), calls=%async_computation | async-start | bytes 524288 | tf_op jit(solution)/shard_map/all_to_all | solution.py:368
  39.3 0.0 copy-start.1
  39.3 2.3 %copy-done.1 = bf16[2,2,768,768]{3,2,1,0:T(8,128)(2,1)S(1)} copy-done((bf16[2,2,768,768]{3,2,1,0:T(8,128)(2,1)S(1)}, bf16[2,2,768,768]{3,2,1,0:T(8,128)(2,1)}, u32[]{:S(2)}) %copy-start.1) | copy-done | bytes 4718616
  41.6 1.3 %product_second.1 = (f32[2,192,256]{2,1,0:T(8,128)S(1)}, f32[2,192,256]{2,1,0:T(8,128)S(1)}) custom-call(f32[4,192,256]{2,1,0:T(8,128)S(1)} %collective-permute-done.12.refs_0_, f32[768,256]{1,0:T(8,128)S(1)} %get-tuple-element.27.refs_1_, bf16[2,2,768,768]{3,2,1,0:T(8,128)(2,1)S(1)} %copy-done.1, f32[256,256]{1,0:T(8,128)} %gram.1.refs_3_), custom_call_target="tpu_custom_call" | custom-call | flops 1000 | bytes 1000 | tf_op jit(solution)/shard_map/product_second/pallas_call | solution.py:246
  42.9 0.2 collective-permute-start.13
  43.1 0.0 copy-done.4
  43.1 0.0 copy-done.5
  43.1 0.0 copy-done.6
  43.1 0.6 tail.1
  43.8 1.0 %collective-permute-done.13.refs_1_ = f32[2,192,256]{2,1,0:T(8,128)S(1)} collective-permute-done((f32[2,192,256]{2,1,0:T(8,128)S(1)}, f32[2,192,256]{2,1,0:T(8,128)S(1)}, u32[]{:S(2)}, u32[]{:S(2)}) %collective-permute-start.13) | collective-permute-done | bytes 393248 | tf_op jit(solution)/shard_map/ppermute | solution.py:275
  44.7 0.0 copy-done.2
  44.7 0.4 add.1
  45.1 4.7 %all-to-all-done = f32[32,8,256]{2,1,0:T(8,128)S(1)} async-done(((f32[32,8,256]{2,1,0:T(8,128)}), f32[32,8,256]{2,1,0:T(8,128)S(1)}, u32[]{:S(2)}, u32[]{:S(2)}) %all-to-all-start) | async-done | bytes 262176 | tf_op jit(solution)/shard_map/all_to_all | solution.py:368
  49.9 1.1 %middle.1 = f32[256,256]{1,0:T(8,128)} custom-call(f32[256,256]{1,0:T(8,128)S(1)} %bitcast.5, f32[256,256]{1,0:T(8,128)S(1)} %get-tuple-element.35.refs_1_, bf16[2,256,256]{2,1,0:T(8,128)(2,1)S(1)} %get-tuple-element.36.refs_2_, bf16[2,256,256]{2,1,0:T(8,128)(2,1)S(1)} %get-tuple-element.31.refs_3_.refs_2_, f32[1,192,256]{2,1,0:T(8,128)S(1)} %get-tuple-element.33.refs_4_), custom_call_target="tpu_custom_call" | custom-call | flops 1000 | bytes 1000 | tf_op jit(solution)/shard_map/middle/pallas_call | solution.py:246
  50.9 2.6 %all-to-all-start.1 = ((f32[32,8,256]{2,1,0:T(8,128)}), f32[32,8,256]{2,1,0:T(8,128)S(1)}, u32[]{:S(2)}, u32[]{:S(2)}) async-start(f32[32,8,256]{2,1,0:T(8,128)} %bitcast.2), calls=%async_computation.1 | async-start | bytes 524288 | tf_op jit(solution)/shard_map/all_to_all | solution.py:385
  53.5 1.7 %collective-permute-start.14 = (f32[1,192,256]{2,1,0:T(8,128)S(1)}, f32[1,192,256]{2,1,0:T(8,128)S(1)}, u32[]{:S(2)}, u32[]{:S(2)}) collective-permute-start(f32[1,192,256]{2,1,0:T(8,128)S(1)} %get-tuple-element.33.refs_4_), channel_id=1, source_target_pairs={{0,2},{1,3},{2,0},{3,1},{4,6},{5,7},{6,4},{7,5},{8,10},{9,11},{10,... | collective-permute-start | bytes 589832 | tf_op jit(solution)/shard_map/ppermute | solution.py:275
  55.2 8.0 %collective-permute-done.14.refs_1_ = f32[1,192,256]{2,1,0:T(8,128)S(1)} collective-permute-done((f32[1,192,256]{2,1,0:T(8,128)S(1)}, f32[1,192,256]{2,1,0:T(8,128)S(1)}, u32[]{:S(2)}, u32[]{:S(2)}) %collective-permute-start.14) | collective-permute-done | bytes 196640 | tf_op jit(solution)/shard_map/ppermute | solution.py:275
  63.2 0.7 %panel_grad.1 = (f32[192,256]{1,0:T(8,128)}, bf16[2,256,256]{2,1,0:T(8,128)(2,1)S(1)}) custom-call(f32[1,192,256]{2,1,0:T(8,128)S(1)} %get-tuple-element.32.refs_0_, f32[1,192,256]{2,1,0:T(8,128)S(1)} %collective-permute-done.14.refs_1_, bf16[2,256,256]{2,1,0:T(8,128)(2,1)S(1)} %get-tuple-element.31.refs_3_.refs_2_), custom_call_target="tpu_custom_call" | custom-call | flops 1000 | bytes 1000 | tf_op jit(solution)/shard_map/panel_grad/pallas_call | solution.py:246
  63.9 0.2 all-to-all-done.1
  64.1 1.1 %diag_grad.1 = f32[256,256]{1,0:T(8,128)} custom-call(f32[256,256]{1,0:T(8,128)S(1)} %bitcast.4, bf16[2,256,256]{2,1,0:T(8,128)(2,1)S(1)} %get-tuple-element.37.refs_1_), custom_call_target="tpu_custom_call" | custom-call | flops 1000 | bytes 1000 | tf_op jit(solution)/shard_map/diag_grad/pallas_call | solution.py:246
  (2 shorter events, 0.1 us)
Async XLA Ops:
  0.6 8.1 %collective-permute-start.2 = (f32[192,256]{1,0:T(8,128)}, f32[192,256]{1,0:T(8,128)S(1)}, u32[]{:S(2)}, u32[]{:S(2)}) collective-permute-start(f32[192,256]{1,0:T(8,128)} %refs_3_.1), channel_id=1, source_target_pairs={{0,2},{1,3},{2,0},{3,1},{4,6},{5,7},{6,4},{7,5},{8,10},{9,11},{10,... | collective-permute-start | bytes 589832 | tf_op jit(solution)/shard_map/ppermute | solution.py:275
  3.6 9.8 %collective-permute-start.1 = (f32[192,256]{1,0:T(8,128)}, f32[192,256]{1,0:T(8,128)S(1)}, u32[]{:S(2)}, u32[]{:S(2)}) collective-permute-start(f32[192,256]{1,0:T(8,128)} %refs_3_.1), channel_id=1, source_target_pairs={{0,24},{1,25},{2,26},{3,27},{4,28},{5,29},{6,30},{7,31},{8,16},{9,... | collective-permute-start | bytes 589832 | tf_op jit(solution)/shard_map/ppermute | solution.py:275
  7.2 9.3 %collective-permute-start = (f32[192,256]{1,0:T(8,128)}, f32[192,256]{1,0:T(8,128)S(1)}, u32[]{:S(2)}, u32[]{:S(2)}) collective-permute-start(f32[192,256]{1,0:T(8,128)} %refs_3_.1), channel_id=1, source_target_pairs={{0,8},{1,9},{2,10},{3,11},{4,12},{5,13},{6,14},{7,15},{8,0},{9,1},... | collective-permute-start | bytes 589832 | tf_op jit(solution)/shard_map/ppermute | solution.py:275
  7.2 12.4 %collective-permute-start.7 = (f32[192,256]{1,0:T(8,128)}, f32[192,256]{1,0:T(8,128)S(1)}, u32[]{:S(2)}, u32[]{:S(2)}) collective-permute-start(f32[192,256]{1,0:T(8,128)} %refs_3_.1), channel_id=1, source_target_pairs={{0,1},{1,0},{2,3},{3,2},{4,5},{5,4},{6,7},{7,6},{8,9},{9,8},{10,11... | collective-permute-start | bytes 589832 | tf_op jit(solution)/shard_map/ppermute | solution.py:275
  8.7 11.4 %collective-permute-start.8 = (f32[192,256]{1,0:T(8,128)S(1)}, f32[192,256]{1,0:T(8,128)S(1)}, u32[]{:S(2)}, u32[]{:S(2)}) collective-permute-start(f32[192,256]{1,0:T(8,128)S(1)} %collective-permute-done.2.refs_2_.refs_0_), channel_id=1, source_target_pairs={{0,1},{1,0},{2,3},{3,2},{4,5},{5,4},{6,7},{7,6},{8,9},{9,8},{10,11... | collective-permute-start | bytes 589832 | tf_op jit(solution)/shard_map/ppermute | solution.py:275
  13.5 7.2 %collective-permute-start.6 = (f32[192,256]{1,0:T(8,128)S(1)}, f32[192,256]{1,0:T(8,128)S(1)}, u32[]{:S(2)}, u32[]{:S(2)}) collective-permute-start(f32[192,256]{1,0:T(8,128)S(1)} %collective-permute-done.1.refs_1_), channel_id=1, source_target_pairs={{0,8},{1,9},{2,10},{3,11},{4,12},{5,13},{6,14},{7,15},{8,0},{9,1},... | collective-permute-start | bytes 589832 | tf_op jit(solution)/shard_map/ppermute | solution.py:275
  16.5 8.8 %collective-permute-start.5 = (f32[192,256]{1,0:T(8,128)S(1)}, f32[192,256]{1,0:T(8,128)S(1)}, u32[]{:S(2)}, u32[]{:S(2)}) collective-permute-start(f32[192,256]{1,0:T(8,128)S(1)} %get-tuple-element.21), channel_id=1, source_target_pairs={{0,6},{1,7},{2,4},{3,5},{4,2},{5,3},{6,0},{7,1},{8,14},{9,15},{10,... | collective-permute-start | bytes 589832 | tf_op jit(solution)/shard_map/ppermute | solution.py:275
  18.1 13.9 %collective-permute-start.3 = (f32[192,256]{1,0:T(8,128)S(1)}, f32[192,256]{1,0:T(8,128)S(1)}, u32[]{:S(2)}, u32[]{:S(2)}) collective-permute-start(f32[192,256]{1,0:T(8,128)S(1)} %get-tuple-element.21), channel_id=1, source_target_pairs={{0,2},{1,3},{2,0},{3,1},{4,6},{5,7},{6,4},{7,5},{8,10},{9,11},{10,... | collective-permute-start | bytes 589832 | tf_op jit(solution)/shard_map/ppermute | solution.py:275
  19.6 12.4 %collective-permute-start.4 = (f32[192,256]{1,0:T(8,128)S(1)}, f32[192,256]{1,0:T(8,128)S(1)}, u32[]{:S(2)}, u32[]{:S(2)}) collective-permute-start(f32[192,256]{1,0:T(8,128)S(1)} %get-tuple-element.20.refs_0_), channel_id=1, source_target_pairs={{0,4},{1,5},{2,6},{3,7},{4,0},{5,1},{6,2},{7,3},{8,12},{9,13},{10,... | collective-permute-start | bytes 589832 | tf_op jit(solution)/shard_map/ppermute | solution.py:275
  20.6 0.9 %copy-start.3 = (f32[192,256]{1,0:T(8,128)S(1)}, f32[192,256]{1,0:T(8,128)}, u32[]{:S(2)}) copy-start(f32[192,256]{1,0:T(8,128)} %refs_3_.1) | copy-start | bytes 589828
  21.6 11.1 %collective-permute-start.10 = (f32[192,256]{1,0:T(8,128)S(1)}, f32[192,256]{1,0:T(8,128)S(1)}, u32[]{:S(2)}, u32[]{:S(2)}) collective-permute-start(f32[192,256]{1,0:T(8,128)S(1)} %get-tuple-element.22.refs_6_.refs_4_), channel_id=1, source_target_pairs={{0,4},{1,5},{2,6},{3,7},{4,0},{5,1},{6,2},{7,3},{8,12},{9,13},{10,... | collective-permute-start | bytes 589832 | tf_op jit(solution)/shard_map/ppermute | solution.py:275
  25.3 7.4 %collective-permute-start.11 = (f32[192,256]{1,0:T(8,128)S(1)}, f32[192,256]{1,0:T(8,128)S(1)}, u32[]{:S(2)}, u32[]{:S(2)}) collective-permute-start(f32[192,256]{1,0:T(8,128)S(1)} %collective-permute-done.5.refs_3_), channel_id=1, source_target_pairs={{0,8},{1,9},{2,10},{3,11},{4,12},{5,13},{6,14},{7,15},{8,0},{9,1},... | collective-permute-start | bytes 589832 | tf_op jit(solution)/shard_map/ppermute | solution.py:275
  26.8 6.0 %collective-permute-start.9 = (f32[192,256]{1,0:T(8,128)S(1)}, f32[192,256]{1,0:T(8,128)S(1)}, u32[]{:S(2)}, u32[]{:S(2)}) collective-permute-start(f32[192,256]{1,0:T(8,128)S(1)} %get-tuple-element.23), channel_id=1, source_target_pairs={{0,2},{1,3},{2,0},{3,1},{4,6},{5,7},{6,4},{7,5},{8,10},{9,11},{10,... | collective-permute-start | bytes 589832 | tf_op jit(solution)/shard_map/ppermute | solution.py:275
  31.9 2.5 %copy-start = (bf16[2,2,768,768]{3,2,1,0:T(8,128)(2,1)}, bf16[2,2,768,768]{3,2,1,0:T(8,128)(2,1)S(1)}, u32[]{:S(2)}) copy-start(bf16[2,2,768,768]{3,2,1,0:T(8,128)(2,1)S(1)} %get-tuple-element.24.refs_8_.refs_9_.refs_2_) | copy-start | bytes 14155780
  32.8 2.4 %collective-permute-start.12 = (f32[4,192,256]{2,1,0:T(8,128)S(1)}, f32[4,192,256]{2,1,0:T(8,128)S(1)}, u32[]{:S(2)}, u32[]{:S(2)}) collective-permute-start(f32[4,192,256]{2,1,0:T(8,128)S(1)} %pick.1), channel_id=1, source_target_pairs={{0,1},{1,0},{2,3},{3,2},{4,5},{5,4},{6,7},{7,6},{8,9},{9,8},{10,11... | collective-permute-start | bytes 2359304 | tf_op jit(solution)/shard_map/ppermute | solution.py:275
  35.2 7.9 %copy-start.4 = (f32[256,256]{1,0:T(8,128)S(1)}, f32[256,256]{1,0:T(8,128)}, u32[]{:S(2)}) copy-start(f32[256,256]{1,0:T(8,128)} %refs_0_.3) | copy-start | bytes 786436
  35.2 7.9 %copy-start.5 = (f32[256,256]{1,0:T(8,128)S(1)}, f32[256,256]{1,0:T(8,128)}, u32[]{:S(2)}) copy-start(f32[256,256]{1,0:T(8,128)} %refs_1_.1) | copy-start | bytes 786436
  35.2 7.9 %copy-start.6 = (f32[256,256]{1,0:T(8,128)S(1)}, f32[256,256]{1,0:T(8,128)}, u32[]{:S(2)}) copy-start(f32[256,256]{1,0:T(8,128)} %refs_2_.2) | copy-start | bytes 786436
  36.5 8.2 %copy-start.2 = (f32[192,256]{1,0:T(8,128)S(1)}, f32[192,256]{1,0:T(8,128)}, u32[]{:S(2)}) copy-start(f32[192,256]{1,0:T(8,128)} %refs_2_.3) | copy-start | bytes 589828
  36.5 13.3 %all-to-all-start = ((f32[32,8,256]{2,1,0:T(8,128)}), f32[32,8,256]{2,1,0:T(8,128)S(1)}, u32[]{:S(2)}, u32[]{:S(2)}) async-start(f32[32,8,256]{2,1,0:T(8,128)} %bitcast), calls=%async_computation | async-start | bytes 524288 | tf_op jit(solution)/shard_map/all_to_all | solution.py:368
  39.3 2.3 %copy-start.1 = (bf16[2,2,768,768]{3,2,1,0:T(8,128)(2,1)S(1)}, bf16[2,2,768,768]{3,2,1,0:T(8,128)(2,1)}, u32[]{:S(2)}) copy-start(bf16[2,2,768,768]{3,2,1,0:T(8,128)(2,1)} %copy-done) | copy-start | bytes 14155780
  42.9 1.8 %collective-permute-start.13 = (f32[2,192,256]{2,1,0:T(8,128)S(1)}, f32[2,192,256]{2,1,0:T(8,128)S(1)}, u32[]{:S(2)}, u32[]{:S(2)}) collective-permute-start(f32[2,192,256]{2,1,0:T(8,128)S(1)} %get-tuple-element.30), channel_id=1, source_target_pairs={{0,1},{1,0},{2,3},{3,2},{4,5},{5,4},{6,7},{7,6},{8,9},{9,8},{10,11... | collective-permute-start | bytes 1179656 | tf_op jit(solution)/shard_map/ppermute | solution.py:275
  50.9 13.2 %all-to-all-start.1 = ((f32[32,8,256]{2,1,0:T(8,128)}), f32[32,8,256]{2,1,0:T(8,128)S(1)}, u32[]{:S(2)}, u32[]{:S(2)}) async-start(f32[32,8,256]{2,1,0:T(8,128)} %bitcast.2), calls=%async_computation.1 | async-start | bytes 524288 | tf_op jit(solution)/shard_map/all_to_all | solution.py:385
  53.5 9.7 %collective-permute-start.14 = (f32[1,192,256]{2,1,0:T(8,128)S(1)}, f32[1,192,256]{2,1,0:T(8,128)S(1)}, u32[]{:S(2)}, u32[]{:S(2)}) collective-permute-start(f32[1,192,256]{2,1,0:T(8,128)S(1)} %get-tuple-element.33.refs_4_), channel_id=1, source_target_pairs={{0,2},{1,3},{2,0},{3,1},{4,6},{5,7},{6,4},{7,5},{8,10},{9,11},{10,... | collective-permute-start | bytes 589832 | tf_op jit(solution)/shard_map/ppermute | solution.py:275

commit v8 on v7

--- a/solution.py
+++ b/solution.py
@@ -206,11 +206,12 @@
         out[pl.ds(i * share, share), :] = left_t
 
 
-def last_kernel(left_t, inv, out):
+def last_kernel(mine, came, left_t, inv, panel_grad, diag_grad):
+    panel_grad[...] = mine[0] + came[0]
     full = dot_parts(left_t[...].T, inv[0], inv[1])
     at = lax.broadcasted_iota(jnp.int32, full.shape, 0)
     across = lax.broadcasted_iota(jnp.int32, full.shape, 1)
-    out[...] = jnp.where(across < at, full, jnp.where(across == at, 0.5 * full, 0.0))
+    diag_grad[...] = jnp.where(across < at, full, jnp.where(across == at, 0.5 * full, 0.0))
 
 
 def add_kernel(keep, came, adjoint, inv, mine, theirs):
@@ -218,11 +219,6 @@
         own = -2.0 * (keep[2 * i] + came[2 * i])
         mine[i] = dot_parts(own if i else adjoint[...] + own, inv[0], inv[1])
         theirs[i] = dot_parts(-2.0 * (keep[2 * i + 1] + came[2 * i + 1]), inv[0], inv[1])
-
-
-def panel_kernel(mine, came, inv, out, inv_on):
-    inv_on[...] = inv[...]
-    out[...] = mine[0] + came[0]
 
 
 def whole(shape):
@@ -384,10 +380,10 @@
             left_t = jnp.tile(dot(inner_t, diag_inverse), (devices, 1))
         gathered = lax.all_to_all(left_t, AXES, 0, 0, tiled=True)
 
-        panel_grad, inv = call(
-            panel_kernel, [f32(*panel.shape), bf16(*inv.shape)], mine, came, inv, name="panel_grad",
-        )
-        (diag_grad,) = call(last_kernel, [f32(size, size)], gathered, inv, name="diag_grad")
+        panel_grad, diag_grad = call(
+            last_kernel, [f32(*panel.shape), f32(size, size)], mine, came, gathered, inv,
+            name="last",
+        )
         return panel_grad, diag_grad
 
     return on_device

time: 65.5 us -> 65.5 us (level)
  Pallas kernels: 12.8 us -> 12.1 us
  waiting for transfers between devices: 24.8 us -> 25.5 us
    all_to_all x1, waiting for transfers between devices: 0.22 us -> 0.93 us  [on_device(): gathered = lax.all_to_all(left_t, AXES, 0, 0, tiled=True)]
    pallas_call x12 -> x11, Pallas kernels: 12.8 us -> 12.1 us  [call(): pl.pallas_call(body, grid=(1,), out_shape=out, in_specs=(in_specs or [VME...]
  transfers between devices with their start and end apart: 17 -> 17, of which waited for: 12 -> 12; matrix products, arithmetic and copies ran while one was open for 0% -> 0% of each run, Pallas kernels for 14% -> 13%
where the time goes in v8:
time: 65.5 us; the launch traced here: 65.2 us
  waiting for transfers between devices  25.5 us (39%)
  starting transfers between devices  23.5 us (36%)
  Pallas kernels  12.1 us (18%)
  local copies, waits for them, and re-layouts  3.28 us (5%)
  between operations  0.77 us (1%)
    ppermute x15, waiting for transfers between devices, flip(): return lax.ppermute(x, AXES, pairs)  19.8 us
    ppermute x15, starting transfers between devices, flip(): return lax.ppermute(x, AXES, pairs)  18.2 us
    pallas_call x11, Pallas kernels, call(): pl.pallas_call(body, grid=(1,), out_shape=out, in_specs=(in_specs or [VME...  12.1 us
    all_to_all x1, waiting for transfers between devices, on_device(): shares = lax.all_to_all(gram_t, AXES, 0, 0, tiled=True)  4.75 us
    unnamed x14, local copies, waits for them, and re-layouts  3.28 us
    all_to_all x1, starting transfers between devices, on_device(): shares = lax.all_to_all(gram_t, AXES, 0, 0, tiled=True)  2.72 us
    all_to_all x1, starting transfers between devices, on_device(): gathered = lax.all_to_all(left_t, AXES, 0, 0, tiled=True)  2.59 us
  transfers between devices with their start and end apart: 17, of which 12 were waited for; matrix products, arithmetic and copies ran while one was open for 0% of the time, Pallas kernels for 13%

profile of v8, /device:TPU:0, one launch (start us, length us, event | category | flops | bytes accessed | tf_op | source)
XLA Modules:
  0.0 65.2 jit_solution(943752977754454182)
XLA Ops:
  0.6 3.0 %collective-permute-start.2 = (f32[192,256]{1,0:T(8,128)}, f32[192,256]{1,0:T(8,128)S(1)}, u32[]{:S(2)}, u32[]{:S(2)}) collective-permute-start(f32[192,256]{1,0:T(8,128)} %refs_3_.1), channel_id=1, source_target_pairs={{0,2},{1,3},{2,0},{3,1},{4,6},{5,7},{6,4},{7,5},{8,10},{9,11},{10,... | collective-permute-start | bytes 589832 | tf_op jit(solution)/shard_map/ppermute | solution.py:271
  3.6 3.6 %collective-permute-start.1 = (f32[192,256]{1,0:T(8,128)}, f32[192,256]{1,0:T(8,128)S(1)}, u32[]{:S(2)}, u32[]{:S(2)}) collective-permute-start(f32[192,256]{1,0:T(8,128)} %refs_3_.1), channel_id=1, source_target_pairs={{0,24},{1,25},{2,26},{3,27},{4,28},{5,29},{6,30},{7,31},{8,16},{9,... | collective-permute-start | bytes 589832 | tf_op jit(solution)/shard_map/ppermute | solution.py:271
  7.2 0.0 collective-permute-start
  7.2 0.0 collective-permute-start.7
  7.2 1.5 %collective-permute-done.2.refs_2_.refs_0_ = f32[192,256]{1,0:T(8,128)S(1)} collective-permute-done((f32[192,256]{1,0:T(8,128)}, f32[192,256]{1,0:T(8,128)S(1)}, u32[]{:S(2)}, u32[]{:S(2)}) %collective-permute-start.2) | collective-permute-done | bytes 196640 | tf_op jit(solution)/shard_map/ppermute | solution.py:271
  8.7 0.0 collective-permute-start.8
  8.8 4.7 %collective-permute-done.1.refs_1_ = f32[192,256]{1,0:T(8,128)S(1)} collective-permute-done((f32[192,256]{1,0:T(8,128)}, f32[192,256]{1,0:T(8,128)S(1)}, u32[]{:S(2)}, u32[]{:S(2)}) %collective-permute-start.1) | collective-permute-done | bytes 196640 | tf_op jit(solution)/shard_map/ppermute | solution.py:271
  13.5 2.5 %collective-permute-start.6 = (f32[192,256]{1,0:T(8,128)S(1)}, f32[192,256]{1,0:T(8,128)S(1)}, u32[]{:S(2)}, u32[]{:S(2)}) collective-permute-start(f32[192,256]{1,0:T(8,128)S(1)} %collective-permute-done.1.refs_1_), channel_id=1, source_target_pairs={{0,8},{1,9},{2,10},{3,11},{4,12},{5,13},{6,14},{7,15},{8,0},{9,1},... | collective-permute-start | bytes 589832 | tf_op jit(solution)/shard_map/ppermute | solution.py:271
  16.0 0.5 collective-permute-done.refs_0_
  16.5 1.6 %collective-permute-start.5 = (f32[192,256]{1,0:T(8,128)S(1)}, f32[192,256]{1,0:T(8,128)S(1)}, u32[]{:S(2)}, u32[]{:S(2)}) collective-permute-start(f32[192,256]{1,0:T(8,128)S(1)} %get-tuple-element.19), channel_id=1, source_target_pairs={{0,6},{1,7},{2,4},{3,5},{4,2},{5,3},{6,0},{7,1},{8,14},{9,15},{10,... | collective-permute-start | bytes 589832 | tf_op jit(solution)/shard_map/ppermute | solution.py:271
  18.1 1.5 %collective-permute-start.3 = (f32[192,256]{1,0:T(8,128)S(1)}, f32[192,256]{1,0:T(8,128)S(1)}, u32[]{:S(2)}, u32[]{:S(2)}) collective-permute-start(f32[192,256]{1,0:T(8,128)S(1)} %get-tuple-element.19), channel_id=1, source_target_pairs={{0,2},{1,3},{2,0},{3,1},{4,6},{5,7},{6,4},{7,5},{8,10},{9,11},{10,... | collective-permute-start | bytes 589832 | tf_op jit(solution)/shard_map/ppermute | solution.py:271
  19.6 0.0 collective-permute-done.7.refs_2_.refs_1_
  19.6 0.5 collective-permute-start.4
  20.1 0.0 collective-permute-done.8.refs_3_.refs_2_
  20.1 0.5 collective-permute-done.6.refs_1_
  20.6 0.0 copy-start.3
  20.6 0.9 %copy-done.3 = f32[192,256]{1,0:T(8,128)S(1)} copy-done((f32[192,256]{1,0:T(8,128)S(1)}, f32[192,256]{1,0:T(8,128)}, u32[]{:S(2)}) %copy-start.3) | copy-done | bytes 196632
  21.6 1.6 %collective-permute-start.10 = (f32[192,256]{1,0:T(8,128)S(1)}, f32[192,256]{1,0:T(8,128)S(1)}, u32[]{:S(2)}, u32[]{:S(2)}) collective-permute-start(f32[192,256]{1,0:T(8,128)S(1)} %get-tuple-element.20.refs_6_.refs_4_), channel_id=1, source_target_pairs={{0,4},{1,5},{2,6},{3,7},{4,0},{5,1},{6,2},{7,3},{8,12},{9,13},{10,... | collective-permute-start | bytes 589832 | tf_op jit(solution)/shard_map/ppermute | solution.py:271
  23.2 2.1 %collective-permute-done.5.refs_3_ = f32[192,256]{1,0:T(8,128)S(1)} collective-permute-done((f32[192,256]{1,0:T(8,128)S(1)}, f32[192,256]{1,0:T(8,128)S(1)}, u32[]{:S(2)}, u32[]{:S(2)}) %collective-permute-start.5) | collective-permute-done | bytes 196640 | tf_op jit(solution)/shard_map/ppermute | solution.py:271
  25.3 1.5 %collective-permute-start.11 = (f32[192,256]{1,0:T(8,128)S(1)}, f32[192,256]{1,0:T(8,128)S(1)}, u32[]{:S(2)}, u32[]{:S(2)}) collective-permute-start(f32[192,256]{1,0:T(8,128)S(1)} %collective-permute-done.5.refs_3_), channel_id=1, source_target_pairs={{0,8},{1,9},{2,10},{3,11},{4,12},{5,13},{6,14},{7,15},{8,0},{9,1},... | collective-permute-start | bytes 589832 | tf_op jit(solution)/shard_map/ppermute | solution.py:271
  26.8 0.5 collective-permute-start.9
  27.3 4.6 %prepare.1 = (f32[256,256]{1,0:T(8,128)S(1)}, bf16[2,2,768,768]{3,2,1,0:T(8,128)(2,1)S(1)}, bf16[2,2,256,768]{3,2,1,0:T(8,128)(2,1)S(1)}) custom-call(f32[192,256]{1,0:T(8,128)S(1)} %collective-permute-done.2.refs_2_.refs_0_, f32[192,256]{1,0:T(8,128)S(1)} %collective-permute-done.7.refs_2_.refs_1_, f32[192,256]{1,0:T(8,128)S(1)} %collective-permute-done.8.refs_3_.refs_2_, ...), custom_call_target="tpu_custom_call" | custom-call | flops 1000 | bytes 1000 | tf_op jit(solution)/shard_map/prepare/pallas_call | solution.py:242
  31.9 0.0 copy-start
  31.9 0.0 collective-permute-done.4.refs_2_
  32.0 0.0 collective-permute-done.3.refs_1_
  32.0 0.7 %collective-permute-done.10.refs_6_ = f32[192,256]{1,0:T(8,128)S(1)} collective-permute-done((f32[192,256]{1,0:T(8,128)S(1)}, f32[192,256]{1,0:T(8,128)S(1)}, u32[]{:S(2)}, u32[]{:S(2)}) %collective-permute-start.10) | collective-permute-done | bytes 196640 | tf_op jit(solution)/shard_map/ppermute | solution.py:271
  32.7 0.0 collective-permute-done.11.refs_7_
  32.7 0.1 collective-permute-done.9.refs_5_
  32.8 0.1 pick.1
  32.8 0.1 collective-permute-start.12
  32.9 1.5 %product_first.1 = (f32[768,256]{1,0:T(8,128)S(1)}, f32[256,256]{1,0:T(8,128)S(1)}) custom-call(f32[192,256]{1,0:T(8,128)S(1)} %get-tuple-element.18.refs_0_, f32[192,256]{1,0:T(8,128)S(1)} %collective-permute-done.3.refs_1_, f32[192,256]{1,0:T(8,128)S(1)} %collective-permute-done.4.refs_2_, f32[192,256]{1,0:T(8,128)S(1)} %collective-permute-done.5.refs_3_, ...), custom_call_target="tpu_custom_call" | custom-call | flops 1000 | bytes 1000 | tf_op jit(solution)/shard_map/product_first/pallas_call | solution.py:242
  34.4 0.0 copy-done
  34.4 0.7 %collective-permute-done.12.refs_0_ = f32[4,192,256]{2,1,0:T(8,128)S(1)} collective-permute-done((f32[4,192,256]{2,1,0:T(8,128)S(1)}, f32[4,192,256]{2,1,0:T(8,128)S(1)}, u32[]{:S(2)}, u32[]{:S(2)}) %collective-permute-start.12) | collective-permute-done | bytes 786464 | tf_op jit(solution)/shard_map/ppermute | solution.py:271
  35.2 0.0 copy-start.4
  35.2 0.0 copy-start.5
  35.2 0.0 copy-start.6
  35.2 1.4 %gram.1.refs_3_ = f32[256,256]{1,0:T(8,128)} custom-call(f32[4,192,256]{2,1,0:T(8,128)S(1)} %collective-permute-done.12.refs_0_, f32[256,256]{1,0:T(8,128)S(1)} %get-tuple-element.26.refs_1_, bf16[2,2,256,768]{3,2,1,0:T(8,128)(2,1)S(1)} %get-tuple-element.24.refs_10_.refs_2_), custom_call_target="tpu_custom_call" | custom-call | flops 1000 | bytes 1000 | tf_op jit(solution)/shard_map/gram/pallas_call | solution.py:242
  36.5 0.0 copy-start.2
  36.5 2.7 %all-to-all-start = ((f32[32,8,256]{2,1,0:T(8,128)}), f32[32,8,256]{2,1,0:T(8,128)S(1)}, u32[]{:S(2)}, u32[]{:S(2)}) async-start(f32[32,8,256]{2,1,0:T(8,128)} %bitcast), calls=%async_computation | async-start | bytes 524288 | tf_op jit(solution)/shard_map/all_to_all | solution.py:364
  39.3 0.0 copy-start.1
  39.3 2.3 %copy-done.1 = bf16[2,2,768,768]{3,2,1,0:T(8,128)(2,1)S(1)} copy-done((bf16[2,2,768,768]{3,2,1,0:T(8,128)(2,1)S(1)}, bf16[2,2,768,768]{3,2,1,0:T(8,128)(2,1)}, u32[]{:S(2)}) %copy-start.1) | copy-done | bytes 4718616
  41.6 1.3 %product_second.1 = (f32[2,192,256]{2,1,0:T(8,128)S(1)}, f32[2,192,256]{2,1,0:T(8,128)S(1)}) custom-call(f32[4,192,256]{2,1,0:T(8,128)S(1)} %collective-permute-done.12.refs_0_, f32[768,256]{1,0:T(8,128)S(1)} %get-tuple-element.25.refs_1_, bf16[2,2,768,768]{3,2,1,0:T(8,128)(2,1)S(1)} %copy-done.1, f32[256,256]{1,0:T(8,128)} %gram.1.refs_3_), custom_call_target="tpu_custom_call" | custom-call | flops 1000 | bytes 1000 | tf_op jit(solution)/shard_map/product_second/pallas_call | solution.py:242
  42.9 0.2 collective-permute-start.13
  43.1 0.0 copy-done.4
  43.1 0.0 copy-done.5
  43.1 0.0 copy-done.6
  43.1 0.6 tail.1
  43.8 1.0 %collective-permute-done.13.refs_1_ = f32[2,192,256]{2,1,0:T(8,128)S(1)} collective-permute-done((f32[2,192,256]{2,1,0:T(8,128)S(1)}, f32[2,192,256]{2,1,0:T(8,128)S(1)}, u32[]{:S(2)}, u32[]{:S(2)}) %collective-permute-start.13) | collective-permute-done | bytes 393248 | tf_op jit(solution)/shard_map/ppermute | solution.py:271
  44.7 0.0 copy-done.2
  44.7 0.4 add.1
  45.1 4.7 %all-to-all-done = f32[32,8,256]{2,1,0:T(8,128)S(1)} async-done(((f32[32,8,256]{2,1,0:T(8,128)}), f32[32,8,256]{2,1,0:T(8,128)S(1)}, u32[]{:S(2)}, u32[]{:S(2)}) %all-to-all-start) | async-done | bytes 262176 | tf_op jit(solution)/shard_map/all_to_all | solution.py:364
  49.9 1.1 %middle.1 = f32[256,256]{1,0:T(8,128)} custom-call(f32[256,256]{1,0:T(8,128)S(1)} %bitcast.5, f32[256,256]{1,0:T(8,128)S(1)} %get-tuple-element.32.refs_1_, bf16[2,256,256]{2,1,0:T(8,128)(2,1)S(1)} %get-tuple-element.33.refs_2_, bf16[2,256,256]{2,1,0:T(8,128)(2,1)S(1)} %get-tuple-element.29.refs_3_, f32[1,192,256]{2,1,0:T(8,128)S(1)} %get-tuple-element.31.refs_4_), custom_call_target="tpu_custom_call" | custom-call | flops 1000 | bytes 1000 | tf_op jit(solution)/shard_map/middle/pallas_call | solution.py:242
  50.9 2.6 %all-to-all-start.1 = ((f32[32,8,256]{2,1,0:T(8,128)}), f32[32,8,256]{2,1,0:T(8,128)S(1)}, u32[]{:S(2)}, u32[]{:S(2)}) async-start(f32[32,8,256]{2,1,0:T(8,128)} %bitcast.2), calls=%async_computation.1 | async-start | bytes 524288 | tf_op jit(solution)/shard_map/all_to_all | solution.py:381
  53.5 1.7 %collective-permute-start.14 = (f32[1,192,256]{2,1,0:T(8,128)S(1)}, f32[1,192,256]{2,1,0:T(8,128)S(1)}, u32[]{:S(2)}, u32[]{:S(2)}) collective-permute-start(f32[1,192,256]{2,1,0:T(8,128)S(1)} %get-tuple-element.31.refs_4_), channel_id=1, source_target_pairs={{0,2},{1,3},{2,0},{3,1},{4,6},{5,7},{6,4},{7,5},{8,10},{9,11},{10,... | collective-permute-start | bytes 589832 | tf_op jit(solution)/shard_map/ppermute | solution.py:271
  55.2 8.0 %collective-permute-done.14.refs_1_ = f32[1,192,256]{2,1,0:T(8,128)S(1)} collective-permute-done((f32[1,192,256]{2,1,0:T(8,128)S(1)}, f32[1,192,256]{2,1,0:T(8,128)S(1)}, u32[]{:S(2)}, u32[]{:S(2)}) %collective-permute-start.14) | collective-permute-done | bytes 196640 | tf_op jit(solution)/shard_map/ppermute | solution.py:271
  63.2 0.9 %all-to-all-done.1 = f32[32,8,256]{2,1,0:T(8,128)S(1)} async-done(((f32[32,8,256]{2,1,0:T(8,128)}), f32[32,8,256]{2,1,0:T(8,128)S(1)}, u32[]{:S(2)}, u32[]{:S(2)}) %all-to-all-start.1) | async-done | bytes 262176 | tf_op jit(solution)/shard_map/all_to_all | solution.py:381
  64.1 1.1 %last.1 = (f32[192,256]{1,0:T(8,128)}, f32[256,256]{1,0:T(8,128)}) custom-call(f32[1,192,256]{2,1,0:T(8,128)S(1)} %get-tuple-element.30.refs_0_, f32[1,192,256]{2,1,0:T(8,128)S(1)} %collective-permute-done.14.refs_1_, f32[256,256]{1,0:T(8,128)S(1)} %bitcast.4, bf16[2,256,256]{2,1,0:T(8,128)(2,1)S(1)} %get-tuple-element.29.refs_3_), custom_call_target="tpu_custom_call" | custom-call | flops 1000 | bytes 1000 | tf_op jit(solution)/shard_map/last/pallas_call | solution.py:242
  (2 shorter events, 0.1 us)
Async XLA Ops:
  0.6 8.1 %collective-permute-start.2 = (f32[192,256]{1,0:T(8,128)}, f32[192,256]{1,0:T(8,128)S(1)}, u32[]{:S(2)}, u32[]{:S(2)}) collective-permute-start(f32[192,256]{1,0:T(8,128)} %refs_3_.1), channel_id=1, source_target_pairs={{0,2},{1,3},{2,0},{3,1},{4,6},{5,7},{6,4},{7,5},{8,10},{9,11},{10,... | collective-permute-start | bytes 589832 | tf_op jit(solution)/shard_map/ppermute | solution.py:271
  3.6 9.8 %collective-permute-start.1 = (f32[192,256]{1,0:T(8,128)}, f32[192,256]{1,0:T(8,128)S(1)}, u32[]{:S(2)}, u32[]{:S(2)}) collective-permute-start(f32[192,256]{1,0:T(8,128)} %refs_3_.1), channel_id=1, source_target_pairs={{0,24},{1,25},{2,26},{3,27},{4,28},{5,29},{6,30},{7,31},{8,16},{9,... | collective-permute-start | bytes 589832 | tf_op jit(solution)/shard_map/ppermute | solution.py:271
  7.2 9.3 %collective-permute-start = (f32[192,256]{1,0:T(8,128)}, f32[192,256]{1,0:T(8,128)S(1)}, u32[]{:S(2)}, u32[]{:S(2)}) collective-permute-start(f32[192,256]{1,0:T(8,128)} %refs_3_.1), channel_id=1, source_target_pairs={{0,8},{1,9},{2,10},{3,11},{4,12},{5,13},{6,14},{7,15},{8,0},{9,1},... | collective-permute-start | bytes 589832 | tf_op jit(solution)/shard_map/ppermute | solution.py:271
  7.2 12.4 %collective-permute-start.7 = (f32[192,256]{1,0:T(8,128)}, f32[192,256]{1,0:T(8,128)S(1)}, u32[]{:S(2)}, u32[]{:S(2)}) collective-permute-start(f32[192,256]{1,0:T(8,128)} %refs_3_.1), channel_id=1, source_target_pairs={{0,1},{1,0},{2,3},{3,2},{4,5},{5,4},{6,7},{7,6},{8,9},{9,8},{10,11... | collective-permute-start | bytes 589832 | tf_op jit(solution)/shard_map/ppermute | solution.py:271
  8.7 11.4 %collective-permute-start.8 = (f32[192,256]{1,0:T(8,128)S(1)}, f32[192,256]{1,0:T(8,128)S(1)}, u32[]{:S(2)}, u32[]{:S(2)}) collective-permute-start(f32[192,256]{1,0:T(8,128)S(1)} %collective-permute-done.2.refs_2_.refs_0_), channel_id=1, source_target_pairs={{0,1},{1,0},{2,3},{3,2},{4,5},{5,4},{6,7},{7,6},{8,9},{9,8},{10,11... | collective-permute-start | bytes 589832 | tf_op jit(solution)/shard_map/ppermute | solution.py:271
  13.5 7.2 %collective-permute-start.6 = (f32[192,256]{1,0:T(8,128)S(1)}, f32[192,256]{1,0:T(8,128)S(1)}, u32[]{:S(2)}, u32[]{:S(2)}) collective-permute-start(f32[192,256]{1,0:T(8,128)S(1)} %collective-permute-done.1.refs_1_), channel_id=1, source_target_pairs={{0,8},{1,9},{2,10},{3,11},{4,12},{5,13},{6,14},{7,15},{8,0},{9,1},... | collective-permute-start | bytes 589832 | tf_op jit(solution)/shard_map/ppermute | solution.py:271
  16.5 8.8 %collective-permute-start.5 = (f32[192,256]{1,0:T(8,128)S(1)}, f32[192,256]{1,0:T(8,128)S(1)}, u32[]{:S(2)}, u32[]{:S(2)}) collective-permute-start(f32[192,256]{1,0:T(8,128)S(1)} %get-tuple-element.19), channel_id=1, source_target_pairs={{0,6},{1,7},{2,4},{3,5},{4,2},{5,3},{6,0},{7,1},{8,14},{9,15},{10,... | collective-permute-start | bytes 589832 | tf_op jit(solution)/shard_map/ppermute | solution.py:271
  18.1 13.9 %collective-permute-start.3 = (f32[192,256]{1,0:T(8,128)S(1)}, f32[192,256]{1,0:T(8,128)S(1)}, u32[]{:S(2)}, u32[]{:S(2)}) collective-permute-start(f32[192,256]{1,0:T(8,128)S(1)} %get-tuple-element.19), channel_id=1, source_target_pairs={{0,2},{1,3},{2,0},{3,1},{4,6},{5,7},{6,4},{7,5},{8,10},{9,11},{10,... | collective-permute-start | bytes 589832 | tf_op jit(solution)/shard_map/ppermute | solution.py:271
  19.6 12.4 %collective-permute-start.4 = (f32[192,256]{1,0:T(8,128)S(1)}, f32[192,256]{1,0:T(8,128)S(1)}, u32[]{:S(2)}, u32[]{:S(2)}) collective-permute-start(f32[192,256]{1,0:T(8,128)S(1)} %get-tuple-element.18.refs_0_), channel_id=1, source_target_pairs={{0,4},{1,5},{2,6},{3,7},{4,0},{5,1},{6,2},{7,3},{8,12},{9,13},{10,... | collective-permute-start | bytes 589832 | tf_op jit(solution)/shard_map/ppermute | solution.py:271
  20.6 0.9 %copy-start.3 = (f32[192,256]{1,0:T(8,128)S(1)}, f32[192,256]{1,0:T(8,128)}, u32[]{:S(2)}) copy-start(f32[192,256]{1,0:T(8,128)} %refs_3_.1) | copy-start | bytes 589828
  21.6 11.1 %collective-permute-start.10 = (f32[192,256]{1,0:T(8,128)S(1)}, f32[192,256]{1,0:T(8,128)S(1)}, u32[]{:S(2)}, u32[]{:S(2)}) collective-permute-start(f32[192,256]{1,0:T(8,128)S(1)} %get-tuple-element.20.refs_6_.refs_4_), channel_id=1, source_target_pairs={{0,4},{1,5},{2,6},{3,7},{4,0},{5,1},{6,2},{7,3},{8,12},{9,13},{10,... | collective-permute-start | bytes 589832 | tf_op jit(solution)/shard_map/ppermute | solution.py:271
  25.3 7.4 %collective-permute-start.11 = (f32[192,256]{1,0:T(8,128)S(1)}, f32[192,256]{1,0:T(8,128)S(1)}, u32[]{:S(2)}, u32[]{:S(2)}) collective-permute-start(f32[192,256]{1,0:T(8,128)S(1)} %collective-permute-done.5.refs_3_), channel_id=1, source_target_pairs={{0,8},{1,9},{2,10},{3,11},{4,12},{5,13},{6,14},{7,15},{8,0},{9,1},... | collective-permute-start | bytes 589832 | tf_op jit(solution)/shard_map/ppermute | solution.py:271
  26.8 6.0 %collective-permute-start.9 = (f32[192,256]{1,0:T(8,128)S(1)}, f32[192,256]{1,0:T(8,128)S(1)}, u32[]{:S(2)}, u32[]{:S(2)}) collective-permute-start(f32[192,256]{1,0:T(8,128)S(1)} %get-tuple-element.21), channel_id=1, source_target_pairs={{0,2},{1,3},{2,0},{3,1},{4,6},{5,7},{6,4},{7,5},{8,10},{9,11},{10,... | collective-permute-start | bytes 589832 | tf_op jit(solution)/shard_map/ppermute | solution.py:271
  31.9 2.5 %copy-start = (bf16[2,2,768,768]{3,2,1,0:T(8,128)(2,1)}, bf16[2,2,768,768]{3,2,1,0:T(8,128)(2,1)S(1)}, u32[]{:S(2)}) copy-start(bf16[2,2,768,768]{3,2,1,0:T(8,128)(2,1)S(1)} %get-tuple-element.22.refs_8_.refs_9_.refs_2_) | copy-start | bytes 14155780
  32.8 2.4 %collective-permute-start.12 = (f32[4,192,256]{2,1,0:T(8,128)S(1)}, f32[4,192,256]{2,1,0:T(8,128)S(1)}, u32[]{:S(2)}, u32[]{:S(2)}) collective-permute-start(f32[4,192,256]{2,1,0:T(8,128)S(1)} %pick.1), channel_id=1, source_target_pairs={{0,1},{1,0},{2,3},{3,2},{4,5},{5,4},{6,7},{7,6},{8,9},{9,8},{10,11... | collective-permute-start | bytes 2359304 | tf_op jit(solution)/shard_map/ppermute | solution.py:271
  35.2 7.9 %copy-start.4 = (f32[256,256]{1,0:T(8,128)S(1)}, f32[256,256]{1,0:T(8,128)}, u32[]{:S(2)}) copy-start(f32[256,256]{1,0:T(8,128)} %refs_0_.3) | copy-start | bytes 786436
  35.2 7.9 %copy-start.5 = (f32[256,256]{1,0:T(8,128)S(1)}, f32[256,256]{1,0:T(8,128)}, u32[]{:S(2)}) copy-start(f32[256,256]{1,0:T(8,128)} %refs_1_.1) | copy-start | bytes 786436
  35.2 7.9 %copy-start.6 = (f32[256,256]{1,0:T(8,128)S(1)}, f32[256,256]{1,0:T(8,128)}, u32[]{:S(2)}) copy-start(f32[256,256]{1,0:T(8,128)} %refs_2_.2) | copy-start | bytes 786436
  36.5 8.2 %copy-start.2 = (f32[192,256]{1,0:T(8,128)S(1)}, f32[192,256]{1,0:T(8,128)}, u32[]{:S(2)}) copy-start(f32[192,256]{1,0:T(8,128)} %refs_2_.3) | copy-start | bytes 589828
  36.5 13.3 %all-to-all-start = ((f32[32,8,256]{2,1,0:T(8,128)}), f32[32,8,256]{2,1,0:T(8,128)S(1)}, u32[]{:S(2)}, u32[]{:S(2)}) async-start(f32[32,8,256]{2,1,0:T(8,128)} %bitcast), calls=%async_computation | async-start | bytes 524288 | tf_op jit(solution)/shard_map/all_to_all | solution.py:364
  39.3 2.3 %copy-start.1 = (bf16[2,2,768,768]{3,2,1,0:T(8,128)(2,1)S(1)}, bf16[2,2,768,768]{3,2,1,0:T(8,128)(2,1)}, u32[]{:S(2)}) copy-start(bf16[2,2,768,768]{3,2,1,0:T(8,128)(2,1)} %copy-done) | copy-start | bytes 14155780
  42.9 1.8 %collective-permute-start.13 = (f32[2,192,256]{2,1,0:T(8,128)S(1)}, f32[2,192,256]{2,1,0:T(8,128)S(1)}, u32[]{:S(2)}, u32[]{:S(2)}) collective-permute-start(f32[2,192,256]{2,1,0:T(8,128)S(1)} %get-tuple-element.28), channel_id=1, source_target_pairs={{0,1},{1,0},{2,3},{3,2},{4,5},{5,4},{6,7},{7,6},{8,9},{9,8},{10,11... | collective-permute-start | bytes 1179656 | tf_op jit(solution)/shard_map/ppermute | solution.py:271
  50.9 13.2 %all-to-all-start.1 = ((f32[32,8,256]{2,1,0:T(8,128)}), f32[32,8,256]{2,1,0:T(8,128)S(1)}, u32[]{:S(2)}, u32[]{:S(2)}) async-start(f32[32,8,256]{2,1,0:T(8,128)} %bitcast.2), calls=%async_computation.1 | async-start | bytes 524288 | tf_op jit(solution)/shard_map/all_to_all | solution.py:381
  53.5 9.7 %collective-permute-start.14 = (f32[1,192,256]{2,1,0:T(8,128)S(1)}, f32[1,192,256]{2,1,0:T(8,128)S(1)}, u32[]{:S(2)}, u32[]{:S(2)}) collective-permute-start(f32[1,192,256]{2,1,0:T(8,128)S(1)} %get-tuple-element.31.refs_4_), channel_id=1, source_target_pairs={{0,2},{1,3},{2,0},{3,1},{4,6},{5,7},{6,4},{7,5},{8,10},{9,11},{10,... | collective-permute-start | bytes 589832 | tf_op jit(solution)/shard_map/ppermute | solution.py:271

commit v9 on v8

--- a/solution.py
+++ b/solution.py
@@ -75,7 +75,7 @@
 def prepare_kernel(blocks, places, *refs):
     rows_of, refs = refs[: len(places)], refs[len(places) :]
     panel, adjoint, trail, start, trail_parts, reduced, landing, panel_here, adjoint_here = refs[:9]
-    rows_here, sems = refs[9:]
+    rows_here, totals, sems = refs[9:]
     rows = trail.shape[0] // blocks
     small = [
         pltpu.make_async_copy(panel, panel_here, sems.at[blocks]),
@@ -103,10 +103,14 @@
             to = slice(piece // 2 * height, (piece // 2 + 1) * height)
             trail_parts[0, piece % 2, at, to] = high
             trail_parts[1, piece % 2, at, to] = low
+        for core in range(2):
+            part = dot_three(
+                row_high[:, i * rows : (i + 1) * rows], row_low[:, i * rows : (i + 1) * rows],
+                trail_parts[0, core, at, :], trail_parts[1, core, at, :],
+            )
+            totals[core] = totals[core] + part if i else part
     for core in range(2):
-        reduced[0, core], reduced[1, core] = parts(
-            dot_three(row_high, row_low, trail_parts[0, core], trail_parts[1, core])
-        )
+        reduced[0, core], reduced[1, core] = parts(totals[core])
 
 
 def tail_kernel(factor, inverse, corner, base, unit, inv):
@@ -234,7 +238,7 @@
 
 
 def call(
-    kernel, out, *args, name, after=(), in_specs=None, out_specs=None, scratch=(), aliases=None
+    kernel, out, *args, name, after=(), in_specs=None, out_specs=None, scratch=(), limit=LIMIT
 ):
     def body(*refs):
         kernel(*refs[: len(args)], *refs[len(args) + len(after) :])
@@ -246,8 +250,7 @@
         in_specs=(in_specs or [VMEM] * len(args)) + [ANY] * len(after),
         out_specs=out_specs or [VMEM] * len(out),
         scratch_shapes=list(scratch),
-        input_output_aliases=aliases or {},
-        compiler_params=pltpu.CompilerParams(vmem_limit_bytes=LIMIT),
+        compiler_params=pltpu.CompilerParams(vmem_limit_bytes=limit),
         cost_estimate=pl.CostEstimate(flops=1000, bytes_accessed=1000, transcendentals=0),
         name=name,
     )(*args, *after)
@@ -293,7 +296,7 @@
             for near, far in ((1, 3), (0, 2)):
                 own, other = call(
                     choose_kernel, [f32(height, size)] * 2, pieces[near], pieces[far],
-                    name="choose", after=(row_blocks[1],) if near else (row_blocks[2], row_blocks[3]),
+                    name="choose", after=(row_blocks[1],) if near else (row_blocks[2],),
                 )
                 diagonal = flip(sets[0][3], plane=1) if sets else flip(other, y=1, col=2)
                 sets.append([own, flip(other, col=2), flip(own, y=1), diagonal])
@@ -301,7 +304,7 @@
         else:
             chosen = jnp.stack([pieces[d] for d in range(cols)] * group)
 
-        blocks = 4
+        blocks = 3
         params = [
             pltpu.with_memory_space_constraint(x, pltpu.HBM)
             for x in (panel, panel_adjoint, trail_adjoint)
@@ -316,7 +319,9 @@
             in_specs=[VMEM] * (cols - 1) + [pl.BlockSpec(memory_space=pltpu.HBM)] * 3,
             scratch=[pltpu.VMEM(trail_adjoint.shape, jnp.float32)]
             + [pltpu.VMEM((height, size), jnp.float32)] * 2
-            + [pltpu.VMEM((rows, size), jnp.float32), pltpu.SemaphoreType.DMA((blocks + 2,))],
+            + [pltpu.VMEM((rows, size), jnp.float32), pltpu.VMEM((2, size, half), jnp.float32)]
+            + [pltpu.SemaphoreType.DMA((blocks + 2,))],
+            limit=LIMIT if paired else 2 * LIMIT,
         )
 
         if paired:

time: 65.5 us -> 65.4 us (level)
  waiting for transfers between devices: 25.5 us -> 22.7 us
  starting transfers between devices: 23.5 us -> 26 us
    ppermute x15, waiting for transfers between devices: 19.8 us -> 17.1 us  [flip(): return lax.ppermute(x, AXES, pairs)]
    ppermute x15, starting transfers between devices: 18.2 us -> 19.9 us  [flip(): return lax.ppermute(x, AXES, pairs)]
    all_to_all x1, starting transfers between devices: 2.72 us -> 3.6 us  [on_device(): shares = lax.all_to_all(gram_t, AXES, 0, 0, tiled=True)]
  transfers between devices with their start and end apart: 17 -> 17, of which waited for: 12 -> 9; matrix products, arithmetic and copies ran while one was open for 0% -> 0% of each run, Pallas kernels for 13% -> 13%
where the time goes in v9:
time: 65.4 us; the launch traced here: 65.1 us
  starting transfers between devices  26 us (40%)
  waiting for transfers between devices  22.7 us (35%)
  Pallas kernels  11.9 us (18%)
  local copies, waits for them, and re-layouts  3.66 us (6%)
  between operations  0.79 us (1%)
    ppermute x15, starting transfers between devices, flip(): return lax.ppermute(x, AXES, pairs)  19.9 us
    ppermute x15, waiting for transfers between devices, flip(): return lax.ppermute(x, AXES, pairs)  17.1 us
    pallas_call x11, Pallas kernels, call(): pl.pallas_call(body, grid=(1,), out_shape=out, in_specs=(in_specs or [VME...  11.9 us
    all_to_all x1, waiting for transfers between devices, on_device(): shares = lax.all_to_all(gram_t, AXES, 0, 0, tiled=True)  4.75 us
    unnamed x14, local copies, waits for them, and re-layouts  3.66 us
    all_to_all x1, starting transfers between devices, on_device(): shares = lax.all_to_all(gram_t, AXES, 0, 0, tiled=True)  3.6 us
    all_to_all x1, starting transfers between devices, on_device(): gathered = lax.all_to_all(left_t, AXES, 0, 0, tiled=True)  2.59 us
  transfers between devices with their start and end apart: 17, of which 9 were waited for; matrix products, arithmetic and copies ran while one was open for 0% of the time, Pallas kernels for 13%

profile of v9, /device:TPU:0, one launch (start us, length us, event | category | flops | bytes accessed | tf_op | source)
XLA Modules:
  0.0 65.1 jit_solution(4120079321775514354)
XLA Ops:
  0.6 5.1 %collective-permute-start.1 = (f32[192,256]{1,0:T(8,128)}, f32[192,256]{1,0:T(8,128)S(1)}, u32[]{:S(2)}, u32[]{:S(2)}) collective-permute-start(f32[192,256]{1,0:T(8,128)} %refs_3_.1), channel_id=1, source_target_pairs={{0,24},{1,25},{2,26},{3,27},{4,28},{5,29},{6,30},{7,31},{8,16},{9,... | collective-permute-start | bytes 589832 | tf_op jit(solution)/shard_map/ppermute | solution.py:274
  5.7 1.5 %collective-permute-start.2 = (f32[192,256]{1,0:T(8,128)}, f32[192,256]{1,0:T(8,128)S(1)}, u32[]{:S(2)}, u32[]{:S(2)}) collective-permute-start(f32[192,256]{1,0:T(8,128)} %refs_3_.1), channel_id=1, source_target_pairs={{0,2},{1,3},{2,0},{3,1},{4,6},{5,7},{6,4},{7,5},{8,10},{9,11},{10,... | collective-permute-start | bytes 589832 | tf_op jit(solution)/shard_map/ppermute | solution.py:274
  7.2 0.0 collective-permute-start
  7.2 0.0 collective-permute-start.7
  7.2 4.5 %collective-permute-done.1.refs_1_ = f32[192,256]{1,0:T(8,128)S(1)} collective-permute-done((f32[192,256]{1,0:T(8,128)}, f32[192,256]{1,0:T(8,128)S(1)}, u32[]{:S(2)}, u32[]{:S(2)}) %collective-permute-start.1) | collective-permute-done | bytes 196640 | tf_op jit(solution)/shard_map/ppermute | solution.py:274
  11.7 3.0 %collective-permute-start.6 = (f32[192,256]{1,0:T(8,128)S(1)}, f32[192,256]{1,0:T(8,128)S(1)}, u32[]{:S(2)}, u32[]{:S(2)}) collective-permute-start(f32[192,256]{1,0:T(8,128)S(1)} %collective-permute-done.1.refs_1_), channel_id=1, source_target_pairs={{0,8},{1,9},{2,10},{3,11},{4,12},{5,13},{6,14},{7,15},{8,0},{9,1},... | collective-permute-start | bytes 589832 | tf_op jit(solution)/shard_map/ppermute | solution.py:274
  14.8 0.0 collective-permute-done.2.refs_2_.refs_0_
  14.8 0.7 %collective-permute-done.refs_0_ = f32[192,256]{1,0:T(8,128)S(1)} collective-permute-done((f32[192,256]{1,0:T(8,128)}, f32[192,256]{1,0:T(8,128)S(1)}, u32[]{:S(2)}, u32[]{:S(2)}) %collective-permute-start) | collective-permute-done | bytes 196640 | tf_op jit(solution)/shard_map/ppermute | solution.py:274
  15.5 2.3 %collective-permute-start.5 = (f32[192,256]{1,0:T(8,128)S(1)}, f32[192,256]{1,0:T(8,128)S(1)}, u32[]{:S(2)}, u32[]{:S(2)}) collective-permute-start(f32[192,256]{1,0:T(8,128)S(1)} %get-tuple-element.19), channel_id=1, source_target_pairs={{0,6},{1,7},{2,4},{3,5},{4,2},{5,3},{6,0},{7,1},{8,14},{9,15},{10,... | collective-permute-start | bytes 589832 | tf_op jit(solution)/shard_map/ppermute | solution.py:274
  17.8 0.0 collective-permute-start.11
  17.8 0.8 %collective-permute-start.3 = (f32[192,256]{1,0:T(8,128)S(1)}, f32[192,256]{1,0:T(8,128)S(1)}, u32[]{:S(2)}, u32[]{:S(2)}) collective-permute-start(f32[192,256]{1,0:T(8,128)S(1)} %get-tuple-element.19), channel_id=1, source_target_pairs={{0,2},{1,3},{2,0},{3,1},{4,6},{5,7},{6,4},{7,5},{8,10},{9,11},{10,... | collective-permute-start | bytes 589832 | tf_op jit(solution)/shard_map/ppermute | solution.py:274
  18.6 0.0 collective-permute-done.7.refs_2_.refs_1_
  18.6 0.5 collective-permute-start.4
  19.1 0.3 collective-permute-done.6.refs_1_
  19.4 0.0 copy-start.3
  19.4 0.9 %copy-done.3 = f32[192,256]{1,0:T(8,128)S(1)} copy-done((f32[192,256]{1,0:T(8,128)S(1)}, f32[192,256]{1,0:T(8,128)}, u32[]{:S(2)}) %copy-start.3) | copy-done | bytes 196632
  20.4 1.6 %collective-permute-start.9 = (f32[192,256]{1,0:T(8,128)S(1)}, f32[192,256]{1,0:T(8,128)S(1)}, u32[]{:S(2)}, u32[]{:S(2)}) collective-permute-start(f32[192,256]{1,0:T(8,128)S(1)} %get-tuple-element.20.refs_6_.refs_4_), channel_id=1, source_target_pairs={{0,4},{1,5},{2,6},{3,7},{4,0},{5,1},{6,2},{7,3},{8,12},{9,13},{10,... | collective-permute-start | bytes 589832 | tf_op jit(solution)/shard_map/ppermute | solution.py:274
  21.9 2.4 %collective-permute-done.5.refs_3_ = f32[192,256]{1,0:T(8,128)S(1)} collective-permute-done((f32[192,256]{1,0:T(8,128)S(1)}, f32[192,256]{1,0:T(8,128)S(1)}, u32[]{:S(2)}, u32[]{:S(2)}) %collective-permute-start.5) | collective-permute-done | bytes 196640 | tf_op jit(solution)/shard_map/ppermute | solution.py:274
  24.3 0.5 collective-permute-start.10
  24.9 0.0 collective-permute-done.11.refs_2_
  24.9 2.4 %collective-permute-start.8 = (f32[192,256]{1,0:T(8,128)S(1)}, f32[192,256]{1,0:T(8,128)S(1)}, u32[]{:S(2)}, u32[]{:S(2)}) collective-permute-start(f32[192,256]{1,0:T(8,128)S(1)} %get-tuple-element.21), channel_id=1, source_target_pairs={{0,2},{1,3},{2,0},{3,1},{4,6},{5,7},{6,4},{7,5},{8,10},{9,11},{10,... | collective-permute-start | bytes 589832 | tf_op jit(solution)/shard_map/ppermute | solution.py:274
  27.3 4.4 %prepare.1 = (f32[256,256]{1,0:T(8,128)S(1)}, bf16[2,2,768,768]{3,2,1,0:T(8,128)(2,1)S(1)}, bf16[2,2,256,768]{3,2,1,0:T(8,128)(2,1)S(1)}) custom-call(f32[192,256]{1,0:T(8,128)S(1)} %collective-permute-done.2.refs_2_.refs_0_, f32[192,256]{1,0:T(8,128)S(1)} %collective-permute-done.7.refs_2_.refs_1_, f32[192,256]{1,0:T(8,128)S(1)} %collective-permute-done.11.refs_2_, ...), custom_call_target="tpu_custom_call" | custom-call | flops 1000 | bytes 1000 | tf_op jit(solution)/shard_map/prepare/pallas_call | solution.py:246
  31.7 0.0 copy-start
  31.7 0.0 collective-permute-done.4.refs_2_
  31.7 0.0 collective-permute-done.3.refs_1_
  31.7 0.0 collective-permute-done.10.refs_7_
  31.8 0.0 collective-permute-done.9.refs_6_
  31.8 0.0 collective-permute-done.8.refs_5_
  31.8 0.1 pick.1
  31.9 0.1 collective-permute-start.12
  31.9 1.5 %product_first.1 = (f32[768,256]{1,0:T(8,128)S(1)}, f32[256,256]{1,0:T(8,128)S(1)}) custom-call(f32[192,256]{1,0:T(8,128)S(1)} %get-tuple-element.18.refs_0_, f32[192,256]{1,0:T(8,128)S(1)} %collective-permute-done.3.refs_1_, f32[192,256]{1,0:T(8,128)S(1)} %collective-permute-done.4.refs_2_, f32[192,256]{1,0:T(8,128)S(1)} %collective-permute-done.5.refs_3_, ...), custom_call_target="tpu_custom_call" | custom-call | flops 1000 | bytes 1000 | tf_op jit(solution)/shard_map/product_first/pallas_call | solution.py:246
  33.5 0.4 copy-done
  33.9 0.3 collective-permute-done.12.refs_0_
  34.2 0.0 copy-start.4
  34.2 0.0 copy-start.5
  34.2 0.0 copy-start.6
  34.2 1.4 %gram.1.refs_3_ = f32[256,256]{1,0:T(8,128)} custom-call(f32[4,192,256]{2,1,0:T(8,128)S(1)} %collective-permute-done.12.refs_0_, f32[256,256]{1,0:T(8,128)S(1)} %get-tuple-element.26.refs_1_, bf16[2,2,256,768]{3,2,1,0:T(8,128)(2,1)S(1)} %get-tuple-element.24.refs_10_.refs_2_), custom_call_target="tpu_custom_call" | custom-call | flops 1000 | bytes 1000 | tf_op jit(solution)/shard_map/gram/pallas_call | solution.py:246
  35.6 0.0 copy-start.2
  35.6 3.6 %all-to-all-start = ((f32[32,8,256]{2,1,0:T(8,128)}), f32[32,8,256]{2,1,0:T(8,128)S(1)}, u32[]{:S(2)}, u32[]{:S(2)}) async-start(f32[32,8,256]{2,1,0:T(8,128)} %bitcast), calls=%async_computation | async-start | bytes 524288 | tf_op jit(solution)/shard_map/all_to_all | solution.py:369
  39.2 0.0 copy-start.1
  39.2 2.3 %copy-done.1 = bf16[2,2,768,768]{3,2,1,0:T(8,128)(2,1)S(1)} copy-done((bf16[2,2,768,768]{3,2,1,0:T(8,128)(2,1)S(1)}, bf16[2,2,768,768]{3,2,1,0:T(8,128)(2,1)}, u32[]{:S(2)}) %copy-start.1) | copy-done | bytes 4718616
  41.5 1.3 %product_second.1 = (f32[2,192,256]{2,1,0:T(8,128)S(1)}, f32[2,192,256]{2,1,0:T(8,128)S(1)}) custom-call(f32[4,192,256]{2,1,0:T(8,128)S(1)} %collective-permute-done.12.refs_0_, f32[768,256]{1,0:T(8,128)S(1)} %get-tuple-element.25.refs_1_, bf16[2,2,768,768]{3,2,1,0:T(8,128)(2,1)S(1)} %copy-done.1, f32[256,256]{1,0:T(8,128)} %gram.1.refs_3_), custom_call_target="tpu_custom_call" | custom-call | flops 1000 | bytes 1000 | tf_op jit(solution)/shard_map/product_second/pallas_call | solution.py:246
  42.9 0.3 collective-permute-start.13
  43.2 0.0 copy-done.4
  43.2 0.0 copy-done.5
  43.2 0.0 copy-done.6
  43.2 0.6 tail.1
  43.8 0.8 %collective-permute-done.13.refs_1_ = f32[2,192,256]{2,1,0:T(8,128)S(1)} collective-permute-done((f32[2,192,256]{2,1,0:T(8,128)S(1)}, f32[2,192,256]{2,1,0:T(8,128)S(1)}, u32[]{:S(2)}, u32[]{:S(2)}) %collective-permute-start.13) | collective-permute-done | bytes 393248 | tf_op jit(solution)/shard_map/ppermute | solution.py:274
  44.7 0.0 copy-done.2
  44.7 0.4 add.1
  45.0 4.7 %all-to-all-done = f32[32,8,256]{2,1,0:T(8,128)S(1)} async-done(((f32[32,8,256]{2,1,0:T(8,128)}), f32[32,8,256]{2,1,0:T(8,128)S(1)}, u32[]{:S(2)}, u32[]{:S(2)}) %all-to-all-start) | async-done | bytes 262176 | tf_op jit(solution)/shard_map/all_to_all | solution.py:369
  49.8 1.1 %middle.1 = f32[256,256]{1,0:T(8,128)} custom-call(f32[256,256]{1,0:T(8,128)S(1)} %bitcast.5, f32[256,256]{1,0:T(8,128)S(1)} %get-tuple-element.32.refs_1_, bf16[2,256,256]{2,1,0:T(8,128)(2,1)S(1)} %get-tuple-element.33.refs_2_, bf16[2,256,256]{2,1,0:T(8,128)(2,1)S(1)} %get-tuple-element.29.refs_3_, f32[1,192,256]{2,1,0:T(8,128)S(1)} %get-tuple-element.31.refs_4_), custom_call_target="tpu_custom_call" | custom-call | flops 1000 | bytes 1000 | tf_op jit(solution)/shard_map/middle/pallas_call | solution.py:246
  50.9 2.6 %all-to-all-start.1 = ((f32[32,8,256]{2,1,0:T(8,128)}), f32[32,8,256]{2,1,0:T(8,128)S(1)}, u32[]{:S(2)}, u32[]{:S(2)}) async-start(f32[32,8,256]{2,1,0:T(8,128)} %bitcast.2), calls=%async_computation.1 | async-start | bytes 524288 | tf_op jit(solution)/shard_map/all_to_all | solution.py:386
  53.5 1.7 %collective-permute-start.14 = (f32[1,192,256]{2,1,0:T(8,128)S(1)}, f32[1,192,256]{2,1,0:T(8,128)S(1)}, u32[]{:S(2)}, u32[]{:S(2)}) collective-permute-start(f32[1,192,256]{2,1,0:T(8,128)S(1)} %get-tuple-element.31.refs_4_), channel_id=1, source_target_pairs={{0,2},{1,3},{2,0},{3,1},{4,6},{5,7},{6,4},{7,5},{8,10},{9,11},{10,... | collective-permute-start | bytes 589832 | tf_op jit(solution)/shard_map/ppermute | solution.py:274
  55.2 8.0 %collective-permute-done.14.refs_1_ = f32[1,192,256]{2,1,0:T(8,128)S(1)} collective-permute-done((f32[1,192,256]{2,1,0:T(8,128)S(1)}, f32[1,192,256]{2,1,0:T(8,128)S(1)}, u32[]{:S(2)}, u32[]{:S(2)}) %collective-permute-start.14) | collective-permute-done | bytes 196640 | tf_op jit(solution)/shard_map/ppermute | solution.py:274
  63.1 0.9 %all-to-all-done.1 = f32[32,8,256]{2,1,0:T(8,128)S(1)} async-done(((f32[32,8,256]{2,1,0:T(8,128)}), f32[32,8,256]{2,1,0:T(8,128)S(1)}, u32[]{:S(2)}, u32[]{:S(2)}) %all-to-all-start.1) | async-done | bytes 262176 | tf_op jit(solution)/shard_map/all_to_all | solution.py:386
  64.1 1.1 %last.1 = (f32[192,256]{1,0:T(8,128)}, f32[256,256]{1,0:T(8,128)}) custom-call(f32[1,192,256]{2,1,0:T(8,128)S(1)} %get-tuple-element.30.refs_0_, f32[1,192,256]{2,1,0:T(8,128)S(1)} %collective-permute-done.14.refs_1_, f32[256,256]{1,0:T(8,128)S(1)} %bitcast.4, bf16[2,256,256]{2,1,0:T(8,128)(2,1)S(1)} %get-tuple-element.29.refs_3_), custom_call_target="tpu_custom_call" | custom-call | flops 1000 | bytes 1000 | tf_op jit(solution)/shard_map/last/pallas_call | solution.py:246
  (2 shorter events, 0.1 us)
Async XLA Ops:
  0.6 11.1 %collective-permute-start.1 = (f32[192,256]{1,0:T(8,128)}, f32[192,256]{1,0:T(8,128)S(1)}, u32[]{:S(2)}, u32[]{:S(2)}) collective-permute-start(f32[192,256]{1,0:T(8,128)} %refs_3_.1), channel_id=1, source_target_pairs={{0,24},{1,25},{2,26},{3,27},{4,28},{5,29},{6,30},{7,31},{8,16},{9,... | collective-permute-start | bytes 589832 | tf_op jit(solution)/shard_map/ppermute | solution.py:274
  5.7 9.0 %collective-permute-start.2 = (f32[192,256]{1,0:T(8,128)}, f32[192,256]{1,0:T(8,128)S(1)}, u32[]{:S(2)}, u32[]{:S(2)}) collective-permute-start(f32[192,256]{1,0:T(8,128)} %refs_3_.1), channel_id=1, source_target_pairs={{0,2},{1,3},{2,0},{3,1},{4,6},{5,7},{6,4},{7,5},{8,10},{9,11},{10,... | collective-permute-start | bytes 589832 | tf_op jit(solution)/shard_map/ppermute | solution.py:274
  7.2 8.3 %collective-permute-start = (f32[192,256]{1,0:T(8,128)}, f32[192,256]{1,0:T(8,128)S(1)}, u32[]{:S(2)}, u32[]{:S(2)}) collective-permute-start(f32[192,256]{1,0:T(8,128)} %refs_3_.1), channel_id=1, source_target_pairs={{0,8},{1,9},{2,10},{3,11},{4,12},{5,13},{6,14},{7,15},{8,0},{9,1},... | collective-permute-start | bytes 589832 | tf_op jit(solution)/shard_map/ppermute | solution.py:274
  7.2 11.4 %collective-permute-start.7 = (f32[192,256]{1,0:T(8,128)}, f32[192,256]{1,0:T(8,128)S(1)}, u32[]{:S(2)}, u32[]{:S(2)}) collective-permute-start(f32[192,256]{1,0:T(8,128)} %refs_3_.1), channel_id=1, source_target_pairs={{0,1},{1,0},{2,3},{3,2},{4,5},{5,4},{6,7},{7,6},{8,9},{9,8},{10,11... | collective-permute-start | bytes 589832 | tf_op jit(solution)/shard_map/ppermute | solution.py:274
  11.7 7.7 %collective-permute-start.6 = (f32[192,256]{1,0:T(8,128)S(1)}, f32[192,256]{1,0:T(8,128)S(1)}, u32[]{:S(2)}, u32[]{:S(2)}) collective-permute-start(f32[192,256]{1,0:T(8,128)S(1)} %collective-permute-done.1.refs_1_), channel_id=1, source_target_pairs={{0,8},{1,9},{2,10},{3,11},{4,12},{5,13},{6,14},{7,15},{8,0},{9,1},... | collective-permute-start | bytes 589832 | tf_op jit(solution)/shard_map/ppermute | solution.py:274
  15.5 8.8 %collective-permute-start.5 = (f32[192,256]{1,0:T(8,128)S(1)}, f32[192,256]{1,0:T(8,128)S(1)}, u32[]{:S(2)}, u32[]{:S(2)}) collective-permute-start(f32[192,256]{1,0:T(8,128)S(1)} %get-tuple-element.19), channel_id=1, source_target_pairs={{0,6},{1,7},{2,4},{3,5},{4,2},{5,3},{6,0},{7,1},{8,14},{9,15},{10,... | collective-permute-start | bytes 589832 | tf_op jit(solution)/shard_map/ppermute | solution.py:274
  17.8 7.1 %collective-permute-start.11 = (f32[192,256]{1,0:T(8,128)S(1)}, f32[192,256]{1,0:T(8,128)S(1)}, u32[]{:S(2)}, u32[]{:S(2)}) collective-permute-start(f32[192,256]{1,0:T(8,128)S(1)} %collective-permute-done.2.refs_2_.refs_0_), channel_id=1, source_target_pairs={{0,1},{1,0},{2,3},{3,2},{4,5},{5,4},{6,7},{7,6},{8,9},{9,8},{10,11... | collective-permute-start | bytes 589832 | tf_op jit(solution)/shard_map/ppermute | solution.py:274
  17.8 13.9 %collective-permute-start.3 = (f32[192,256]{1,0:T(8,128)S(1)}, f32[192,256]{1,0:T(8,128)S(1)}, u32[]{:S(2)}, u32[]{:S(2)}) collective-permute-start(f32[192,256]{1,0:T(8,128)S(1)} %get-tuple-element.19), channel_id=1, source_target_pairs={{0,2},{1,3},{2,0},{3,1},{4,6},{5,7},{6,4},{7,5},{8,10},{9,11},{10,... | collective-permute-start | bytes 589832 | tf_op jit(solution)/shard_map/ppermute | solution.py:274
  18.6 13.1 %collective-permute-start.4 = (f32[192,256]{1,0:T(8,128)S(1)}, f32[192,256]{1,0:T(8,128)S(1)}, u32[]{:S(2)}, u32[]{:S(2)}) collective-permute-start(f32[192,256]{1,0:T(8,128)S(1)} %get-tuple-element.18.refs_0_), channel_id=1, source_target_pairs={{0,4},{1,5},{2,6},{3,7},{4,0},{5,1},{6,2},{7,3},{8,12},{9,13},{10,... | collective-permute-start | bytes 589832 | tf_op jit(solution)/shard_map/ppermute | solution.py:274
  19.4 0.9 %copy-start.3 = (f32[192,256]{1,0:T(8,128)S(1)}, f32[192,256]{1,0:T(8,128)}, u32[]{:S(2)}) copy-start(f32[192,256]{1,0:T(8,128)} %refs_3_.1) | copy-start | bytes 589828
  20.4 11.4 %collective-permute-start.9 = (f32[192,256]{1,0:T(8,128)S(1)}, f32[192,256]{1,0:T(8,128)S(1)}, u32[]{:S(2)}, u32[]{:S(2)}) collective-permute-start(f32[192,256]{1,0:T(8,128)S(1)} %get-tuple-element.20.refs_6_.refs_4_), channel_id=1, source_target_pairs={{0,4},{1,5},{2,6},{3,7},{4,0},{5,1},{6,2},{7,3},{8,12},{9,13},{10,... | collective-permute-start | bytes 589832 | tf_op jit(solution)/shard_map/ppermute | solution.py:274
  24.3 7.4 %collective-permute-start.10 = (f32[192,256]{1,0:T(8,128)S(1)}, f32[192,256]{1,0:T(8,128)S(1)}, u32[]{:S(2)}, u32[]{:S(2)}) collective-permute-start(f32[192,256]{1,0:T(8,128)S(1)} %collective-permute-done.5.refs_3_), channel_id=1, source_target_pairs={{0,8},{1,9},{2,10},{3,11},{4,12},{5,13},{6,14},{7,15},{8,0},{9,1},... | collective-permute-start | bytes 589832 | tf_op jit(solution)/shard_map/ppermute | solution.py:274
  24.9 6.9 %collective-permute-start.8 = (f32[192,256]{1,0:T(8,128)S(1)}, f32[192,256]{1,0:T(8,128)S(1)}, u32[]{:S(2)}, u32[]{:S(2)}) collective-permute-start(f32[192,256]{1,0:T(8,128)S(1)} %get-tuple-element.21), channel_id=1, source_target_pairs={{0,2},{1,3},{2,0},{3,1},{4,6},{5,7},{6,4},{7,5},{8,10},{9,11},{10,... | collective-permute-start | bytes 589832 | tf_op jit(solution)/shard_map/ppermute | solution.py:274
  31.7 2.2 %copy-start = (bf16[2,2,768,768]{3,2,1,0:T(8,128)(2,1)}, bf16[2,2,768,768]{3,2,1,0:T(8,128)(2,1)S(1)}, u32[]{:S(2)}) copy-start(bf16[2,2,768,768]{3,2,1,0:T(8,128)(2,1)S(1)} %get-tuple-element.22.refs_8_.refs_9_.refs_2_) | copy-start | bytes 14155780
  31.9 2.4 %collective-permute-start.12 = (f32[4,192,256]{2,1,0:T(8,128)S(1)}, f32[4,192,256]{2,1,0:T(8,128)S(1)}, u32[]{:S(2)}, u32[]{:S(2)}) collective-permute-start(f32[4,192,256]{2,1,0:T(8,128)S(1)} %pick.1), channel_id=1, source_target_pairs={{0,1},{1,0},{2,3},{3,2},{4,5},{5,4},{6,7},{7,6},{8,9},{9,8},{10,11... | collective-permute-start | bytes 2359304 | tf_op jit(solution)/shard_map/ppermute | solution.py:274
  34.2 9.0 %copy-start.4 = (f32[256,256]{1,0:T(8,128)S(1)}, f32[256,256]{1,0:T(8,128)}, u32[]{:S(2)}) copy-start(f32[256,256]{1,0:T(8,128)} %refs_0_.3) | copy-start | bytes 786436
  34.2 9.0 %copy-start.5 = (f32[256,256]{1,0:T(8,128)S(1)}, f32[256,256]{1,0:T(8,128)}, u32[]{:S(2)}) copy-start(f32[256,256]{1,0:T(8,128)} %refs_1_.1) | copy-start | bytes 786436
  34.2 9.0 %copy-start.6 = (f32[256,256]{1,0:T(8,128)S(1)}, f32[256,256]{1,0:T(8,128)}, u32[]{:S(2)}) copy-start(f32[256,256]{1,0:T(8,128)} %refs_2_.2) | copy-start | bytes 786436
  35.6 9.1 %copy-start.2 = (f32[192,256]{1,0:T(8,128)S(1)}, f32[192,256]{1,0:T(8,128)}, u32[]{:S(2)}) copy-start(f32[192,256]{1,0:T(8,128)} %refs_2_.3) | copy-start | bytes 589828
  35.6 14.2 %all-to-all-start = ((f32[32,8,256]{2,1,0:T(8,128)}), f32[32,8,256]{2,1,0:T(8,128)S(1)}, u32[]{:S(2)}, u32[]{:S(2)}) async-start(f32[32,8,256]{2,1,0:T(8,128)} %bitcast), calls=%async_computation | async-start | bytes 524288 | tf_op jit(solution)/shard_map/all_to_all | solution.py:369
  39.2 2.3 %copy-start.1 = (bf16[2,2,768,768]{3,2,1,0:T(8,128)(2,1)S(1)}, bf16[2,2,768,768]{3,2,1,0:T(8,128)(2,1)}, u32[]{:S(2)}) copy-start(bf16[2,2,768,768]{3,2,1,0:T(8,128)(2,1)} %copy-done) | copy-start | bytes 14155780
  42.9 1.8 %collective-permute-start.13 = (f32[2,192,256]{2,1,0:T(8,128)S(1)}, f32[2,192,256]{2,1,0:T(8,128)S(1)}, u32[]{:S(2)}, u32[]{:S(2)}) collective-permute-start(f32[2,192,256]{2,1,0:T(8,128)S(1)} %get-tuple-element.28), channel_id=1, source_target_pairs={{0,1},{1,0},{2,3},{3,2},{4,5},{5,4},{6,7},{7,6},{8,9},{9,8},{10,11... | collective-permute-start | bytes 1179656 | tf_op jit(solution)/shard_map/ppermute | solution.py:274
  50.9 13.2 %all-to-all-start.1 = ((f32[32,8,256]{2,1,0:T(8,128)}), f32[32,8,256]{2,1,0:T(8,128)S(1)}, u32[]{:S(2)}, u32[]{:S(2)}) async-start(f32[32,8,256]{2,1,0:T(8,128)} %bitcast.2), calls=%async_computation.1 | async-start | bytes 524288 | tf_op jit(solution)/shard_map/all_to_all | solution.py:386
  53.5 9.7 %collective-permute-start.14 = (f32[1,192,256]{2,1,0:T(8,128)S(1)}, f32[1,192,256]{2,1,0:T(8,128)S(1)}, u32[]{:S(2)}, u32[]{:S(2)}) collective-permute-start(f32[1,192,256]{2,1,0:T(8,128)S(1)} %get-tuple-element.31.refs_4_), channel_id=1, source_target_pairs={{0,2},{1,3},{2,0},{3,1},{4,6},{5,7},{6,4},{7,5},{8,10},{9,11},{10,... | collective-permute-start | bytes 589832 | tf_op jit(solution)/shard_map/ppermute | solution.py:274
